TPU v7x, 32 devices: a whole 2x2x4 slice. The times are simulated.
32 devices in a mesh: grp: 8 (over z, x), rot: 4 (over y, core).
Axes of the slice: x: 2, y: 2, z: 4, core: 2. Of those that a mesh axis runs over, the one named last changes fastest.
Arguments:
- features: bfloat16 [32768, 256], P(('grp', 'rot')), may hold values from -64 to 64
- w_msg: bfloat16 [2, 256, 256], replicated, may hold values from -0.375 to 0.375
- w_upd: bfloat16 [2, 256, 256], replicated, may hold values from -0.375 to 0.375
- local_tiles: bfloat16 [8, 4, 8, 3, 128, 128], P('grp', 'rot'), may hold values from -0.25 to 0.25
- local_src: int32 [8, 4, 8, 3], P('grp', 'rot'), may hold values from 0 to 7
- local_live: int32 [8, 4, 8, 3], P('grp', 'rot'), may hold values 0 or 1
- border_tiles: bfloat16 [8, 4, 4, 128, 128], P('grp', 'rot'), may hold values from -0.25 to 0.25
- border_rows: int32 [8, 4, 4, 128], P('grp', 'rot'), may hold values from 0 to 1023
- border_block: int32 [8, 4, 4], P('grp', 'rot'), may hold values from 0 to 7
- ball_order: int32 [8, 4, 1024], P('grp', 'rot'), may hold values from 0 to 1023, each once within a row
- w_ball_qkv: bfloat16 [256, 768], replicated, may hold values from -32 to 32
- w_ball_out: bfloat16 [256, 256], replicated, may hold values from -0.375 to 0.375
- w_mlp_in: bfloat16 [256, 1024], replicated, may hold values from -0.375 to 0.375
- w_mlp_out: bfloat16 [1024, 256], replicated, may hold values from -0.1875 to 0.1875
- w_rot_qkv: bfloat16 [256, 768], replicated, may hold values from -32 to 32
- w_rot_out: bfloat16 [256, 256], replicated, may hold values from -0.375 to 0.375
- relay_peer: int32 [8, 4, 1024], P('grp', 'rot'), may hold values from 0 to 3, as said below
- relay_rank: int32 [8, 4, 1024], P('grp', 'rot'), may hold values from 0 to 511, as said below
- relay_inbox: int32 [8, 4, 4, 512], P('grp', 'rot'), may hold values from 0 to 1024, as said below
Outputs:
- points_out: float32 [32768, 256], P(('grp', 'rot'))
Inputs may be any that keep to these rules, and one draw needn't show every extreme that they name: `relay_peer`: each partition (g, r) relays exactly 512 of its points to partition (g, (r + 1) mod 4) and at most 171 to each other partition of its group, itself included, with 171 reached; every partition owns exactly 1024 points. `relay_rank`: for a fixed partition and owner, the ranks of the relayed points are 0, 1, 2 and so on without gaps. relay_inbox[g, o, s, c] is the owner row of the point that (g, s) relays to (g, o) with rank c, or 1024 where no such point exists; each owner row 0 .. 1023 appears exactly once for each (g, o).
All inputs are finite; a program needn't handle non-finite values. No bound on the sum of `local_live` on one device may be relied on, other than what follows from the above.
Results may differ from a plain program's by a relative error of at most 0.017.
Values may be sent and summed in bfloat16 or wider, within the bound.
No kernel may reach another device: no remote copies, remote signals or barrier semaphores. Data moves between devices by JAX's collectives and lax.ppermute only.
A program may use at most 64 MiB of HBM per device.

v0:
```python
import math

import jax
import jax.numpy as jnp
from jax import lax
from jax.sharding import PartitionSpec as P

HEADS = 8
HEAD = 32
BALL = 256
TILE = 128
PTS_DEV = 1024


EPSILON = 1e-06


def padded_2(cells, sides, width):
    for axis, dim in sides:
        count = lax.axis_size(axis)
        ends = count - 1
        head = lax.slice_in_dim(cells, 0, width, axis=dim)
        tail = lax.slice_in_dim(cells, cells.shape[dim] - width, cells.shape[dim], axis=dim)
        cells = jnp.concatenate(
            [
                lax.ppermute(tail, axis, [(i, (i + 1) % count) for i in range(ends)]),
                cells,
                lax.ppermute(head, axis, [((i + 1) % count, i) for i in range(ends)]),
            ],
            axis=dim,
        )
    return cells


def normed(values):
    return values * lax.rsqrt(jnp.mean(values * values, axis=-1, keepdims=True) + EPSILON)


def attend(rows_in, weight_qkv, weight_out):
    width = rows_in.shape[1]
    joined = jnp.dot(rows_in, weight_qkv, preferred_element_type=jnp.float32).astype(jnp.bfloat16)
    balls = rows_in.shape[0] // BALL
    query = joined[:, :width].reshape(balls, BALL, HEADS, HEAD)
    keys_all = joined[:, width : 2 * width].reshape(balls, BALL, HEADS, HEAD)
    values_all = joined[:, 2 * width :].reshape(balls, BALL, HEADS, HEAD)
    scores = jnp.einsum(
        "bqhe,bkhe->bhqk", query, keys_all, preferred_element_type=jnp.float32
    ) / math.sqrt(HEAD)
    weights = jax.nn.softmax(scores, axis=-1).astype(jnp.bfloat16)
    mixed = jnp.einsum(
        "bhqk,bkhe->bqhe", weights, values_all, preferred_element_type=jnp.float32
    ).astype(jnp.bfloat16)
    return jnp.dot(mixed.reshape(-1, width), weight_out, preferred_element_type=jnp.float32)


def message_layer(
    state, weight_in, weight_out, edge_tiles, edge_source, edge_live, rim_tiles, rim_rows, rim_block
):
    width = state.shape[1]
    blocks_count = state.shape[0] // TILE
    messages = jnp.dot(
        normed(state).astype(jnp.bfloat16), weight_in, preferred_element_type=jnp.float32
    ).astype(jnp.bfloat16)
    picked = messages[rim_rows]
    along_grp = padded_2(picked[0:2], (("grp", 0),), 1)
    along_rot = padded_2(picked[2:4], (("rot", 0),), 1)
    received = jnp.stack([along_grp[0], along_grp[3], along_rot[0], along_rot[3]])
    blocks = messages.reshape(blocks_count, TILE, width)
    sources = blocks[edge_source] * edge_live[:, :, None, None].astype(jnp.bfloat16)
    gathered = jnp.einsum("bkij,bkjd->bid", edge_tiles, sources, preferred_element_type=jnp.float32)
    border = jnp.einsum("jik,jkd->jid", rim_tiles, received, preferred_element_type=jnp.float32)
    one_hot = (rim_block[None, :] == jnp.arange(blocks_count)[:, None]).astype(jnp.float32)
    gathered = gathered + jnp.einsum(
        "bj,jid->bid", one_hot, border, precision=lax.Precision.HIGHEST
    )
    hidden = jax.nn.gelu(gathered.reshape(-1, width)).astype(jnp.bfloat16)
    return state + jnp.dot(hidden, weight_out, preferred_element_type=jnp.float32)


def ball_layer(state, order_rows, weight_qkv, weight_out, mlp_first, mlp_second):
    balled = state[order_rows]
    balled = balled + attend(normed(balled).astype(jnp.bfloat16), weight_qkv, weight_out)
    hidden = jax.nn.gelu(
        jnp.dot(normed(balled).astype(jnp.bfloat16), mlp_first, preferred_element_type=jnp.float32)
    ).astype(jnp.bfloat16)
    balled = balled + jnp.dot(hidden, mlp_second, preferred_element_type=jnp.float32)
    return jnp.zeros_like(state).at[order_rows].set(balled)


def owner_work(incoming, inbox_rows, weight_qkv, weight_out):
    width = incoming.shape[2]
    total_rows = inbox_rows.size
    owned = (
        jnp.zeros((weight_rows() + 1, width), jnp.bfloat16)
        .at[inbox_rows.reshape(-1)]
        .set(incoming.reshape(total_rows, width))
    )
    owned = owned[:-1]
    change = attend(owned, weight_qkv, weight_out).astype(jnp.bfloat16)
    padded = jnp.concatenate([change, jnp.zeros((1, width), jnp.bfloat16)], axis=0)
    return padded[inbox_rows]


def weight_rows():
    return PTS_DEV


def relay_layer(state, peer_rows, rank_rows, inbox_rows, weight_qkv, weight_out):
    points, width = state.shape
    members = lax.axis_size("rot")
    capacity = inbox_rows.shape[1]
    relay_input = normed(state).astype(jnp.bfloat16)
    slot_index = peer_rows * capacity + rank_rows
    outgoing = (
        jnp.zeros((members * capacity, width), jnp.bfloat16)
        .at[slot_index]
        .set(relay_input)
        .reshape(members, capacity, width)
    )
    incoming = lax.all_to_all(outgoing, "rot", split_axis=0, concat_axis=0, tiled=True)
    change_rows = owner_work(incoming, inbox_rows, weight_qkv, weight_out)
    returned = lax.all_to_all(change_rows, "rot", split_axis=0, concat_axis=0, tiled=True)
    update = returned.reshape(members * capacity, width)[slot_index]
    return state + update.astype(jnp.float32)


def local(
    features,
    w_msg,
    w_upd,
    local_tiles,
    local_src,
    local_live,
    border_tiles,
    border_rows,
    border_block,
    ball_order,
    w_ball_qkv,
    w_ball_out,
    w_mlp_in,
    w_mlp_out,
    w_rot_qkv,
    w_rot_out,
    relay_peer,
    relay_rank,
    relay_inbox,
):
    state = features.astype(jnp.float32)
    for layer_index in range(w_msg.shape[0]):
        state = message_layer(
            state,
            w_msg[layer_index],
            w_upd[layer_index],
            local_tiles[0, 0],
            local_src[0, 0],
            local_live[0, 0],
            border_tiles[0, 0],
            border_rows[0, 0],
            border_block[0, 0],
        )
    state = ball_layer(state, ball_order[0, 0], w_ball_qkv, w_ball_out, w_mlp_in, w_mlp_out)
    return relay_layer(
        state, relay_peer[0, 0], relay_rank[0, 0], relay_inbox[0, 0], w_rot_qkv, w_rot_out
    )


def solution(mesh):
    in_specs = (
        P(("grp", "rot"), None),
        P(),
        P(),
        P("grp", "rot", None, None, None, None),
        P("grp", "rot", None, None),
        P("grp", "rot", None, None),
        P("grp", "rot", None, None, None),
        P("grp", "rot", None, None),
        P("grp", "rot", None),
        P("grp", "rot", None),
        P(),
        P(),
        P(),
        P(),
        P(),
        P(),
        P("grp", "rot", None),
        P("grp", "rot", None),
        P("grp", "rot", None, None),
    )
    out_specs = P(("grp", "rot"), None)
    return jax.shard_map(local, mesh=mesh, in_specs=in_specs, out_specs=out_specs, check_vma=False)
```

profile of v0, /device:TPU:0, one launch (start us, length us, event | category | flops | bytes accessed | tf_op | source)
XLA Modules:
  0.0 163.9 jit_solution(6424681236137814082)
XLA Ops:
  0.0 1.3 copy.37
  1.5 0.7 fusion.145
  2.2 1.3 convolution_convert_fusion.4
  3.5 2.0 %gather_fusion.1 = bf16[512,256]{1,0:T(8,128)(2,1)S(1)} fusion(bf16[1024,256]{1,0:T(8,128)(2,1)S(1)} %convolution_convert_fusion.4, s32[1024]{0:T(1024)S(1)} %pad_clamp_fusion), kind=kCustom, calls=%fused_computation.1 | custom fusion | bytes 526336 | tf_op jit(solution)/shard_map/gather | solution.py:64
  5.4 0.7 slice_bitcast_fusion.7
  6.1 5.5 %collective-permute-start = (bf16[1,128,256]{2,1,0:T(8,128)(2,1)}, bf16[1,128,256]{2,1,0:T(8,128)(2,1)}, u32[]{:S(2)}, u32[]{:S(2)}) collective-permute-start(bf16[1,128,256]{2,1,0:T(8,128)(2,1)} %get-tuple-element.15), channel_id=1, source_target_pairs={{0,4},{4,8},{8,12},{12,16},{16,20},{20,24},{24,28},{1,5},{5,9},{9,... | collective-permute-start | bytes 196616 | tf_op jit(solution)/shard_map/ppermute | solution.py:26
  11.5 1.3 collective-permute-start.1
  12.8 2.1 %collective-permute-start.2 = (bf16[1,128,256]{2,1,0:T(8,128)(2,1)S(1)}, bf16[1,128,256]{2,1,0:T(8,128)(2,1)}, u32[]{:S(2)}, u32[]{:S(2)}) collective-permute-start(bf16[1,128,256]{2,1,0:T(8,128)(2,1)S(1)} %get-tuple-element.16), channel_id=1, source_target_pairs={{0,1},{1,2},{2,3},{4,5},{5,6},{6,7},{8,9},{9,10},{10,11},{12,13},{... | collective-permute-start | bytes 196616 | tf_op jit(solution)/shard_map/ppermute | solution.py:26
  14.9 1.3 collective-permute-start.3
  16.4 0.7 copy.71
  17.1 0.6 gather_fusion
  18.0 1.2 collective-permute-done.3
  19.2 2.1 %fusion.118 = f32[4,256,128]{2,1,0:T(8,128)} fusion(bf16[1,128,256]{2,1,0:T(8,128)(2,1)} %collective-permute-done.3, bf16[1,128,256]{2,1,0:T(8,128)(2,1)} %collective-permute-done.2, bf16[1,128,256]{2,1,0:T(8,128)(2,1)} %collective-permute-done.1, bf16[1,128,256]{2,1,0:T(8,128)(2,1)} %collective-permute-done, bf16[1,1,4,128,128]{4,3,2,1,0:T(8,128)(2,1)} %param.25), kind=kOutput, calls=%fused_computation.120 | convolution fusion | flops 33947648 | bytes 917504 | tf_op jit(solution)/shard_map/jik,jkd->jid/dot_general | solution.py:71
  21.3 1.3 copy.64
  22.6 1.5 fusion.81
  24.1 1.7 %fusion.53 = bf16[8,128,256]{2,1,0:T(8,128)(2,1)S(1)} fusion(bf16[8,3,128,256]{3,2,1,0:T(8,128)(2,1)S(1)} %bitcast.154, f32[8,128,256]{2,0,1:T(8,128)S(1)} %fusion.81, bf16[1,1,8,3,128,128]{5,4,3,2,1,0:T(8,128)(2,1)S(1)} %copy-done, bf16[8,3]{1,0:T(8,128)(2,1)} %bitcast.167), kind=kOutput, calls=%fused_computation.68 | convolution fusion | flops 207093760 | bytes 3932208 | tf_op jit(solution)/shard_map/bkij,bkjd->bid/dot_general | solution.py:70
  25.8 0.4 multiply_reduce_fusion.5
  26.2 0.4 convolution_convert_fusion.3
  26.6 2.0 %gather_fusion.3 = bf16[512,256]{1,0:T(8,128)(2,1)S(1)} fusion(bf16[1024,256]{1,0:T(8,128)(2,1)S(1)} %convolution_convert_fusion.3, s32[1024]{0:T(1024)S(1)} %pad_clamp_fusion), kind=kCustom, calls=%fused_computation.3 | custom fusion | bytes 526336 | tf_op jit(solution)/shard_map/gather | solution.py:64
  28.6 4.5 %collective-permute-start.4 = (bf16[1,128,256]{2,1,0:T(8,128)(2,1)S(1)}, bf16[1,128,256]{2,1,0:T(8,128)(2,1)S(1)}, u32[]{:S(2)}, u32[]{:S(2)}) collective-permute-start(bf16[1,128,256]{2,1,0:T(8,128)(2,1)S(1)} %get-tuple-element.11), channel_id=1, source_target_pairs={{0,4},{4,8},{8,12},{12,16},{16,20},{20,24},{24,28},{1,5},{5,9},{9,... | collective-permute-start | bytes 196616 | tf_op jit(solution)/shard_map/ppermute | solution.py:26
  33.1 1.3 collective-permute-start.5
  34.4 4.5 %collective-permute-start.6 = (bf16[1,128,256]{2,1,0:T(8,128)(2,1)S(1)}, bf16[1,128,256]{2,1,0:T(8,128)(2,1)S(1)}, u32[]{:S(2)}, u32[]{:S(2)}) collective-permute-start(bf16[1,128,256]{2,1,0:T(8,128)(2,1)S(1)} %get-tuple-element.12), channel_id=1, source_target_pairs={{0,1},{1,2},{2,3},{4,5},{5,6},{6,7},{8,9},{9,10},{10,11},{12,13},{... | collective-permute-start | bytes 196616 | tf_op jit(solution)/shard_map/ppermute | solution.py:26
  39.0 1.3 collective-permute-start.7
  40.3 1.9 %gather_fusion.2 = bf16[24,128,256]{2,1,0:T(8,128)(2,1)} fusion(bf16[8,128,256]{2,1,0:T(8,128)(2,1)S(1)} %bitcast.145, s32[1024]{0:T(1024)S(1)} %pad_clamp_fusion.1), kind=kCustom, calls=%fused_computation.2 | custom fusion | bytes 3145824 | tf_op jit(solution)/shard_map/gather | solution.py:69
  42.2 0.3 fusion.126
  42.5 0.2 copy.66
  42.8 0.8 fusion.79
  43.6 2.4 %fusion.65 = bf16[8,128,256]{2,1,0:T(8,128)(2,1)S(1)} fusion(bf16[8,3,128,256]{3,2,1,0:T(8,128)(2,1)} %bitcast.153, f32[8,128,256]{2,0,1:T(8,128)S(1)} %fusion.79, bf16[1,1,8,3,128,128]{5,4,3,2,1,0:T(8,128)(2,1)S(1)} %copy-done, bf16[8,3]{1,0:T(8,128)(2,1)S(1)} %bitcast.168), kind=kOutput, calls=%fused_computation.76 | convolution fusion | flops 207093760 | bytes 3932208 | tf_op jit(solution)/shard_map/bkij,bkjd->bid/dot_general | solution.py:70
  46.0 0.3 convolution_add_fusion.1
  46.3 0.3 copy.43
  46.7 3.6 %gather_fusion.4 = f32[1024,256]{1,0:T(8,128)S(1)} fusion(f32[1024,256]{1,0:T(8,128)S(1)} %copy.43, s32[1024]{0:T(1024)S(1)} %broadcast_clamp_fusion.2), kind=kCustom, calls=%fused_computation.4 | custom fusion | bytes 2101248 | tf_op jit(solution)/shard_map/gather | solution.py:81
  50.5 0.3 copy.52
  50.9 0.6 convolution_convert_fusion.1
  51.5 0.9 fusion.160
  52.4 1.2 copy.45
  53.7 1.2 reshape.271
  55.1 1.2 reshape.272
  56.5 0.4 reshape.270
  56.9 7.3 %fusion.161 = (f32[4,8,256]{2,1,0:T(8,128)S(1)}, f32[4,8,256,256]{2,3,1,0:T(8,128)}) fusion(bf16[4,256,8,32]{1,0,3,2:T(4,128)(2,1)} %reshape.272, bf16[4,256,8,32]{1,0,3,2:T(4,128)(2,1)} %reshape.271), kind=kOutput, calls=%fused_computation.186 | convolution fusion | flops 140509440 | bytes 9469952 | tf_op jit(solution)/shard_map/sub | solution.py:49
  64.2 4.2 %fusion.40 = bf16[4,256,8,32]{1,3,2,0:T(8,128)(2,1)S(1)} fusion(f32[4,8,256,256]{2,3,1,0:T(8,128)} %get-tuple-element.22, f32[4,8,256]{2,1,0:T(8,128)S(1)} %get-tuple-element.21, bf16[4,256,8,32]{1,0,3,2:T(4,128)(2,1)S(1)} %reshape.270), kind=kOutput, calls=%fused_computation.57 | convolution fusion | flops 138674176 | bytes 9469952 | tf_op jit(solution)/shard_map/bhqk,bkhe->bqhe/dot_general | solution.py:50
  68.5 0.4 copy.51
  69.0 0.3 multiply_reduce_fusion.3
  69.5 3.0 %fusion.25 = f32[1024,256]{0,1:T(8,128)S(1)} fusion(f32[1024,256]{0,1:T(8,128)S(1)} %get-tuple-element.24, bf16[1024,256]{1,0:T(8,128)(2,1)S(1)} %copy-done.15, bf16[256,1024]{1,0:T(8,128)(2,1)} %param.31, f32[1024]{0:T(1024)S(1)} %add_rsqrt_fusion.1), kind=kOutput, calls=%fused_computation.45 | convolution fusion | flops 1083965440 | bytes 3149824 | tf_op jit(solution)/shard_map/dot_general | solution.py:86
  72.5 0.3 copy.54
  72.9 5.3 %scatter_custom_fusion = f32[1024,256]{1,0:T(8,128)S(1)} fusion(s32[1024]{0:T(1024)S(1)} %bitcast.163, f32[1024,256]{1,0:T(8,128)S(1)} %copy.54, f32[]{:T(128)} %constant.16.clone.1), kind=kCustom, calls=%fused_computation.106 | custom fusion | bytes 1048580 | tf_op jit(solution)/shard_map/scatter | solution.py:87
  78.4 6.5 %scatter_custom_fusion.1 = bf16[2048,256]{1,0:T(8,128)(2,1)} fusion(s32[1024]{0:T(1024)S(1)} %bitcast.160, f32[1024,256]{1,0:T(8,128)S(1)} %scatter_custom_fusion, f32[1024]{0:T(1024)S(1)} %add_rsqrt_fusion, bf16[]{:T(256)} %constant.28.clone.1), kind=kCustom, calls=%fused_computation.92 | custom fusion | flops 524288 | bytes 2101250 | tf_op jit(solution)/shard_map/scatter | solution.py:117
  84.8 3.8 %all-to-all-start = ((bf16[4,512,256]{2,1,0:T(8,128)(2,1)}), bf16[4,512,256]{2,1,0:T(8,128)(2,1)S(1)}, u32[]{:S(2)}, u32[]{:S(2)}) async-start(bf16[4,512,256]{2,1,0:T(8,128)(2,1)} %bitcast.40), calls=%async_computation | async-start | bytes 2097152 | tf_op jit(solution)/shard_map/all_to_all | solution.py:120
  88.7 14.4 %all-to-all-done = bf16[4,512,256]{2,1,0:T(8,128)(2,1)S(1)} async-done(((bf16[4,512,256]{2,1,0:T(8,128)(2,1)}), bf16[4,512,256]{2,1,0:T(8,128)(2,1)S(1)}, u32[]{:S(2)}, u32[]{:S(2)}) %all-to-all-start) | async-done | bytes 1048608 | tf_op jit(solution)/shard_map/all_to_all | solution.py:120
  103.1 9.3 %scatter_custom_fusion.2 = bf16[1025,256]{1,0:T(8,128)(2,1)S(1)} fusion(s32[2048]{0:T(1024)S(1)} %bitcast.164, bf16[2048,256]{1,0:T(8,128)(2,1)S(1)} %bitcast.155, bf16[]{:T(256)} %constant.28.clone.1), kind=kCustom, calls=%fused_computation.118 | custom fusion | bytes 524802 | tf_op jit(solution)/shard_map/scatter | solution.py:96
  112.4 1.6 convolution_convert_fusion
  114.0 0.9 fusion.159
  114.9 1.2 copy.56
  116.1 1.2 reshape.277
  117.6 1.2 reshape.278
  118.9 0.4 reshape.276
  119.3 7.3 %fusion.170 = (f32[4,8,256]{2,1,0:T(8,128)S(1)}, f32[4,8,256,256]{2,3,1,0:T(8,128)}) fusion(bf16[4,256,8,32]{1,0,3,2:T(4,128)(2,1)} %reshape.278, bf16[4,256,8,32]{1,0,3,2:T(4,128)(2,1)} %reshape.277), kind=kOutput, calls=%fused_computation.187 | convolution fusion | flops 140509440 | bytes 9469952 | tf_op jit(solution)/shard_map/sub | solution.py:49
  126.7 4.2 %fusion.41 = bf16[4,256,8,32]{1,3,2,0:T(8,128)(2,1)S(1)} fusion(f32[4,8,256,256]{2,3,1,0:T(8,128)} %get-tuple-element.26, f32[4,8,256]{2,1,0:T(8,128)S(1)} %get-tuple-element.25, bf16[4,256,8,32]{1,0,3,2:T(4,128)(2,1)S(1)} %reshape.276), kind=kOutput, calls=%fused_computation.58 | convolution fusion | flops 138674176 | bytes 9469952 | tf_op jit(solution)/shard_map/bhqk,bkhe->bqhe/dot_general | solution.py:50
  130.9 0.4 copy.62
  131.4 0.4 convolution_convert_fusion.2
  131.8 9.1 %gather_fusion.5 = bf16[2048,256]{1,0:T(8,128)(2,1)} fusion(bf16[1025,256]{1,0:T(8,128)(2,1)S(1)} %concatenate.3, s32[2048]{0:T(1024)S(1)} %broadcast_clamp_fusion), kind=kCustom, calls=%fused_computation.5 | custom fusion | bytes 2105344 | tf_op jit(solution)/shard_map/gather | solution.py:101
  140.9 3.5 %all-to-all-start.1 = ((bf16[4,512,256]{2,1,0:T(8,128)(2,1)}), bf16[4,512,256]{2,1,0:T(8,128)(2,1)S(1)}, u32[]{:S(2)}, u32[]{:S(2)}) async-start(bf16[4,512,256]{2,1,0:T(8,128)(2,1)} %bitcast.148), calls=%async_computation.1 | async-start | bytes 2097152 | tf_op jit(solution)/shard_map/all_to_all | solution.py:122
  144.4 14.4 %all-to-all-done.1 = bf16[4,512,256]{2,1,0:T(8,128)(2,1)S(1)} async-done(((bf16[4,512,256]{2,1,0:T(8,128)(2,1)}), bf16[4,512,256]{2,1,0:T(8,128)(2,1)S(1)}, u32[]{:S(2)}, u32[]{:S(2)}) %all-to-all-start.1) | async-done | bytes 1048608 | tf_op jit(solution)/shard_map/all_to_all | solution.py:122
  158.8 3.9 %gather_fusion.6 = bf16[1024,256]{1,0:T(8,128)(2,1)S(1)} fusion(bf16[2048,256]{1,0:T(8,128)(2,1)S(1)} %bitcast.146, s32[1024]{0:T(1024)S(1)} %broadcast_clamp_fusion.1), kind=kCustom, calls=%fused_computation.6 | custom fusion | bytes 1052672 | tf_op jit(solution)/shard_map/gather | solution.py:123
  162.8 1.1 convert_add_fusion.1
  (72 shorter events, 2.3 us)
Async XLA Ops:
  0.0 24.1 %copy-start = (bf16[1,1,8,3,128,128]{5,4,3,2,1,0:T(8,128)(2,1)S(1)}, bf16[1,1,8,3,128,128]{5,4,3,2,1,0:T(8,128)(2,1)}, u32[]{:S(2)}) copy-start(bf16[1,1,8,3,128,128]{5,4,3,2,1,0:T(8,128)(2,1)} %param.22) | copy-start | bytes 2359300
  0.0 16.2 %copy-start.13 = (s32[1,1,8,3]{2,1,3,0:T(1,128)S(1)}, s32[1,1,8,3]{2,1,3,0:T(1,128)}, u32[]{:S(2)}) copy-start(s32[1,1,8,3]{2,1,3,0:T(1,128)} %param.23) | copy-start | bytes 292
  0.0 16.4 %copy-start.14 = (s32[1,1,8,3]{2,1,3,0:T(1,128)S(1)}, s32[1,1,8,3]{2,1,3,0:T(1,128)}, u32[]{:S(2)}) copy-start(s32[1,1,8,3]{2,1,3,0:T(1,128)} %param.24) | copy-start | bytes 292
  0.0 17.1 %copy-start.10 = (s32[1,1,1024]{2,1,0:T(1,128)S(1)}, s32[1,1,1024]{2,1,0:T(1,128)}, u32[]{:S(2)}) copy-start(s32[1,1,1024]{2,1,0:T(1,128)} %param.28) | copy-start | bytes 12292
  0.0 17.1 %copy-start.9 = (s32[1,1,1024]{2,1,0:T(1,128)S(1)}, s32[1,1,1024]{2,1,0:T(1,128)}, u32[]{:S(2)}) copy-start(s32[1,1,1024]{2,1,0:T(1,128)} %param.35) | copy-start | bytes 12292
  0.0 17.1 %copy-start.8 = (s32[1,1,1024]{2,1,0:T(1,128)S(1)}, s32[1,1,1024]{2,1,0:T(1,128)}, u32[]{:S(2)}) copy-start(s32[1,1,1024]{2,1,0:T(1,128)} %param.36) | copy-start | bytes 12292
  6.1 11.7 %collective-permute-start = (bf16[1,128,256]{2,1,0:T(8,128)(2,1)}, bf16[1,128,256]{2,1,0:T(8,128)(2,1)}, u32[]{:S(2)}, u32[]{:S(2)}) collective-permute-start(bf16[1,128,256]{2,1,0:T(8,128)(2,1)} %get-tuple-element.15), channel_id=1, source_target_pairs={{0,4},{4,8},{8,12},{12,16},{16,20},{20,24},{24,28},{1,5},{5,9},{9,... | collective-permute-start | bytes 196616 | tf_op jit(solution)/shard_map/ppermute | solution.py:26
  11.5 6.5 %collective-permute-start.1 = (bf16[1,128,256]{2,1,0:T(8,128)(2,1)}, bf16[1,128,256]{2,1,0:T(8,128)(2,1)}, u32[]{:S(2)}, u32[]{:S(2)}) collective-permute-start(bf16[1,128,256]{2,1,0:T(8,128)(2,1)} %get-tuple-element.17), channel_id=1, source_target_pairs={{4,0},{8,4},{12,8},{16,12},{20,16},{24,20},{28,24},{5,1},{9,5},{13... | collective-permute-start | bytes 196616 | tf_op jit(solution)/shard_map/ppermute | solution.py:28
  12.8 5.2 %collective-permute-start.2 = (bf16[1,128,256]{2,1,0:T(8,128)(2,1)S(1)}, bf16[1,128,256]{2,1,0:T(8,128)(2,1)}, u32[]{:S(2)}, u32[]{:S(2)}) collective-permute-start(bf16[1,128,256]{2,1,0:T(8,128)(2,1)S(1)} %get-tuple-element.16), channel_id=1, source_target_pairs={{0,1},{1,2},{2,3},{4,5},{5,6},{6,7},{8,9},{9,10},{10,11},{12,13},{... | collective-permute-start | bytes 196616 | tf_op jit(solution)/shard_map/ppermute | solution.py:26
  14.9 4.2 %collective-permute-start.3 = (bf16[1,128,256]{2,1,0:T(8,128)(2,1)S(1)}, bf16[1,128,256]{2,1,0:T(8,128)(2,1)}, u32[]{:S(2)}, u32[]{:S(2)}) collective-permute-start(bf16[1,128,256]{2,1,0:T(8,128)(2,1)S(1)} %get-tuple-element.18), channel_id=1, source_target_pairs={{1,0},{2,1},{3,2},{5,4},{6,5},{7,6},{9,8},{10,9},{11,10},{13,12},{... | collective-permute-start | bytes 196616 | tf_op jit(solution)/shard_map/ppermute | solution.py:28
  22.5 3.3 %copy-start.2 = (bf16[2,256,256]{2,1,0:T(8,128)(2,1)S(1)}, bf16[2,256,256]{2,1,0:T(8,128)(2,1)}, u32[]{:S(2)}) copy-start(bf16[2,256,256]{2,1,0:T(8,128)(2,1)} %param.21) | copy-start | bytes 786436
  24.0 2.2 %copy-start.6 = (bf16[2,256,256]{2,1,0:T(8,128)(2,1)S(1)}, bf16[2,256,256]{2,1,0:T(8,128)(2,1)}, u32[]{:S(2)}) copy-start(bf16[2,256,256]{2,1,0:T(8,128)(2,1)} %param.20) | copy-start | bytes 786436
  25.8 14.5 %copy-start.7 = (s32[1,1,4,512]{3,2,1,0:T(4,128)S(1)}, s32[1,1,4,512]{3,2,1,0:T(4,128)}, u32[]{:S(2)}) copy-start(s32[1,1,4,512]{3,2,1,0:T(4,128)} %param.37) | copy-start | bytes 24580
  26.2 16.0 %copy-start.16 = (bf16[1,1,4,128,128]{4,3,2,1,0:T(8,128)(2,1)S(1)}, bf16[1,1,4,128,128]{4,3,2,1,0:T(8,128)(2,1)}, u32[]{:S(2)}) copy-start(bf16[1,1,4,128,128]{4,3,2,1,0:T(8,128)(2,1)} %param.25) | copy-start | bytes 393220
  26.6 16.2 %copy-start.11 = (s32[1,1,4]{2,1,0:T(1,128)S(1)}, s32[1,1,4]{2,1,0:T(1,128)}, u32[]{:S(2)}) copy-start(s32[1,1,4]{2,1,0:T(1,128)} %param.27) | copy-start | bytes 52
  28.5 15.0 %copy-start.12 = (bf16[1,1,8,3]{3,2,1,0:T(8,128)(2,1)S(1)}, bf16[1,1,8,3]{3,2,1,0:T(8,128)(2,1)}, u32[]{:S(2)}) copy-start(bf16[1,1,8,3]{3,2,1,0:T(8,128)(2,1)} %copy.71) | copy-start | bytes 148
  28.6 13.6 %collective-permute-start.4 = (bf16[1,128,256]{2,1,0:T(8,128)(2,1)S(1)}, bf16[1,128,256]{2,1,0:T(8,128)(2,1)S(1)}, u32[]{:S(2)}, u32[]{:S(2)}) collective-permute-start(bf16[1,128,256]{2,1,0:T(8,128)(2,1)S(1)} %get-tuple-element.11), channel_id=1, source_target_pairs={{0,4},{4,8},{8,12},{12,16},{16,20},{20,24},{24,28},{1,5},{5,9},{9,... | collective-permute-start | bytes 196616 | tf_op jit(solution)/shard_map/ppermute | solution.py:26
  33.1 9.1 %collective-permute-start.5 = (bf16[1,128,256]{2,1,0:T(8,128)(2,1)S(1)}, bf16[1,128,256]{2,1,0:T(8,128)(2,1)S(1)}, u32[]{:S(2)}, u32[]{:S(2)}) collective-permute-start(bf16[1,128,256]{2,1,0:T(8,128)(2,1)S(1)} %get-tuple-element.13), channel_id=1, source_target_pairs={{4,0},{8,4},{12,8},{16,12},{20,16},{24,20},{28,24},{5,1},{9,5},{13... | collective-permute-start | bytes 196616 | tf_op jit(solution)/shard_map/ppermute | solution.py:28
  34.4 7.8 %collective-permute-start.6 = (bf16[1,128,256]{2,1,0:T(8,128)(2,1)S(1)}, bf16[1,128,256]{2,1,0:T(8,128)(2,1)S(1)}, u32[]{:S(2)}, u32[]{:S(2)}) collective-permute-start(bf16[1,128,256]{2,1,0:T(8,128)(2,1)S(1)} %get-tuple-element.12), channel_id=1, source_target_pairs={{0,1},{1,2},{2,3},{4,5},{5,6},{6,7},{8,9},{9,10},{10,11},{12,13},{... | collective-permute-start | bytes 196616 | tf_op jit(solution)/shard_map/ppermute | solution.py:26
  39.0 3.2 %collective-permute-start.7 = (bf16[1,128,256]{2,1,0:T(8,128)(2,1)S(1)}, bf16[1,128,256]{2,1,0:T(8,128)(2,1)S(1)}, u32[]{:S(2)}, u32[]{:S(2)}) collective-permute-start(bf16[1,128,256]{2,1,0:T(8,128)(2,1)S(1)} %get-tuple-element.14), channel_id=1, source_target_pairs={{1,0},{2,1},{3,2},{5,4},{6,5},{7,6},{9,8},{10,9},{11,10},{13,12},{... | collective-permute-start | bytes 196616 | tf_op jit(solution)/shard_map/ppermute | solution.py:28
  42.8 3.2 %copy-start.3 = (bf16[2,256,256]{2,1,0:T(8,128)(2,1)S(1)}, bf16[2,256,256]{2,1,0:T(8,128)(2,1)}, u32[]{:S(2)}) copy-start(bf16[2,256,256]{2,1,0:T(8,128)(2,1)} %param.21) | copy-start | bytes 786436
  46.7 4.2 %copy-start.1 = (bf16[256,768]{1,0:T(8,128)(2,1)S(1)}, bf16[256,768]{1,0:T(8,128)(2,1)}, u32[]{:S(2)}) copy-start(bf16[256,768]{1,0:T(8,128)(2,1)} %param.29) | copy-start | bytes 1179652
  64.2 4.8 %copy-start.5 = (bf16[256,256]{1,0:T(8,128)(2,1)S(1)}, bf16[256,256]{1,0:T(8,128)(2,1)}, u32[]{:S(2)}) copy-start(bf16[256,256]{1,0:T(8,128)(2,1)} %param.30) | copy-start | bytes 393220
  68.5 1.0 copy-start.15
  84.8 18.2 %all-to-all-start = ((bf16[4,512,256]{2,1,0:T(8,128)(2,1)}), bf16[4,512,256]{2,1,0:T(8,128)(2,1)S(1)}, u32[]{:S(2)}, u32[]{:S(2)}) async-start(bf16[4,512,256]{2,1,0:T(8,128)(2,1)} %bitcast.40), calls=%async_computation | async-start | bytes 2097152 | tf_op jit(solution)/shard_map/all_to_all | solution.py:120
  126.7 4.8 %copy-start.4 = (bf16[256,256]{1,0:T(8,128)(2,1)S(1)}, bf16[256,256]{1,0:T(8,128)(2,1)}, u32[]{:S(2)}) copy-start(bf16[256,256]{1,0:T(8,128)(2,1)} %param.34) | copy-start | bytes 393220
  140.9 18.0 %all-to-all-start.1 = ((bf16[4,512,256]{2,1,0:T(8,128)(2,1)}), bf16[4,512,256]{2,1,0:T(8,128)(2,1)S(1)}, u32[]{:S(2)}, u32[]{:S(2)}) async-start(bf16[4,512,256]{2,1,0:T(8,128)(2,1)} %bitcast.148), calls=%async_computation.1 | async-start | bytes 2097152 | tf_op jit(solution)/shard_map/all_to_all | solution.py:122
where the time goes:
time: 166 us; the launch traced here: 164 us
  local copies, waits for them, and re-layouts  54.9 us (33%)
  matrix products  40.1 us (24%)
  waiting for transfers between devices  30.2 us (18%)
  starting transfers between devices  29.1 us (18%)
  other arithmetic  8.88 us (5%)
    ppermute x4, starting transfers between devices, padded_2(): lax.ppermute(tail, axis, [(i, (i + 1) % count) for i in range(ends)])  16.6 us
    sub x2, matrix products, attend(): weights = jax.nn.softmax(scores, axis=-1).astype(jnp.bfloat16)  14.7 us
    all_to_all x1, waiting for transfers between devices, relay_layer(): lax.all_to_all(outgoing, 'rot', split_axis=0, concat_axis=0, tiled=True)  14.4 us
    all_to_all x1, waiting for transfers between devices, relay_layer(): lax.all_to_all(change_rows, 'rot', split_axis=0, concat_axis=0, tiled=True)  14.4 us
    scatter x1, local copies, waits for them, and re-layouts, owner_work(): owned = jnp.zeros((weight_rows() + 1, width), jnp.bfloat16).at[inbox_rows...  9.32 us
    gather x1, local copies, waits for them, and re-layouts, owner_work(): return padded[inbox_rows]  9.06 us
    dot_general x2, matrix products, attend(): jnp.einsum('bhqk,bkhe->bqhe', weights, values_all, preferred_element_type...  8.45 us
    scatter x1, other arithmetic, relay_layer(): outgoing = jnp.zeros((members * capacity, width), jnp.bfloat16).at[slot_i...  6.48 us
  transfers between devices with their start and end apart: 10, of which 4 were waited for; matrix products, arithmetic and copies ran while one was open for 2% of the time, Pallas kernels for 0%

commit v1 on v0

v1 whole, which is shorter than its diff:
```python
import math

import jax
import jax.numpy as jnp
from jax import lax
from jax.experimental import pallas as pl
from jax.experimental.pallas import tpu as pltpu
from jax.sharding import PartitionSpec as P

HEADS = 8
BALL = 256
EPSILON = 1e-06
F32 = jnp.float32
BF16 = jnp.bfloat16
LANES = 128


def up_to(count, unit):
    return -(-count // unit) * unit


def dot(left, right):
    return jnp.dot(left, right, preferred_element_type=F32)


def dot_rows(left, right):
    return lax.dot_general(left, right, (((1,), (1,)), ((), ())), preferred_element_type=F32)


def normed(values):
    return values * lax.rsqrt(jnp.mean(values * values, axis=-1, keepdims=True) + EPSILON)


def iota(shape, axis):
    return lax.broadcasted_iota(jnp.int32, shape, axis)


def hot(mask):
    return jnp.where(mask, 1.0, 0.0).astype(BF16)


def column(lane_row):
    return jnp.transpose(jnp.broadcast_to(lane_row, (LANES, LANES)))


def picks(lane_rows, width):
    count = lane_rows.shape[1]
    out = []
    for start in range(0, count, LANES):
        col = column(lane_rows[:, start : start + LANES])
        out.append(
            jnp.concatenate(
                [hot(col == iota((LANES, LANES), 1) + at) for at in range(0, width, LANES)], axis=1
            )
        )
    return jnp.concatenate(out, axis=0)


def places(lane_rows, height):
    return hot(iota((height, lane_rows.shape[1]), 0) == lane_rows)


def attention(rows_in, weight_qkv, store):
    width = rows_in.shape[1]
    head = width // HEADS
    scale = math.log2(math.e) / math.sqrt(head)
    lane_head = iota((1, width), 1) // head
    masks = [hot(lane_head == h) for h in range(HEADS)]
    for at in range(0, rows_in.shape[0], BALL):
        joined = dot(rows_in[at : at + BALL], weight_qkv).astype(BF16)
        query = joined[:, :width]
        keys = joined[:, width : 2 * width]
        values = joined[:, 2 * width :]
        mixed = jnp.zeros((BALL, width), F32)
        for h in range(HEADS):
            scores = dot_rows(query * masks[h], keys)
            top = jnp.max(scores, axis=-1, keepdims=True)
            raw = jnp.exp2((scores - top) * scale)
            weights = raw * (1.0 / jnp.sum(raw, axis=-1, keepdims=True))
            mixed = mixed + dot(weights.astype(BF16), values * masks[h])
        store(at, mixed.astype(BF16))


def gelu(values):
    inner = math.sqrt(2.0 / math.pi) * (values + 0.044715 * (values * values * values))
    return 0.5 * values * (1.0 + jnp.tanh(inner))


def make_rims(messages, rim_rows_ref, out_refs):
    par_grp = lax.rem(lax.axis_index("grp"), 2)
    par_rot = lax.rem(lax.axis_index("rot"), 2)
    sides = (1 - par_grp, par_grp, 3 - par_rot, 2 + par_rot)
    for side, out in zip(sides, out_refs):
        out[...] = dot(picks(rim_rows_ref[0, 0, pl.ds(side, 1), :], messages.shape[0]), messages).astype(BF16)


def first_kernel(features, w_msg, rim_rows, messages_out, *rims_out):
    messages = dot(normed(features[...].astype(F32)).astype(BF16), w_msg[0]).astype(BF16)
    messages_out[...] = messages
    make_rims(messages, rim_rows, rims_out)


def local_kernel(messages, tiles, source, live, aggregate):
    tile = tiles.shape[-1]
    blocks, sources = tiles.shape[2], tiles.shape[3]
    for b in range(blocks):
        total = None
        for k in range(sources):
            rows = messages[pl.ds(pl.multiple_of(source[0, 0, b, k] * tile, tile), tile), :]
            weight = tiles[0, 0, b, k] * live[0, 0, b, k].astype(BF16)
            part = dot(weight, rows)
            total = part if total is None else total + part
        aggregate[b * tile : (b + 1) * tile, :] = total


def add_border(total, received, tiles, block):
    grp, rot = lax.axis_index("grp"), lax.axis_index("rot")
    par_grp, par_rot = lax.rem(grp, 2), lax.rem(rot, 2)
    sides = (1 - par_grp, par_grp, 3 - par_rot, 2 + par_rot)
    size = tiles.shape[-2]
    for side, rows in zip(sides, received):
        index = jnp.where(side < 2, grp, rot)
        count = jnp.where(side < 2, lax.axis_size("grp"), lax.axis_size("rot"))
        above = lax.rem(side, 2) == 1
        inside = jnp.where(above, index + 1 < count, index > 0)
        part = dot(tiles[0, 0, pl.ds(side, 1)][0], rows[...]) * inside.astype(F32)
        at = pl.ds(pl.multiple_of(block[0, 0, side] * size, size), size)
        total[at, :] += part


def middle_kernel(
    state, aggregate, rec0, rec1, rec2, rec3, tiles, block, w_msg, w_upd, rim_rows,
    state_out, messages_out, rim0, rim1, rim2, rim3, total,
):
    total[...] = aggregate[...]
    add_border(total, (rec0, rec1, rec2, rec3), tiles, block)
    new = state[...].astype(F32) + dot(gelu(total[...]).astype(BF16), w_upd[0])
    state_out[...] = new
    messages = dot(normed(new).astype(BF16), w_msg[1]).astype(BF16)
    messages_out[...] = messages
    make_rims(messages, rim_rows, (rim0, rim1, rim2, rim3))


def slot_of(peer, rank, me, members, capacity, light):
    away = lax.rem(peer - me + members, members)
    base = jnp.where(away == 1, 0, capacity + light * jnp.where(away == 0, 0, away - 1))
    return base + rank


def ball_kernel(
    state, aggregate, rec0, rec1, rec2, rec3, tiles, block, w_upd, order,
    w_qkv, w_out, w_in, w_mlp_out, peer, rank, state_out, *refs, members, capacity, light,
):
    *outgoing, total, mixed = refs
    total[...] = aggregate[...]
    add_border(total, (rec0, rec1, rec2, rec3), tiles, block)
    points = state.shape[0]
    new = state[...] + dot(gelu(total[...]).astype(BF16), w_upd[1])
    unit = normed(new).astype(BF16)
    balled = dot(picks(order[0], points), unit).astype(BF16)

    def store(at, value):
        mixed[at : at + BALL, :] = value

    attention(balled, w_qkv[...], store)
    back = dot(places(order[0], points), mixed[...]).astype(BF16)
    new = new + dot(back, w_out[...])
    hidden = gelu(dot(normed(new).astype(BF16), w_in[...])).astype(BF16)
    new = new + dot(hidden, w_mlp_out[...])
    state_out[...] = new
    me = lax.axis_index("rot")
    slots = slot_of(peer[0], rank[0], me, members, capacity, light)
    unit = normed(new).astype(BF16)
    total_slots = capacity + (members - 1) * light
    sent = dot(places(slots, total_slots), unit).astype(BF16)
    outgoing[0][...] = sent[:capacity]
    for j in range(1, members):
        at = capacity + (j - 1) * light
        outgoing[j][...] = sent[at : at + light]


def senders(members):
    return [1, 0] + list(range(2, members))


def owner_kernel(inbox, w_qkv, *refs, members, capacity, light, wide):
    incoming, returned = refs[:members], refs[members : 2 * members]
    rows_in, mixed = refs[2 * members :]
    me = lax.axis_index("rot")
    points = mixed.shape[0]
    indices = []
    rows_in[...] = jnp.zeros_like(rows_in)
    at = 0
    for away, rows in zip(senders(members), incoming):
        height = capacity if away == 1 else light
        span = capacity if away == 1 else wide
        sender = lax.rem(me - away + members, members)
        rows_in[at : at + height, :] = rows[...]
        indices.append(inbox[0, 0, pl.ds(sender, 1), :][:, :span])
        at += span
    owned = dot(places(jnp.concatenate(indices, axis=1), points), rows_in[...]).astype(BF16)

    def store(at, value):
        mixed[at : at + BALL, :] = value

    attention(owned, w_qkv[...], store)
    for index, out in zip(indices, returned):
        out[...] = dot(picks(index, points), mixed[...])[: out.shape[0]].astype(BF16)


def last_kernel(state, peer, rank, w_out, *refs, members, capacity, light, wide):
    returned, out, rows_in = refs[:members], refs[members], refs[members + 1]
    me = lax.axis_index("rot")
    rows_in[...] = jnp.zeros_like(rows_in)
    at = 0
    for away, rows in zip(senders(members), returned):
        height = capacity if away == 1 else light
        rows_in[at : at + height, :] = rows[...]
        at += capacity if away == 1 else wide
    slots = slot_of(peer[0], rank[0], me, members, capacity, wide)
    update = dot(picks(slots, rows_in.shape[0]), rows_in[...]).astype(BF16)
    out[...] = state[...] + dot(update, w_out[...])


VMEM = pl.BlockSpec(memory_space=pltpu.VMEM)
SMEM = pl.BlockSpec(memory_space=pltpu.SMEM)


def call(kernel, args, outs, scalars=(), scratch=(), flops=0, name=None):
    return pl.pallas_call(
        kernel,
        out_shape=[jax.ShapeDtypeStruct(shape, kind) for shape, kind in outs],
        in_specs=[SMEM if i in scalars else VMEM for i in range(len(args))],
        out_specs=[VMEM] * len(outs),
        scratch_shapes=[pltpu.VMEM(shape, kind) for shape, kind in scratch],
        compiler_params=pltpu.CompilerParams(vmem_limit_bytes=48 * 1024 * 1024),
        cost_estimate=pl.CostEstimate(flops=flops, bytes_accessed=1 << 20, transcendentals=0),
        name=name,
    )(*args)


def swaps(axis, first):
    n_grp, n_rot = lax.axis_size("grp"), lax.axis_size("rot")
    count = n_grp if axis == "grp" else n_rot
    partner = {i: i for i in range(count)}
    for low in range(first, count - 1, 2):
        partner[low], partner[low + 1] = low + 1, low
    if axis == "rot" and first == 1 and count % 2 == 0:
        partner[0], partner[count - 1] = count - 1, 0
    out = []
    for g in range(n_grp):
        for r in range(n_rot):
            to = (partner[g], r) if axis == "grp" else (g, partner[r])
            if to == (g, r) and axis == "grp" and n_rot % 2 == 0:
                to = (g, r ^ 1)
            out.append((g * n_rot + r, to[0] * n_rot + to[1]))
    return out


def exchange(rims):
    plan = [swaps("grp", 0), swaps("grp", 1), swaps("rot", 0), swaps("rot", 1)]
    moved = [None] * 4
    for i in (1, 0, 3, 2):
        moved[i] = lax.ppermute(rims[i], ("grp", "rot"), plan[i])
    return moved


def relay(parts, members, back):
    moved = []
    for away, rows in zip(senders(members), parts):
        if away == 0:
            moved.append(rows)
            continue
        step = members - away if back else away
        moved.append(lax.ppermute(rows, "rot", [(i, (i + step) % members) for i in range(members)]))
    return moved


def local(
    features, w_msg, w_upd, local_tiles, local_src, local_live, border_tiles, border_rows,
    border_block, ball_order, w_ball_qkv, w_ball_out, w_mlp_in, w_mlp_out, w_rot_qkv,
    w_rot_out, relay_peer, relay_rank, relay_inbox,
):
    points, width = features.shape
    members, capacity = lax.axis_size("rot"), relay_inbox.shape[-1]
    rim = border_rows.shape[-1]
    most = up_to(points - capacity, members - 1) // (members - 1)
    light, wide = up_to(most, 16), up_to(most, LANES)
    rims_shape = [((rim, width), BF16)] * 4
    grid, grid16 = ((points, width), F32), ((points, width), BF16)

    messages, *rims = call(
        first_kernel, (features, w_msg, border_rows), [grid16] + rims_shape, name="first_messages"
    )
    received = exchange(rims)
    (aggregate,) = call(
        local_kernel, (messages, local_tiles, local_src, local_live), [grid], scalars=(2, 3),
        name="local_edges",
    )
    state, messages, *rims = call(
        middle_kernel,
        (features, aggregate, *received, border_tiles, border_block, w_msg, w_upd, border_rows),
        [grid, grid16] + rims_shape, scalars=(7,), scratch=[grid], name="second_messages",
    )
    received = exchange(rims)
    (aggregate,) = call(
        local_kernel, (messages, local_tiles, local_src, local_live), [grid], scalars=(2, 3),
        name="local_edges_again",
    )
    sizes = dict(members=members, capacity=capacity, light=light)
    part_shapes = [((capacity, width), BF16)] + [((light, width), BF16)] * (members - 1)

    def bound(kernel, **kw):
        return lambda *refs: kernel(*refs, **kw)

    state, *parts = call(
        bound(ball_kernel, **sizes),
        (
            state, aggregate, *received, border_tiles, border_block, w_upd, ball_order,
            w_ball_qkv, w_ball_out, w_mlp_in, w_mlp_out, relay_peer, relay_rank,
        ),
        [grid] + part_shapes, scalars=(7,), scratch=[grid, grid16], name="ball_layer",
    )
    parts = relay(parts, members, False)
    rows_in = ((capacity + (members - 1) * wide, width), BF16)
    parts = call(
        bound(owner_kernel, wide=wide, **sizes), (relay_inbox, w_rot_qkv, *parts), part_shapes,
        scratch=[rows_in, grid16], name="owner_layer",
    )
    parts = relay(parts, members, True)
    (out,) = call(
        bound(last_kernel, wide=wide, **sizes), (state, relay_peer, relay_rank, w_rot_out, *parts),
        [grid], scratch=[rows_in], name="relayed_changes",
    )
    return out


def solution(mesh):
    table = P("grp", "rot", None)
    in_specs = (
        P(("grp", "rot"), None), P(), P(),
        P("grp", "rot", None, None, None, None),
        P("grp", "rot", None, None), P("grp", "rot", None, None),
        P("grp", "rot", None, None, None),
        P("grp", "rot", None, None), table, table,
        P(), P(), P(), P(), P(), P(),
        table, table, P("grp", "rot", None, None),
    )
    out_specs = P(("grp", "rot"), None)
    return jax.shard_map(local, mesh=mesh, in_specs=in_specs, out_specs=out_specs, check_vma=False)
```

time: 166 us -> 61.1 us (0.37); the launches traced: 164 us -> 60.9 us
  local copies, waits for them, and re-layouts: 54.9 us -> 3 us
  matrix products: 40.1 us -> 0 us
  Pallas kernels: 0 us -> 28.9 us
  waiting for transfers between devices: 30.2 us -> 14.7 us
  starting transfers between devices: 29.1 us -> 14.1 us
  other arithmetic: 8.88 us -> 0 us
    pallas_call x0 -> x7, Pallas kernels: none -> 28.9 us  [call(): pl.pallas_call(kernel, out_shape=[jax.ShapeDtypeStruct(shape, kind) for s...]
    all_to_all x2 -> x0, waiting for transfers between devices: 28.8 us -> none  [the longest x1 14.4 us: relay_layer(): lax.all_to_all(outgoing, 'rot', split_axis=0, concat_axis=0, tiled=True)]
    dot_general x17 -> x0, matrix products: 25.4 us -> none  [the longest x2 8.45 us: attend(): jnp.einsum('bhqk,bkhe->bqhe', weights, values_all, preferred_element_type...]
    gather x8 -> x0, local copies, waits for them, and re-layouts: 23.4 us -> none  [the longest x1 9.06 us: owner_work(): return padded[inbox_rows]]
    sub x2 -> x0, matrix products: 14.7 us -> none  [attend(): weights = jax.nn.softmax(scores, axis=-1).astype(jnp.bfloat16)]
    scatter x2 -> x0, local copies, waits for them, and re-layouts: 14.6 us -> none  [the longest x1 9.32 us: owner_work(): owned = jnp.zeros((weight_rows() + 1, width), jnp.bfloat16).at[inbox_rows...]
    ppermute x8 -> x14, waiting for transfers between devices: 1.35 us -> 14.7 us  [the longest x6 11.5 us: relay(): lax.ppermute(rows, 'rot', [(i, (i + step) % members) for i in range(membe...]
    ppermute x8 -> x14, starting transfers between devices: 21.8 us -> 14.1 us  [the longest x8 8.6 us: exchange(): moved[i] = lax.ppermute(rims[i], ('grp', 'rot'), plan[i])]
  transfers between devices with their start and end apart: 10 -> 14, of which waited for: 4 -> 7; matrix products, arithmetic and copies ran while one was open for 2% -> 0% of each run, Pallas kernels for 0% -> 4%
where the time goes in v1:
time: 61.1 us; the launch traced here: 60.9 us
  Pallas kernels  28.9 us (47%)
  waiting for transfers between devices  14.7 us (24%)
  starting transfers between devices  14.1 us (23%)
  local copies, waits for them, and re-layouts  3 us (5%)
    pallas_call x7, Pallas kernels, call(): pl.pallas_call(kernel, out_shape=[jax.ShapeDtypeStruct(shape, kind) for s...  28.9 us
    ppermute x6, waiting for transfers between devices, relay(): lax.ppermute(rows, 'rot', [(i, (i + step) % members) for i in range(membe...  11.5 us
    ppermute x8, starting transfers between devices, exchange(): moved[i] = lax.ppermute(rims[i], ('grp', 'rot'), plan[i])  8.6 us
    ppermute x6, starting transfers between devices, relay(): lax.ppermute(rows, 'rot', [(i, (i + step) % members) for i in range(membe...  5.54 us
    ppermute x8, waiting for transfers between devices, exchange(): moved[i] = lax.ppermute(rims[i], ('grp', 'rot'), plan[i])  3.17 us
    unnamed x46, local copies, waits for them, and re-layouts  3 us
  transfers between devices with their start and end apart: 14, of which 7 were waited for; matrix products, arithmetic and copies ran while one was open for 0% of the time, Pallas kernels for 4%

profile of v1, /device:TPU:0, one launch (start us, length us, event | category | flops | bytes accessed | tf_op | source)
XLA Modules:
  0.0 60.9 jit_solution(863485941030310340)
XLA Ops:
  0.0 1.1 %copy-done.1 = bf16[1024,256]{1,0:T(8,128)(2,1)S(1)} copy-done((bf16[1024,256]{1,0:T(8,128)(2,1)S(1)}, bf16[1024,256]{1,0:T(8,128)(2,1)}, u32[]{:S(2)}) %copy-start.1) | copy-done | bytes 524312
  1.1 0.9 %copy-done.3 = bf16[2,256,256]{2,1,0:T(8,128)(2,1)S(1)} copy-done((bf16[2,256,256]{2,1,0:T(8,128)(2,1)S(1)}, bf16[2,256,256]{2,1,0:T(8,128)(2,1)}, u32[]{:S(2)}) %copy-start.3) | copy-done | bytes 262168
  2.1 0.7 %copy-done.16 = s32[1,1,4,128]{3,2,1,0:T(4,128)S(1)} copy-done((s32[1,1,4,128]{3,2,1,0:T(4,128)S(1)}, s32[1,1,4,128]{3,2,1,0:T(4,128)}, u32[]{:S(2)}) %copy-start.16) | copy-done | bytes 2072
  2.8 0.9 %first_messages.1 = (bf16[1024,256]{1,0:T(8,128)(2,1)S(1)}, bf16[128,256]{1,0:T(8,128)(2,1)S(1)}, bf16[128,256]{1,0:T(8,128)(2,1)S(1)}, bf16[128,256]{1,0:T(8,128)(2,1)S(1)}, bf16[128,256]{1,0:T(8,128)(2,1)S(1)}) custom-call(bf16[1024,256]{1,0:T(8,128)(2,1)S(1)} %copy-done.1, bf16[2,256,256]{2,1,0:T(8,128)(2,1)S(1)} %copy-done.3, s32[1,1,4,128]{3,2,1,0:T(4,128)S(1)} %copy-done.16), custom_call_target="tpu_custom_call" | custom-call | bytes 1048576 | tf_op jit(solution)/shard_map/first_messages/pallas_call | solution.py:230
  3.7 3.0 %collective-permute-start = (bf16[128,256]{1,0:T(8,128)(2,1)S(1)}, bf16[128,256]{1,0:T(8,128)(2,1)S(1)}, u32[]{:S(2)}, u32[]{:S(2)}) collective-permute-start(bf16[128,256]{1,0:T(8,128)(2,1)S(1)} %get-tuple-element.26), channel_id=1, source_target_pairs={{0,4},{1,5},{2,6},{3,7},{4,0},{5,1},{6,2},{7,3},{8,12},{9,13},{10,... | collective-permute-start | bytes 196616 | tf_op jit(solution)/shard_map/ppermute | solution.py:264
  6.7 0.0 collective-permute-start.1
  6.7 0.5 collective-permute-start.2
  7.2 1.1 %collective-permute-start.3 = (bf16[128,256]{1,0:T(8,128)(2,1)S(1)}, bf16[128,256]{1,0:T(8,128)(2,1)S(1)}, u32[]{:S(2)}, u32[]{:S(2)}) collective-permute-start(bf16[128,256]{1,0:T(8,128)(2,1)S(1)} %get-tuple-element.29), channel_id=1, source_target_pairs={{0,3},{1,2},{2,1},{3,0},{4,7},{5,6},{6,5},{7,4},{8,11},{9,10},{10,... | collective-permute-start | bytes 196616 | tf_op jit(solution)/shard_map/ppermute | solution.py:264
  8.3 0.0 copy-done.20
  8.4 0.1 copy.20.source
  8.4 0.0 copy-done.21
  8.4 0.1 copy.21.live
  8.5 0.0 copy-done
  8.5 0.0 copy-start.8
  8.5 0.0 copy-start.17
  8.6 0.0 copy-start.19
  8.6 1.2 %local_edges.1.aggregate = f32[1024,256]{1,0:T(8,128)S(1)} custom-call(bf16[1024,256]{1,0:T(8,128)(2,1)S(1)} %get-tuple-element.25.messages, bf16[1,1,8,3,128,128]{5,4,3,2,1,0:T(8,128)(2,1)S(1)} %copy-done, s32[1,1,8,3]{3,2,1,0:T(8,128)S(1)} %copy.20.source, s32[1,1,8,3]{3,2,1,0:T(8,128)S(1)} %copy.21.live), custom_call_target="tpu_custom_call" | custom-call | bytes 1048576 | tf_op jit(solution)/shard_map/local_edges/pallas_call | solution.py:230
  9.8 0.0 collective-permute-done.rec0
  9.8 0.0 collective-permute-done.1.rec1
  9.8 0.0 collective-permute-done.2.rec2
  9.8 1.6 %collective-permute-done.3.rec3 = bf16[128,256]{1,0:T(8,128)(2,1)S(1)} collective-permute-done((bf16[128,256]{1,0:T(8,128)(2,1)S(1)}, bf16[128,256]{1,0:T(8,128)(2,1)S(1)}, u32[]{:S(2)}, u32[]{:S(2)}) %collective-permute-start.3) | collective-permute-done | bytes 65568 | tf_op jit(solution)/shard_map/ppermute | solution.py:264
  11.4 0.0 copy-done.2
  11.4 0.0 copy-done.4
  11.4 0.0 copy-done.5
  11.4 0.0 copy-done.8
  11.4 0.0 copy-done.17
  11.5 0.0 copy-done.19
  11.5 1.8 %second_messages.1 = (f32[1024,256]{1,0:T(8,128)S(1)}, bf16[1024,256]{1,0:T(8,128)(2,1)S(1)}, bf16[128,256]{1,0:T(8,128)(2,1)S(1)}, bf16[128,256]{1,0:T(8,128)(2...) custom-call(bf16[1024,256]{1,0:T(8,128)(2,1)S(1)} %copy-done.2, ...), custom_call_target="tpu_custom_call" | custom-call | bytes 1048576 | tf_op jit(solution)/shard_map/second_messages/pallas_call | solution.py:230
  13.3 2.1 %collective-permute-start.4 = (bf16[128,256]{1,0:T(8,128)(2,1)S(1)}, bf16[128,256]{1,0:T(8,128)(2,1)S(1)}, u32[]{:S(2)}, u32[]{:S(2)}) collective-permute-start(bf16[128,256]{1,0:T(8,128)(2,1)S(1)} %get-tuple-element.32), channel_id=1, source_target_pairs={{0,4},{1,5},{2,6},{3,7},{4,0},{5,1},{6,2},{7,3},{8,12},{9,13},{10,... | collective-permute-start | bytes 196616 | tf_op jit(solution)/shard_map/ppermute | solution.py:264
  15.5 0.2 collective-permute-start.5
  15.6 0.3 collective-permute-start.6
  16.0 1.3 %collective-permute-start.7 = (bf16[128,256]{1,0:T(8,128)(2,1)S(1)}, bf16[128,256]{1,0:T(8,128)(2,1)S(1)}, u32[]{:S(2)}, u32[]{:S(2)}) collective-permute-start(bf16[128,256]{1,0:T(8,128)(2,1)S(1)} %get-tuple-element.35), channel_id=1, source_target_pairs={{0,3},{1,2},{2,1},{3,0},{4,7},{5,6},{6,5},{7,4},{8,11},{9,10},{10,... | collective-permute-start | bytes 196616 | tf_op jit(solution)/shard_map/ppermute | solution.py:264
  17.3 0.0 copy-start.13
  17.3 0.0 copy-start.14
  17.3 0.0 copy-start.18
  17.3 1.2 %local_edges_again.1.refs_1_ = f32[1024,256]{1,0:T(8,128)S(1)} custom-call(bf16[1024,256]{1,0:T(8,128)(2,1)S(1)} %get-tuple-element.31.messages, bf16[1,1,8,3,128,128]{5,4,3,2,1,0:T(8,128)(2,1)S(1)} %copy-done, s32[1,1,8,3]{3,2,1,0:T(8,128)S(1)} %copy.20.source, s32[1,1,8,3]{3,2,1,0:T(8,128)S(1)} %copy.21.live), custom_call_target="tpu_custom_call" | custom-call | bytes 1048576 | tf_op jit(solution)/shard_map/local_edges_again/pallas_call | solution.py:230
  18.5 0.3 collective-permute-done.4.refs_2_
  18.9 0.0 collective-permute-done.5.refs_3_
  18.9 0.0 collective-permute-done.6.refs_4_
  18.9 1.2 %collective-permute-done.7.refs_5_ = bf16[128,256]{1,0:T(8,128)(2,1)S(1)} collective-permute-done((bf16[128,256]{1,0:T(8,128)(2,1)S(1)}, bf16[128,256]{1,0:T(8,128)(2,1)S(1)}, u32[]{:S(2)}, u32[]{:S(2)}) %collective-permute-start.7) | collective-permute-done | bytes 65568 | tf_op jit(solution)/shard_map/ppermute | solution.py:264
  20.1 0.0 copy-done.6
  20.1 0.0 copy-done.7
  20.1 0.0 copy-done.10
  20.1 0.0 copy-done.12
  20.1 0.0 copy-done.13
  20.1 0.0 copy-start.9
  20.1 0.0 copy-start.15
  20.2 12.5 %ball_layer.1 = (f32[1024,256]{1,0:T(8,128)S(1)}, bf16[512,256]{1,0:T(8,128)(2,1)S(1)}, bf16[176,256]{1,0:T(8,128)(2,1)S(1)}, bf16[176,256]{1,0:T(8,128)(2,1)S(1)}, bf16[176,256]{1,0:T(8,128)(2,1)S(1)}) custom-call(f32[1024,256]{1,0:T(8,128)S(1)} %get-tuple-element.30.refs_0_, f32[1024,256]{1,0:T(8,128)S(1)} %local_edges_again.1.refs_1_, ...), custom_call_target="tpu_custom_call" | custom-call | bytes 1048576 | tf_op jit(solution)/shard_map/ball_layer/pallas_call | solution.py:230
  32.6 0.2 collective-permute-start.8
  32.8 1.5 %collective-permute-start.9 = (bf16[176,256]{1,0:T(8,128)(2,1)S(1)}, bf16[176,256]{1,0:T(8,128)(2,1)S(1)}, u32[]{:S(2)}, u32[]{:S(2)}) collective-permute-start(bf16[176,256]{1,0:T(8,128)(2,1)S(1)} %get-tuple-element.39), channel_id=1, source_target_pairs={{0,2},{1,3},{2,0},{3,1},{4,6},{5,7},{6,4},{7,5},{8,10},{9,11},{10,... | collective-permute-start | bytes 270344 | tf_op jit(solution)/shard_map/ppermute | solution.py:275
  34.3 1.3 %collective-permute-start.10 = (bf16[176,256]{1,0:T(8,128)(2,1)S(1)}, bf16[176,256]{1,0:T(8,128)(2,1)S(1)}, u32[]{:S(2)}, u32[]{:S(2)}) collective-permute-start(bf16[176,256]{1,0:T(8,128)(2,1)S(1)} %get-tuple-element.40), channel_id=1, source_target_pairs={{0,3},{1,0},{2,1},{3,2},{4,7},{5,4},{6,5},{7,6},{8,11},{9,8},{10,9... | collective-permute-start | bytes 270344 | tf_op jit(solution)/shard_map/ppermute | solution.py:275
  35.7 2.6 %collective-permute-done.9.refs_4_ = bf16[176,256]{1,0:T(8,128)(2,1)S(1)} collective-permute-done((bf16[176,256]{1,0:T(8,128)(2,1)S(1)}, bf16[176,256]{1,0:T(8,128)(2,1)S(1)}, u32[]{:S(2)}, u32[]{:S(2)}) %collective-permute-start.9) | collective-permute-done | bytes 90144 | tf_op jit(solution)/shard_map/ppermute | solution.py:275
  38.3 1.0 %collective-permute-done.10.refs_5_ = bf16[176,256]{1,0:T(8,128)(2,1)S(1)} collective-permute-done((bf16[176,256]{1,0:T(8,128)(2,1)S(1)}, bf16[176,256]{1,0:T(8,128)(2,1)S(1)}, u32[]{:S(2)}, u32[]{:S(2)}) %collective-permute-start.10) | collective-permute-done | bytes 90144 | tf_op jit(solution)/shard_map/ppermute | solution.py:275
  39.2 1.2 %collective-permute-done.8.refs_2_ = bf16[512,256]{1,0:T(8,128)(2,1)S(1)} collective-permute-done((bf16[512,256]{1,0:T(8,128)(2,1)S(1)}, bf16[512,256]{1,0:T(8,128)(2,1)S(1)}, u32[]{:S(2)}, u32[]{:S(2)}) %collective-permute-start.8) | collective-permute-done | bytes 262176 | tf_op jit(solution)/shard_map/ppermute | solution.py:275
  40.4 0.0 copy-done.15
  40.4 9.1 %owner_layer.1 = (bf16[512,256]{1,0:T(8,128)(2,1)S(1)}, bf16[176,256]{1,0:T(8,128)(2,1)S(1)}, bf16[176,256]{1,0:T(8,128)(2,1)S(1)}, bf16[176,256]{1,0:T(8,128)(2,1)S(1)}) custom-call(s32[1,1,4,512]{3,2,1,0:T(4,128)S(1)} %copy-done.15, bf16[256,768]{1,0:T(8,128)(2,1)S(1)} %copy-done.9, bf16[512,256]{1,0:T(8,128)(2,1)S(1)} %collective-permute-done.8.refs_2_, ...), custom_call_target="tpu_custom_call" | custom-call | bytes 1048576 | tf_op jit(solution)/shard_map/owner_layer/pallas_call | solution.py:230
  49.5 2.0 %collective-permute-start.11 = (bf16[512,256]{1,0:T(8,128)(2,1)S(1)}, bf16[512,256]{1,0:T(8,128)(2,1)S(1)}, u32[]{:S(2)}, u32[]{:S(2)}) collective-permute-start(bf16[512,256]{1,0:T(8,128)(2,1)S(1)} %get-tuple-element.41), channel_id=1, source_target_pairs={{0,3},{1,0},{2,1},{3,2},{4,7},{5,4},{6,5},{7,6},{8,11},{9,8},{10,9... | collective-permute-start | bytes 786440 | tf_op jit(solution)/shard_map/ppermute | solution.py:275
  51.5 0.5 collective-permute-start.12
  52.0 0.0 collective-permute-start.13
  52.0 6.7 %collective-permute-done.12.refs_6_ = bf16[176,256]{1,0:T(8,128)(2,1)S(1)} collective-permute-done((bf16[176,256]{1,0:T(8,128)(2,1)S(1)}, bf16[176,256]{1,0:T(8,128)(2,1)S(1)}, u32[]{:S(2)}, u32[]{:S(2)}) %collective-permute-start.12) | collective-permute-done | bytes 90144 | tf_op jit(solution)/shard_map/ppermute | solution.py:275
  58.8 0.0 collective-permute-done.13.refs_7_
  58.8 0.0 collective-permute-done.11.refs_4_
  58.8 0.0 copy-done.11
  58.8 2.1 %relayed_changes.1 = f32[1024,256]{1,0:T(8,128)} custom-call(f32[1024,256]{1,0:T(8,128)S(1)} %get-tuple-element.36.refs_0_, s32[1,1,1024]{2,1,0:T(1,128)S(1)} %copy-done.13, s32[1,1,1024]{2,1,0:T(1,128)S(1)} %copy-done.14, bf16[256,256]{1,0:T(8,128)(2,1)S(1)} %copy-done.11, bf16[512,256]{1,0:T(8,128)(2,1)S(1)} %collective-permute-done.11.refs_4_, ...), custom_call_target="tpu_custom_call" | custom-call | bytes 1048576 | tf_op jit(solution)/shard_map/relayed_changes/pallas_call | solution.py:230
  (17 shorter events, 0.0 us)
Async XLA Ops:
  0.0 8.5 %copy-start = (bf16[1,1,8,3,128,128]{5,4,3,2,1,0:T(8,128)(2,1)S(1)}, bf16[1,1,8,3,128,128]{5,4,3,2,1,0:T(8,128)(2,1)}, u32[]{:S(2)}) copy-start(bf16[1,1,8,3,128,128]{5,4,3,2,1,0:T(8,128)(2,1)} %tiles.5) | copy-start | bytes 2359300
  0.0 1.1 %copy-start.1 = (bf16[1024,256]{1,0:T(8,128)(2,1)S(1)}, bf16[1024,256]{1,0:T(8,128)(2,1)}, u32[]{:S(2)}) copy-start(bf16[1024,256]{1,0:T(8,128)(2,1)} %state.1) | copy-start | bytes 1572868
  1.1 0.9 %copy-start.3 = (bf16[2,256,256]{2,1,0:T(8,128)(2,1)S(1)}, bf16[2,256,256]{2,1,0:T(8,128)(2,1)}, u32[]{:S(2)}) copy-start(bf16[2,256,256]{2,1,0:T(8,128)(2,1)} %w_msg.3) | copy-start | bytes 786436
  2.1 0.7 %copy-start.16 = (s32[1,1,4,128]{3,2,1,0:T(4,128)S(1)}, s32[1,1,4,128]{3,2,1,0:T(4,128)}, u32[]{:S(2)}) copy-start(s32[1,1,4,128]{3,2,1,0:T(4,128)} %rim_rows.3) | copy-start | bytes 6148
  3.7 6.1 %collective-permute-start = (bf16[128,256]{1,0:T(8,128)(2,1)S(1)}, bf16[128,256]{1,0:T(8,128)(2,1)S(1)}, u32[]{:S(2)}, u32[]{:S(2)}) collective-permute-start(bf16[128,256]{1,0:T(8,128)(2,1)S(1)} %get-tuple-element.26), channel_id=1, source_target_pairs={{0,4},{1,5},{2,6},{3,7},{4,0},{5,1},{6,2},{7,3},{8,12},{9,13},{10,... | collective-permute-start | bytes 196616 | tf_op jit(solution)/shard_map/ppermute | solution.py:264
  6.7 1.6 %copy-start.20 = (s32[1,1,8,3]{2,1,3,0:T(1,128)S(1)}, s32[1,1,8,3]{2,1,3,0:T(1,128)}, u32[]{:S(2)}) copy-start(s32[1,1,8,3]{2,1,3,0:T(1,128)} %param.23) | copy-start | bytes 292
  6.7 3.1 %collective-permute-start.1 = (bf16[128,256]{1,0:T(8,128)(2,1)S(1)}, bf16[128,256]{1,0:T(8,128)(2,1)S(1)}, u32[]{:S(2)}, u32[]{:S(2)}) collective-permute-start(bf16[128,256]{1,0:T(8,128)(2,1)S(1)} %get-tuple-element.27), channel_id=1, source_target_pairs={{0,1},{1,0},{2,3},{3,2},{4,8},{5,9},{6,10},{7,11},{8,4},{9,5},{10,... | collective-permute-start | bytes 196616 | tf_op jit(solution)/shard_map/ppermute | solution.py:264
  6.7 3.1 %collective-permute-start.2 = (bf16[128,256]{1,0:T(8,128)(2,1)S(1)}, bf16[128,256]{1,0:T(8,128)(2,1)S(1)}, u32[]{:S(2)}, u32[]{:S(2)}) collective-permute-start(bf16[128,256]{1,0:T(8,128)(2,1)S(1)} %get-tuple-element.28), channel_id=1, source_target_pairs={{0,1},{1,0},{2,3},{3,2},{4,5},{5,4},{6,7},{7,6},{8,9},{9,8},{10,11... | collective-permute-start | bytes 196616 | tf_op jit(solution)/shard_map/ppermute | solution.py:264
  7.2 1.2 %copy-start.21 = (s32[1,1,8,3]{2,1,3,0:T(1,128)S(1)}, s32[1,1,8,3]{2,1,3,0:T(1,128)}, u32[]{:S(2)}) copy-start(s32[1,1,8,3]{2,1,3,0:T(1,128)} %param.24) | copy-start | bytes 292
  7.2 4.2 %collective-permute-start.3 = (bf16[128,256]{1,0:T(8,128)(2,1)S(1)}, bf16[128,256]{1,0:T(8,128)(2,1)S(1)}, u32[]{:S(2)}, u32[]{:S(2)}) collective-permute-start(bf16[128,256]{1,0:T(8,128)(2,1)S(1)} %get-tuple-element.29), channel_id=1, source_target_pairs={{0,3},{1,2},{2,1},{3,0},{4,7},{5,6},{6,5},{7,4},{8,11},{9,10},{10,... | collective-permute-start | bytes 196616 | tf_op jit(solution)/shard_map/ppermute | solution.py:264
  8.5 2.9 %copy-start.2 = (bf16[1024,256]{1,0:T(8,128)(2,1)S(1)}, bf16[1024,256]{1,0:T(8,128)(2,1)}, u32[]{:S(2)}) copy-start(bf16[1024,256]{1,0:T(8,128)(2,1)} %state.1) | copy-start | bytes 1572868
  8.5 2.9 %copy-start.4 = (bf16[2,256,256]{2,1,0:T(8,128)(2,1)S(1)}, bf16[2,256,256]{2,1,0:T(8,128)(2,1)}, u32[]{:S(2)}) copy-start(bf16[2,256,256]{2,1,0:T(8,128)(2,1)} %w_msg.3) | copy-start | bytes 786436
  8.5 2.9 %copy-start.5 = (bf16[2,256,256]{2,1,0:T(8,128)(2,1)S(1)}, bf16[2,256,256]{2,1,0:T(8,128)(2,1)}, u32[]{:S(2)}) copy-start(bf16[2,256,256]{2,1,0:T(8,128)(2,1)} %refs_8_.1) | copy-start | bytes 786436
  8.5 2.9 %copy-start.8 = (bf16[1,1,4,128,128]{4,3,2,1,0:T(8,128)(2,1)S(1)}, bf16[1,1,4,128,128]{4,3,2,1,0:T(8,128)(2,1)}, u32[]{:S(2)}) copy-start(bf16[1,1,4,128,128]{4,3,2,1,0:T(8,128)(2,1)} %refs_6_.1) | copy-start | bytes 393220
  8.5 2.9 %copy-start.17 = (s32[1,1,4,128]{3,2,1,0:T(4,128)S(1)}, s32[1,1,4,128]{3,2,1,0:T(4,128)}, u32[]{:S(2)}) copy-start(s32[1,1,4,128]{3,2,1,0:T(4,128)} %rim_rows.3) | copy-start | bytes 6148
  8.6 2.9 %copy-start.19 = (s32[1,1,4]{2,1,0:T(1,128)S(1)}, s32[1,1,4]{2,1,0:T(1,128)}, u32[]{:S(2)}) copy-start(s32[1,1,4]{2,1,0:T(1,128)} %refs_7_.1) | copy-start | bytes 52
  13.3 5.6 %collective-permute-start.4 = (bf16[128,256]{1,0:T(8,128)(2,1)S(1)}, bf16[128,256]{1,0:T(8,128)(2,1)S(1)}, u32[]{:S(2)}, u32[]{:S(2)}) collective-permute-start(bf16[128,256]{1,0:T(8,128)(2,1)S(1)} %get-tuple-element.32), channel_id=1, source_target_pairs={{0,4},{1,5},{2,6},{3,7},{4,0},{5,1},{6,2},{7,3},{8,12},{9,13},{10,... | collective-permute-start | bytes 196616 | tf_op jit(solution)/shard_map/ppermute | solution.py:264
  15.5 3.4 %collective-permute-start.5 = (bf16[128,256]{1,0:T(8,128)(2,1)S(1)}, bf16[128,256]{1,0:T(8,128)(2,1)S(1)}, u32[]{:S(2)}, u32[]{:S(2)}) collective-permute-start(bf16[128,256]{1,0:T(8,128)(2,1)S(1)} %get-tuple-element.33), channel_id=1, source_target_pairs={{0,1},{1,0},{2,3},{3,2},{4,8},{5,9},{6,10},{7,11},{8,4},{9,5},{10,... | collective-permute-start | bytes 196616 | tf_op jit(solution)/shard_map/ppermute | solution.py:264
  15.6 3.2 %collective-permute-start.6 = (bf16[128,256]{1,0:T(8,128)(2,1)S(1)}, bf16[128,256]{1,0:T(8,128)(2,1)S(1)}, u32[]{:S(2)}, u32[]{:S(2)}) collective-permute-start(bf16[128,256]{1,0:T(8,128)(2,1)S(1)} %get-tuple-element.34), channel_id=1, source_target_pairs={{0,1},{1,0},{2,3},{3,2},{4,5},{5,4},{6,7},{7,6},{8,9},{9,8},{10,11... | collective-permute-start | bytes 196616 | tf_op jit(solution)/shard_map/ppermute | solution.py:264
  16.0 4.1 %collective-permute-start.7 = (bf16[128,256]{1,0:T(8,128)(2,1)S(1)}, bf16[128,256]{1,0:T(8,128)(2,1)S(1)}, u32[]{:S(2)}, u32[]{:S(2)}) collective-permute-start(bf16[128,256]{1,0:T(8,128)(2,1)S(1)} %get-tuple-element.35), channel_id=1, source_target_pairs={{0,3},{1,2},{2,1},{3,0},{4,7},{5,6},{6,5},{7,4},{8,11},{9,10},{10,... | collective-permute-start | bytes 196616 | tf_op jit(solution)/shard_map/ppermute | solution.py:264
  17.3 2.8 %copy-start.6 = (bf16[256,1024]{1,0:T(8,128)(2,1)S(1)}, bf16[256,1024]{1,0:T(8,128)(2,1)}, u32[]{:S(2)}) copy-start(bf16[256,1024]{1,0:T(8,128)(2,1)} %refs_12_.1) | copy-start | bytes 1572868
  17.3 2.8 %copy-start.7 = (bf16[1024,256]{1,0:T(8,128)(2,1)S(1)}, bf16[1024,256]{1,0:T(8,128)(2,1)}, u32[]{:S(2)}) copy-start(bf16[1024,256]{1,0:T(8,128)(2,1)} %refs_13_.1) | copy-start | bytes 1572868
  17.3 2.8 %copy-start.10 = (bf16[256,768]{1,0:T(8,128)(2,1)S(1)}, bf16[256,768]{1,0:T(8,128)(2,1)}, u32[]{:S(2)}) copy-start(bf16[256,768]{1,0:T(8,128)(2,1)} %refs_10_.1) | copy-start | bytes 1179652
  17.3 2.8 %copy-start.12 = (bf16[256,256]{1,0:T(8,128)(2,1)S(1)}, bf16[256,256]{1,0:T(8,128)(2,1)}, u32[]{:S(2)}) copy-start(bf16[256,256]{1,0:T(8,128)(2,1)} %refs_11_.1) | copy-start | bytes 393220
  17.3 2.8 %copy-start.13 = (s32[1,1,1024]{2,1,0:T(1,128)S(1)}, s32[1,1,1024]{2,1,0:T(1,128)}, u32[]{:S(2)}) copy-start(s32[1,1,1024]{2,1,0:T(1,128)} %refs_1_.3) | copy-start | bytes 12292
  17.3 2.8 %copy-start.14 = (s32[1,1,1024]{2,1,0:T(1,128)S(1)}, s32[1,1,1024]{2,1,0:T(1,128)}, u32[]{:S(2)}) copy-start(s32[1,1,1024]{2,1,0:T(1,128)} %refs_2_.1) | copy-start | bytes 12292
  17.3 2.8 %copy-start.18 = (s32[1,1,1024]{2,1,0:T(1,128)S(1)}, s32[1,1,1024]{2,1,0:T(1,128)}, u32[]{:S(2)}) copy-start(s32[1,1,1024]{2,1,0:T(1,128)} %refs_9_.1) | copy-start | bytes 12292
  20.1 20.3 %copy-start.9 = (bf16[256,768]{1,0:T(8,128)(2,1)S(1)}, bf16[256,768]{1,0:T(8,128)(2,1)}, u32[]{:S(2)}) copy-start(bf16[256,768]{1,0:T(8,128)(2,1)} %refs_1_.2) | copy-start | bytes 1179652
  20.1 20.3 %copy-start.15 = (s32[1,1,4,512]{3,2,1,0:T(4,128)S(1)}, s32[1,1,4,512]{3,2,1,0:T(4,128)}, u32[]{:S(2)}) copy-start(s32[1,1,4,512]{3,2,1,0:T(4,128)} %refs_0_.1) | copy-start | bytes 24580
  32.6 7.8 %collective-permute-start.8 = (bf16[512,256]{1,0:T(8,128)(2,1)S(1)}, bf16[512,256]{1,0:T(8,128)(2,1)S(1)}, u32[]{:S(2)}, u32[]{:S(2)}) collective-permute-start(bf16[512,256]{1,0:T(8,128)(2,1)S(1)} %get-tuple-element.37), channel_id=1, source_target_pairs={{0,1},{1,2},{2,3},{3,0},{4,5},{5,6},{6,7},{7,4},{8,9},{9,10},{10,1... | collective-permute-start | bytes 786440 | tf_op jit(solution)/shard_map/ppermute | solution.py:275
  32.8 5.5 %collective-permute-start.9 = (bf16[176,256]{1,0:T(8,128)(2,1)S(1)}, bf16[176,256]{1,0:T(8,128)(2,1)S(1)}, u32[]{:S(2)}, u32[]{:S(2)}) collective-permute-start(bf16[176,256]{1,0:T(8,128)(2,1)S(1)} %get-tuple-element.39), channel_id=1, source_target_pairs={{0,2},{1,3},{2,0},{3,1},{4,6},{5,7},{6,4},{7,5},{8,10},{9,11},{10,... | collective-permute-start | bytes 270344 | tf_op jit(solution)/shard_map/ppermute | solution.py:275
  34.3 4.9 %collective-permute-start.10 = (bf16[176,256]{1,0:T(8,128)(2,1)S(1)}, bf16[176,256]{1,0:T(8,128)(2,1)S(1)}, u32[]{:S(2)}, u32[]{:S(2)}) collective-permute-start(bf16[176,256]{1,0:T(8,128)(2,1)S(1)} %get-tuple-element.40), channel_id=1, source_target_pairs={{0,3},{1,0},{2,1},{3,2},{4,7},{5,4},{6,5},{7,6},{8,11},{9,8},{10,9... | collective-permute-start | bytes 270344 | tf_op jit(solution)/shard_map/ppermute | solution.py:275
  40.4 18.4 %copy-start.11 = (bf16[256,256]{1,0:T(8,128)(2,1)S(1)}, bf16[256,256]{1,0:T(8,128)(2,1)}, u32[]{:S(2)}) copy-start(bf16[256,256]{1,0:T(8,128)(2,1)} %refs_3_.1) | copy-start | bytes 393220
  49.5 9.3 %collective-permute-start.11 = (bf16[512,256]{1,0:T(8,128)(2,1)S(1)}, bf16[512,256]{1,0:T(8,128)(2,1)S(1)}, u32[]{:S(2)}, u32[]{:S(2)}) collective-permute-start(bf16[512,256]{1,0:T(8,128)(2,1)S(1)} %get-tuple-element.41), channel_id=1, source_target_pairs={{0,3},{1,0},{2,1},{3,2},{4,7},{5,4},{6,5},{7,6},{8,11},{9,8},{10,9... | collective-permute-start | bytes 786440 | tf_op jit(solution)/shard_map/ppermute | solution.py:275
  51.5 7.3 %collective-permute-start.12 = (bf16[176,256]{1,0:T(8,128)(2,1)S(1)}, bf16[176,256]{1,0:T(8,128)(2,1)S(1)}, u32[]{:S(2)}, u32[]{:S(2)}) collective-permute-start(bf16[176,256]{1,0:T(8,128)(2,1)S(1)} %get-tuple-element.43), channel_id=1, source_target_pairs={{0,2},{1,3},{2,0},{3,1},{4,6},{5,7},{6,4},{7,5},{8,10},{9,11},{10,... | collective-permute-start | bytes 270344 | tf_op jit(solution)/shard_map/ppermute | solution.py:275
  52.0 6.7 %collective-permute-start.13 = (bf16[176,256]{1,0:T(8,128)(2,1)S(1)}, bf16[176,256]{1,0:T(8,128)(2,1)S(1)}, u32[]{:S(2)}, u32[]{:S(2)}) collective-permute-start(bf16[176,256]{1,0:T(8,128)(2,1)S(1)} %get-tuple-element.44), channel_id=1, source_target_pairs={{0,1},{1,2},{2,3},{3,0},{4,5},{5,6},{6,7},{7,4},{8,9},{9,10},{10,1... | collective-permute-start | bytes 270344 | tf_op jit(solution)/shard_map/ppermute | solution.py:275

commit v2 on v1

--- a/solution.py
+++ b/solution.py
@@ -43,17 +43,18 @@
     return jnp.transpose(jnp.broadcast_to(lane_row, (LANES, LANES)))
 
 
+def columns(lane_rows):
+    count = lane_rows.shape[1]
+    return jnp.concatenate([column(lane_rows[:, at : at + LANES]) for at in range(0, count, LANES)], axis=0)
+
+
+def picks_by(cols, width):
+    lane = iota(cols.shape, 1)
+    return jnp.concatenate([hot(cols == lane + at) for at in range(0, width, LANES)], axis=1)
+
+
 def picks(lane_rows, width):
-    count = lane_rows.shape[1]
-    out = []
-    for start in range(0, count, LANES):
-        col = column(lane_rows[:, start : start + LANES])
-        out.append(
-            jnp.concatenate(
-                [hot(col == iota((LANES, LANES), 1) + at) for at in range(0, width, LANES)], axis=1
-            )
-        )
-    return jnp.concatenate(out, axis=0)
+    return picks_by(columns(lane_rows), width)
 
 
 def places(lane_rows, height):
@@ -66,38 +67,49 @@
     scale = math.log2(math.e) / math.sqrt(head)
     lane_head = iota((1, width), 1) // head
     masks = [hot(lane_head == h) for h in range(HEADS)]
-    for at in range(0, rows_in.shape[0], BALL):
-        joined = dot(rows_in[at : at + BALL], weight_qkv).astype(BF16)
-        query = joined[:, :width]
-        keys = joined[:, width : 2 * width]
-        values = joined[:, 2 * width :]
-        mixed = jnp.zeros((BALL, width), F32)
+    joined = dot(rows_in, weight_qkv).astype(BF16)
+
+    def mix(ball, weights, values):
+        spread = jnp.concatenate([values * mask for mask in masks], axis=0)
+        store(ball, dot(jnp.concatenate(weights, axis=1), spread).astype(BF16))
+
+    pending = None
+    for ball in range(rows_in.shape[0] // BALL):
+        own = joined[ball * BALL : (ball + 1) * BALL]
+        query, keys, values = own[:, :width], own[:, width : 2 * width], own[:, 2 * width :]
+        weights = []
         for h in range(HEADS):
             scores = dot_rows(query * masks[h], keys)
             top = jnp.max(scores, axis=-1, keepdims=True)
             raw = jnp.exp2((scores - top) * scale)
-            weights = raw * (1.0 / jnp.sum(raw, axis=-1, keepdims=True))
-            mixed = mixed + dot(weights.astype(BF16), values * masks[h])
-        store(at, mixed.astype(BF16))
+            weights.append((raw * (1.0 / jnp.sum(raw, axis=-1, keepdims=True))).astype(BF16))
+        if pending is not None:
+            mix(*pending)
+        pending = (ball, weights, values)
+    mix(*pending)
 
 
 def gelu(values):
-    inner = math.sqrt(2.0 / math.pi) * (values + 0.044715 * (values * values * values))
-    return 0.5 * values * (1.0 + jnp.tanh(inner))
-
-
-def make_rims(messages, rim_rows_ref, out_refs):
-    par_grp = lax.rem(lax.axis_index("grp"), 2)
-    par_rot = lax.rem(lax.axis_index("rot"), 2)
-    sides = (1 - par_grp, par_grp, 3 - par_rot, 2 + par_rot)
-    for side, out in zip(sides, out_refs):
-        out[...] = dot(picks(rim_rows_ref[0, 0, pl.ds(side, 1), :], messages.shape[0]), messages).astype(BF16)
-
-
-def first_kernel(features, w_msg, rim_rows, messages_out, *rims_out):
+    root = math.sqrt(2.0 / math.pi)
+    inner = values * (root + (root * 0.044715) * (values * values))
+    return values * (0.5 + 0.5 * jnp.tanh(inner))
+
+
+def rim_kernel(rim_rows, chosen):
+    par_grp, par_rot = lax.rem(lax.axis_index("grp"), 2), lax.rem(lax.axis_index("rot"), 2)
+    for at, side in enumerate((1 - par_grp, par_grp, 3 - par_rot, 2 + par_rot)):
+        chosen[at] = columns(rim_rows[0, 0, pl.ds(side, 1), :])
+
+
+def make_rims(messages, chosen, out_refs):
+    for at, out in enumerate(out_refs):
+        out[...] = dot(picks_by(chosen[at], messages.shape[0]), messages).astype(BF16)
+
+
+def first_kernel(chosen, features, w_msg, messages_out, *rims_out):
     messages = dot(normed(features[...].astype(F32)).astype(BF16), w_msg[0]).astype(BF16)
     messages_out[...] = messages
-    make_rims(messages, rim_rows, rims_out)
+    make_rims(messages, chosen, rims_out)
 
 
 def local_kernel(messages, tiles, source, live, aggregate):
@@ -129,7 +141,7 @@
 
 
 def middle_kernel(
-    state, aggregate, rec0, rec1, rec2, rec3, tiles, block, w_msg, w_upd, rim_rows,
+    state, aggregate, rec0, rec1, rec2, rec3, tiles, block, w_msg, w_upd, chosen,
     state_out, messages_out, rim0, rim1, rim2, rim3, total,
 ):
     total[...] = aggregate[...]
@@ -138,7 +150,7 @@
     state_out[...] = new
     messages = dot(normed(new).astype(BF16), w_msg[1]).astype(BF16)
     messages_out[...] = messages
-    make_rims(messages, rim_rows, (rim0, rim1, rim2, rim3))
+    make_rims(messages, chosen, (rim0, rim1, rim2, rim3))
 
 
 def slot_of(peer, rank, me, members, capacity, light):
@@ -148,31 +160,44 @@
 
 
 def ball_kernel(
-    state, aggregate, rec0, rec1, rec2, rec3, tiles, block, w_upd, order,
-    w_qkv, w_out, w_in, w_mlp_out, peer, rank, state_out, *refs, members, capacity, light,
+    state, aggregate, rec0, rec1, rec2, rec3, tiles, block, w_upd, order, w_qkv,
+    state_out, mixed, total,
 ):
-    *outgoing, total, mixed = refs
     total[...] = aggregate[...]
     add_border(total, (rec0, rec1, rec2, rec3), tiles, block)
     points = state.shape[0]
     new = state[...] + dot(gelu(total[...]).astype(BF16), w_upd[1])
+    state_out[...] = new
     unit = normed(new).astype(BF16)
-    balled = dot(picks(order[0], points), unit).astype(BF16)
-
-    def store(at, value):
-        mixed[at : at + BALL, :] = value
-
-    attention(balled, w_qkv[...], store)
+    balled = [
+        dot(picks(order[0][:, at : at + BALL], points), unit).astype(BF16)
+        for at in range(0, points, BALL)
+    ]
+
+    def store(ball, value):
+        mixed[ball * BALL : (ball + 1) * BALL, :] = value
+
+    attention(jnp.concatenate(balled, axis=0), w_qkv[...], store)
+
+
+def feed_kernel(
+    state, mixed, order, w_out, w_in, w_mlp_out, peer, rank, state_out, *outgoing,
+    members, capacity, light,
+):
+    points = state.shape[0]
     back = dot(places(order[0], points), mixed[...]).astype(BF16)
-    new = new + dot(back, w_out[...])
-    hidden = gelu(dot(normed(new).astype(BF16), w_in[...])).astype(BF16)
-    new = new + dot(hidden, w_mlp_out[...])
-    state_out[...] = new
+    starts = range(0, points, BALL)
+    pieces = [state[at : at + BALL, :] + dot(back[at : at + BALL], w_out[...]) for at in starts]
+    inner = [dot(normed(piece).astype(BF16), w_in[...]) for piece in pieces]
+    units = []
+    for at, piece, values in zip(starts, pieces, inner):
+        piece = piece + dot(gelu(values).astype(BF16), w_mlp_out[...])
+        state_out[at : at + BALL, :] = piece
+        units.append(normed(piece).astype(BF16))
     me = lax.axis_index("rot")
     slots = slot_of(peer[0], rank[0], me, members, capacity, light)
-    unit = normed(new).astype(BF16)
     total_slots = capacity + (members - 1) * light
-    sent = dot(places(slots, total_slots), unit).astype(BF16)
+    sent = dot(places(slots, total_slots), jnp.concatenate(units, axis=0)).astype(BF16)
     outgoing[0][...] = sent[:capacity]
     for j in range(1, members):
         at = capacity + (j - 1) * light
@@ -189,19 +214,21 @@
     me = lax.axis_index("rot")
     points = mixed.shape[0]
     indices = []
-    rows_in[...] = jnp.zeros_like(rows_in)
     at = 0
     for away, rows in zip(senders(members), incoming):
         height = capacity if away == 1 else light
         span = capacity if away == 1 else wide
         sender = lax.rem(me - away + members, members)
         rows_in[at : at + height, :] = rows[...]
+        if span > height:
+            rows_in[at + height : at + span, :] = jnp.zeros((span - height, rows_in.shape[1]), BF16)
         indices.append(inbox[0, 0, pl.ds(sender, 1), :][:, :span])
         at += span
-    owned = dot(places(jnp.concatenate(indices, axis=1), points), rows_in[...]).astype(BF16)
-
-    def store(at, value):
-        mixed[at : at + BALL, :] = value
+    index_row = jnp.concatenate(indices, axis=1)
+    owned = dot(places(index_row, points), rows_in[...]).astype(BF16)
+
+    def store(ball, value):
+        mixed[ball * BALL : (ball + 1) * BALL, :] = value
 
     attention(owned, w_qkv[...], store)
     for index, out in zip(indices, returned):
@@ -209,14 +236,16 @@
 
 
 def last_kernel(state, peer, rank, w_out, *refs, members, capacity, light, wide):
-    returned, out, rows_in = refs[:members], refs[members], refs[members + 1]
+    returned, out, rows_in = refs[:members], *refs[members:]
     me = lax.axis_index("rot")
-    rows_in[...] = jnp.zeros_like(rows_in)
     at = 0
     for away, rows in zip(senders(members), returned):
         height = capacity if away == 1 else light
+        span = capacity if away == 1 else wide
         rows_in[at : at + height, :] = rows[...]
-        at += capacity if away == 1 else wide
+        if span > height:
+            rows_in[at + height : at + span, :] = jnp.zeros((span - height, rows_in.shape[1]), BF16)
+        at += span
     slots = slot_of(peer[0], rank[0], me, members, capacity, wide)
     update = dot(picks(slots, rows_in.shape[0]), rows_in[...]).astype(BF16)
     out[...] = state[...] + dot(update, w_out[...])
@@ -226,7 +255,7 @@
 SMEM = pl.BlockSpec(memory_space=pltpu.SMEM)
 
 
-def call(kernel, args, outs, scalars=(), scratch=(), flops=0, name=None):
+def call(kernel, args, outs, scalars=(), scratch=(), flops=0, moved=1 << 20, name=None):
     return pl.pallas_call(
         kernel,
         out_shape=[jax.ShapeDtypeStruct(shape, kind) for shape, kind in outs],
@@ -234,9 +263,13 @@
         out_specs=[VMEM] * len(outs),
         scratch_shapes=[pltpu.VMEM(shape, kind) for shape, kind in scratch],
         compiler_params=pltpu.CompilerParams(vmem_limit_bytes=48 * 1024 * 1024),
-        cost_estimate=pl.CostEstimate(flops=flops, bytes_accessed=1 << 20, transcendentals=0),
+        cost_estimate=pl.CostEstimate(flops=flops, bytes_accessed=moved, transcendentals=0),
         name=name,
     )(*args)
+
+
+def bound(kernel, **kw):
+    return lambda *refs: kernel(*refs, **kw)
 
 
 def swaps(axis, first):
@@ -266,13 +299,13 @@
 
 
 def relay(parts, members, back):
-    moved = []
-    for away, rows in zip(senders(members), parts):
+    moved = list(parts)
+    for at, away in reversed(list(enumerate(senders(members)))):
         if away == 0:
-            moved.append(rows)
             continue
         step = members - away if back else away
-        moved.append(lax.ppermute(rows, "rot", [(i, (i + step) % members) for i in range(members)]))
+        turn = [(i, (i + step) % members) for i in range(members)]
+        moved[at] = lax.ppermute(parts[at], "rot", turn)
     return moved
 
 
@@ -289,8 +322,12 @@
     rims_shape = [((rim, width), BF16)] * 4
     grid, grid16 = ((points, width), F32), ((points, width), BF16)
 
+    (chosen,) = call(
+        rim_kernel, (border_rows,), [((4, rim, LANES), jnp.int32)], flops=1 << 31,
+        moved=1 << 23, name="rim_rows",
+    )
     messages, *rims = call(
-        first_kernel, (features, w_msg, border_rows), [grid16] + rims_shape, name="first_messages"
+        first_kernel, (chosen, features, w_msg), [grid16] + rims_shape, name="first_messages"
     )
     received = exchange(rims)
     (aggregate,) = call(
@@ -299,7 +336,7 @@
     )
     state, messages, *rims = call(
         middle_kernel,
-        (features, aggregate, *received, border_tiles, border_block, w_msg, w_upd, border_rows),
+        (features, aggregate, *received, border_tiles, border_block, w_msg, w_upd, chosen),
         [grid, grid16] + rims_shape, scalars=(7,), scratch=[grid], name="second_messages",
     )
     received = exchange(rims)
@@ -310,16 +347,18 @@
     sizes = dict(members=members, capacity=capacity, light=light)
     part_shapes = [((capacity, width), BF16)] + [((light, width), BF16)] * (members - 1)
 
-    def bound(kernel, **kw):
-        return lambda *refs: kernel(*refs, **kw)
-
-    state, *parts = call(
-        bound(ball_kernel, **sizes),
+    state, mixed = call(
+        ball_kernel,
         (
             state, aggregate, *received, border_tiles, border_block, w_upd, ball_order,
-            w_ball_qkv, w_ball_out, w_mlp_in, w_mlp_out, relay_peer, relay_rank,
+            w_ball_qkv,
         ),
-        [grid] + part_shapes, scalars=(7,), scratch=[grid, grid16], name="ball_layer",
+        [grid, grid16], scalars=(7,), scratch=[grid], name="ball_attention",
+    )
+    state, *parts = call(
+        bound(feed_kernel, **sizes),
+        (state, mixed, ball_order, w_ball_out, w_mlp_in, w_mlp_out, relay_peer, relay_rank),
+        [grid] + part_shapes, name="feed_forward",
     )
     parts = relay(parts, members, False)
     rows_in = ((capacity + (members - 1) * wide, width), BF16)

time: 61.1 us -> 52.1 us (0.85)
  Pallas kernels: 28.9 us -> 21.7 us
  local copies, waits for them, and re-layouts: 3 us -> 1.23 us
    pallas_call x7 -> x9, Pallas kernels: 28.9 us -> 21.7 us  [call(): pl.pallas_call(kernel, out_shape=[jax.ShapeDtypeStruct(shape, kind) for s...]
    unnamed x46 -> x40, local copies, waits for them, and re-layouts: 3 us -> 1.23 us
  transfers between devices with their start and end apart: 14 -> 14, of which waited for: 7 -> 8; matrix products, arithmetic and copies ran while one was open for 0% -> 0% of each run, Pallas kernels for 4% -> 5%
where the time goes in v2:
time: 52.1 us; the launch traced here: 52 us
  Pallas kernels  21.7 us (42%)
  waiting for transfers between devices  14.7 us (28%)
  starting transfers between devices  14.1 us (27%)
  local copies, waits for them, and re-layouts  1.23 us (2%)
    pallas_call x9, Pallas kernels, call(): pl.pallas_call(kernel, out_shape=[jax.ShapeDtypeStruct(shape, kind) for s...  21.7 us
    ppermute x6, waiting for transfers between devices, relay(): moved[at] = lax.ppermute(parts[at], 'rot', turn)  11.5 us
    ppermute x8, starting transfers between devices, exchange(): moved[i] = lax.ppermute(rims[i], ('grp', 'rot'), plan[i])  8.59 us
    ppermute x6, starting transfers between devices, relay(): moved[at] = lax.ppermute(parts[at], 'rot', turn)  5.54 us
    ppermute x8, waiting for transfers between devices, exchange(): moved[i] = lax.ppermute(rims[i], ('grp', 'rot'), plan[i])  3.25 us
    unnamed x40, local copies, waits for them, and re-layouts  1.23 us
  transfers between devices with their start and end apart: 14, of which 8 were waited for; matrix products, arithmetic and copies ran while one was open for 0% of the time, Pallas kernels for 5%

profile of v2, /device:TPU:0, one launch (start us, length us, event | category | flops | bytes accessed | tf_op | source)
XLA Modules:
  0.0 52.0 jit_solution(14670857365272923240)
XLA Ops:
  0.0 0.0 copy-start.1
  0.0 0.8 %copy-done.16 = s32[1,1,4,128]{3,2,1,0:T(4,128)S(1)} copy-done((s32[1,1,4,128]{3,2,1,0:T(4,128)S(1)}, s32[1,1,4,128]{3,2,1,0:T(4,128)}, u32[]{:S(2)}) %copy-start.16) | copy-done | bytes 2072
  0.8 0.1 rim_rows.2.chosen
  0.9 0.1 copy-done.2
  1.0 0.2 copy-done.1
  1.1 0.9 %first_messages.1 = (bf16[1024,256]{1,0:T(8,128)(2,1)S(1)}, bf16[128,256]{1,0:T(8,128)(2,1)S(1)}, bf16[128,256]{1,0:T(8,128)(2,1)S(1)}, bf16[128,256]{1,0:T(8,128)(2,1)S(1)}, bf16[128,256]{1,0:T(8,128)(2,1)S(1)}) custom-call(s32[4,128,128]{2,1,0:T(8,128)S(1)} %rim_rows.2.chosen, bf16[1024,256]{1,0:T(8,128)(2,1)S(1)} %copy-done.1, ...), custom_call_target="tpu_custom_call" | custom-call | bytes 1048576 | tf_op jit(solution)/shard_map/first_messages/pallas_call | solution.py:259
  2.1 3.0 %collective-permute-start = (bf16[128,256]{1,0:T(8,128)(2,1)S(1)}, bf16[128,256]{1,0:T(8,128)(2,1)S(1)}, u32[]{:S(2)}, u32[]{:S(2)}) collective-permute-start(bf16[128,256]{1,0:T(8,128)(2,1)S(1)} %get-tuple-element.28), channel_id=1, source_target_pairs={{0,4},{1,5},{2,6},{3,7},{4,0},{5,1},{6,2},{7,3},{8,12},{9,13},{10,... | collective-permute-start | bytes 196616 | tf_op jit(solution)/shard_map/ppermute | solution.py:297
  5.1 0.0 collective-permute-start.1
  5.1 0.5 collective-permute-start.2
  5.6 1.1 %collective-permute-start.3 = (bf16[128,256]{1,0:T(8,128)(2,1)S(1)}, bf16[128,256]{1,0:T(8,128)(2,1)S(1)}, u32[]{:S(2)}, u32[]{:S(2)}) collective-permute-start(bf16[128,256]{1,0:T(8,128)(2,1)S(1)} %get-tuple-element.31), channel_id=1, source_target_pairs={{0,3},{1,2},{2,1},{3,0},{4,7},{5,6},{6,5},{7,4},{8,11},{9,10},{10,... | collective-permute-start | bytes 196616 | tf_op jit(solution)/shard_map/ppermute | solution.py:297
  6.7 0.0 copy-done.17
  6.7 0.1 copy.20.source
  6.8 0.0 copy-done.18
  6.8 0.1 copy.21.live
  6.9 0.0 copy-done
  6.9 1.2 %local_edges.1.aggregate = f32[1024,256]{1,0:T(8,128)S(1)} custom-call(bf16[1024,256]{1,0:T(8,128)(2,1)S(1)} %get-tuple-element.27.messages, bf16[1,1,8,3,128,128]{5,4,3,2,1,0:T(8,128)(2,1)S(1)} %copy-done, s32[1,1,8,3]{3,2,1,0:T(8,128)S(1)} %copy.20.source, s32[1,1,8,3]{3,2,1,0:T(8,128)S(1)} %copy.21.live), custom_call_target="tpu_custom_call" | custom-call | bytes 1048576 | tf_op jit(solution)/shard_map/local_edges/pallas_call | solution.py:259
  8.1 0.1 collective-permute-done.rec0
  8.2 0.0 collective-permute-done.1.rec1
  8.2 0.0 collective-permute-done.2.rec2
  8.2 1.6 %collective-permute-done.3.rec3 = bf16[128,256]{1,0:T(8,128)(2,1)S(1)} collective-permute-done((bf16[128,256]{1,0:T(8,128)(2,1)S(1)}, bf16[128,256]{1,0:T(8,128)(2,1)S(1)}, u32[]{:S(2)}, u32[]{:S(2)}) %collective-permute-start.3) | collective-permute-done | bytes 65568 | tf_op jit(solution)/shard_map/ppermute | solution.py:297
  9.8 0.0 copy-done.3
  9.8 0.0 copy-done.6
  9.8 0.0 copy-done.15
  9.8 1.8 %second_messages.1 = (f32[1024,256]{1,0:T(8,128)S(1)}, bf16[1024,256]{1,0:T(8,128)(2,1)S(1)}, bf16[128,256]{1,0:T(8,128)(2,1)S(1)}, bf16[128,256]{1,0:T(8,128)(2...) custom-call(bf16[1024,256]{1,0:T(8,128)(2,1)S(1)} %copy-done.1, ...), custom_call_target="tpu_custom_call" | custom-call | bytes 1048576 | tf_op jit(solution)/shard_map/second_messages/pallas_call | solution.py:259
  11.6 2.1 %collective-permute-start.4 = (bf16[128,256]{1,0:T(8,128)(2,1)S(1)}, bf16[128,256]{1,0:T(8,128)(2,1)S(1)}, u32[]{:S(2)}, u32[]{:S(2)}) collective-permute-start(bf16[128,256]{1,0:T(8,128)(2,1)S(1)} %get-tuple-element.34), channel_id=1, source_target_pairs={{0,4},{1,5},{2,6},{3,7},{4,0},{5,1},{6,2},{7,3},{8,12},{9,13},{10,... | collective-permute-start | bytes 196616 | tf_op jit(solution)/shard_map/ppermute | solution.py:297
  13.8 0.2 collective-permute-start.5
  14.0 0.3 collective-permute-start.6
  14.3 1.3 %collective-permute-start.7 = (bf16[128,256]{1,0:T(8,128)(2,1)S(1)}, bf16[128,256]{1,0:T(8,128)(2,1)S(1)}, u32[]{:S(2)}, u32[]{:S(2)}) collective-permute-start(bf16[128,256]{1,0:T(8,128)(2,1)S(1)} %get-tuple-element.37), channel_id=1, source_target_pairs={{0,3},{1,2},{2,1},{3,0},{4,7},{5,6},{6,5},{7,4},{8,11},{9,10},{10,... | collective-permute-start | bytes 196616 | tf_op jit(solution)/shard_map/ppermute | solution.py:297
  15.6 1.2 %local_edges_again.1.aggregate = f32[1024,256]{1,0:T(8,128)S(1)} custom-call(bf16[1024,256]{1,0:T(8,128)(2,1)S(1)} %get-tuple-element.33.messages, bf16[1,1,8,3,128,128]{5,4,3,2,1,0:T(8,128)(2,1)S(1)} %copy-done, s32[1,1,8,3]{3,2,1,0:T(8,128)S(1)} %copy.20.source, s32[1,1,8,3]{3,2,1,0:T(8,128)S(1)} %copy.21.live), custom_call_target="tpu_custom_call" | custom-call | bytes 1048576 | tf_op jit(solution)/shard_map/local_edges_again/pallas_call | solution.py:259
  16.8 0.4 collective-permute-done.4.rec0
  17.2 0.0 collective-permute-done.5.rec1
  17.2 0.0 collective-permute-done.6.rec2
  17.2 1.2 %collective-permute-done.7.rec3 = bf16[128,256]{1,0:T(8,128)(2,1)S(1)} collective-permute-done((bf16[128,256]{1,0:T(8,128)(2,1)S(1)}, bf16[128,256]{1,0:T(8,128)(2,1)S(1)}, u32[]{:S(2)}, u32[]{:S(2)}) %collective-permute-start.7) | collective-permute-done | bytes 65568 | tf_op jit(solution)/shard_map/ppermute | solution.py:297
  18.4 0.0 copy-done.8
  18.4 0.0 copy-done.11
  18.4 0.0 copy-start.9
  18.4 0.0 copy-start.12
  18.4 0.0 copy-start.13
  18.4 5.2 %ball_attention.1 = (f32[1024,256]{1,0:T(8,128)S(1)}, bf16[1024,256]{1,0:T(8,128)(2,1)S(1)}) custom-call(f32[1024,256]{1,0:T(8,128)S(1)} %get-tuple-element.32.state, f32[1024,256]{1,0:T(8,128)S(1)} %local_edges_again.1.aggregate, bf16[128,256]{1,0:T(8,128)(2,1)S(1)} %collective-permute-done.4.rec0, bf16[128,256]{1,0:T(8,128)(2,1)S(1)} %collective-permute-done.5.rec1, ...), custom_call_target="tpu_custom_call" | custom-call | bytes 1048576 | tf_op jit(solution)/shard_map/ball_attention/pallas_call | solution.py:259
  23.7 0.0 copy-done.4
  23.7 0.0 copy-done.5
  23.7 0.0 copy-done.9
  23.7 0.0 copy-done.12
  23.7 0.0 copy-done.13
  23.7 0.0 copy-start.7
  23.8 0.0 copy-start.14
  23.8 3.7 %feed_forward.1 = (f32[1024,256]{1,0:T(8,128)S(1)}, bf16[512,256]{1,0:T(8,128)(2,1)S(1)}, bf16[176,256]{1,0:T(8,128)(2,1)S(1)}, bf16[176,256]{1,0:T(8,128)(2,1)S(1)}, bf16[176,256]{1,0:T(8,128)(2,1)S(1)}) custom-call(f32[1024,256]{1,0:T(8,128)S(1)} %get-tuple-element.38.refs_0_, bf16[1024,256]{1,0:T(8,128)(2,1)S(1)} %get-tuple-element.39.refs_1_, ...), custom_call_target="tpu_custom_call" | custom-call | bytes 1048576 | tf_op jit(solution)/shard_map/feed_forward/pallas_call | solution.py:259
  27.5 0.2 collective-permute-start.8
  27.7 1.5 %collective-permute-start.9 = (bf16[176,256]{1,0:T(8,128)(2,1)S(1)}, bf16[176,256]{1,0:T(8,128)(2,1)S(1)}, u32[]{:S(2)}, u32[]{:S(2)}) collective-permute-start(bf16[176,256]{1,0:T(8,128)(2,1)S(1)} %get-tuple-element.43), channel_id=1, source_target_pairs={{0,2},{1,3},{2,0},{3,1},{4,6},{5,7},{6,4},{7,5},{8,10},{9,11},{10,... | collective-permute-start | bytes 270344 | tf_op jit(solution)/shard_map/ppermute | solution.py:308
  29.2 1.4 %collective-permute-start.10 = (bf16[176,256]{1,0:T(8,128)(2,1)S(1)}, bf16[176,256]{1,0:T(8,128)(2,1)S(1)}, u32[]{:S(2)}, u32[]{:S(2)}) collective-permute-start(bf16[176,256]{1,0:T(8,128)(2,1)S(1)} %get-tuple-element.44), channel_id=1, source_target_pairs={{0,3},{1,0},{2,1},{3,2},{4,7},{5,4},{6,5},{7,6},{8,11},{9,8},{10,9... | collective-permute-start | bytes 270344 | tf_op jit(solution)/shard_map/ppermute | solution.py:308
  30.5 2.6 %collective-permute-done.9.refs_4_ = bf16[176,256]{1,0:T(8,128)(2,1)S(1)} collective-permute-done((bf16[176,256]{1,0:T(8,128)(2,1)S(1)}, bf16[176,256]{1,0:T(8,128)(2,1)S(1)}, u32[]{:S(2)}, u32[]{:S(2)}) %collective-permute-start.9) | collective-permute-done | bytes 90144 | tf_op jit(solution)/shard_map/ppermute | solution.py:308
  33.1 1.0 %collective-permute-done.10.refs_5_ = bf16[176,256]{1,0:T(8,128)(2,1)S(1)} collective-permute-done((bf16[176,256]{1,0:T(8,128)(2,1)S(1)}, bf16[176,256]{1,0:T(8,128)(2,1)S(1)}, u32[]{:S(2)}, u32[]{:S(2)}) %collective-permute-start.10) | collective-permute-done | bytes 90144 | tf_op jit(solution)/shard_map/ppermute | solution.py:308
  34.1 1.2 %collective-permute-done.8.refs_2_ = bf16[512,256]{1,0:T(8,128)(2,1)S(1)} collective-permute-done((bf16[512,256]{1,0:T(8,128)(2,1)S(1)}, bf16[512,256]{1,0:T(8,128)(2,1)S(1)}, u32[]{:S(2)}, u32[]{:S(2)}) %collective-permute-start.8) | collective-permute-done | bytes 262176 | tf_op jit(solution)/shard_map/ppermute | solution.py:308
  35.3 0.0 copy-done.7
  35.3 0.0 copy-done.14
  35.3 5.3 %owner_layer.1 = (bf16[512,256]{1,0:T(8,128)(2,1)S(1)}, bf16[176,256]{1,0:T(8,128)(2,1)S(1)}, bf16[176,256]{1,0:T(8,128)(2,1)S(1)}, bf16[176,256]{1,0:T(8,128)(2,1)S(1)}) custom-call(s32[1,1,4,512]{3,2,1,0:T(4,128)S(1)} %copy-done.14, bf16[256,768]{1,0:T(8,128)(2,1)S(1)} %copy-done.7, bf16[512,256]{1,0:T(8,128)(2,1)S(1)} %collective-permute-done.8.refs_2_, ...), custom_call_target="tpu_custom_call" | custom-call | bytes 1048576 | tf_op jit(solution)/shard_map/owner_layer/pallas_call | solution.py:259
  40.6 2.0 %collective-permute-start.11 = (bf16[512,256]{1,0:T(8,128)(2,1)S(1)}, bf16[512,256]{1,0:T(8,128)(2,1)S(1)}, u32[]{:S(2)}, u32[]{:S(2)}) collective-permute-start(bf16[512,256]{1,0:T(8,128)(2,1)S(1)} %get-tuple-element.45), channel_id=1, source_target_pairs={{0,3},{1,0},{2,1},{3,2},{4,7},{5,4},{6,5},{7,6},{8,11},{9,8},{10,9... | collective-permute-start | bytes 786440 | tf_op jit(solution)/shard_map/ppermute | solution.py:308
  42.6 0.5 collective-permute-start.12
  43.1 0.0 collective-permute-start.13
  43.1 6.7 %collective-permute-done.12.refs_6_ = bf16[176,256]{1,0:T(8,128)(2,1)S(1)} collective-permute-done((bf16[176,256]{1,0:T(8,128)(2,1)S(1)}, bf16[176,256]{1,0:T(8,128)(2,1)S(1)}, u32[]{:S(2)}, u32[]{:S(2)}) %collective-permute-start.12) | collective-permute-done | bytes 90144 | tf_op jit(solution)/shard_map/ppermute | solution.py:308
  49.8 0.0 collective-permute-done.13.refs_7_
  49.8 0.0 collective-permute-done.11.refs_4_
  49.8 0.0 copy-done.10
  49.8 2.1 %relayed_changes.1 = f32[1024,256]{1,0:T(8,128)} custom-call(f32[1024,256]{1,0:T(8,128)S(1)} %get-tuple-element.40.refs_0_, s32[1,1,1024]{2,1,0:T(1,128)S(1)} %copy-done.12, s32[1,1,1024]{2,1,0:T(1,128)S(1)} %copy-done.13, bf16[256,256]{1,0:T(8,128)(2,1)S(1)} %copy-done.10, bf16[512,256]{1,0:T(8,128)(2,1)S(1)} %collective-permute-done.11.refs_4_, ...), custom_call_target="tpu_custom_call" | custom-call | bytes 1048576 | tf_op jit(solution)/shard_map/relayed_changes/pallas_call | solution.py:259
  (13 shorter events, 0.0 us)
Async XLA Ops:
  0.0 1.0 %copy-start.2 = (bf16[2,256,256]{2,1,0:T(8,128)(2,1)S(1)}, bf16[2,256,256]{2,1,0:T(8,128)(2,1)}, u32[]{:S(2)}) copy-start(bf16[2,256,256]{2,1,0:T(8,128)(2,1)} %w_msg.3) | copy-start | bytes 786436
  0.0 1.1 %copy-start.1 = (bf16[1024,256]{1,0:T(8,128)(2,1)S(1)}, bf16[1024,256]{1,0:T(8,128)(2,1)}, u32[]{:S(2)}) copy-start(bf16[1024,256]{1,0:T(8,128)(2,1)} %state.1) | copy-start | bytes 1572868
  0.0 0.8 %copy-start.16 = (s32[1,1,4,128]{3,2,1,0:T(4,128)S(1)}, s32[1,1,4,128]{3,2,1,0:T(4,128)}, u32[]{:S(2)}) copy-start(s32[1,1,4,128]{3,2,1,0:T(4,128)} %rim_rows.3) | copy-start | bytes 6148
  1.1 5.7 %copy-start = (bf16[1,1,8,3,128,128]{5,4,3,2,1,0:T(8,128)(2,1)S(1)}, bf16[1,1,8,3,128,128]{5,4,3,2,1,0:T(8,128)(2,1)}, u32[]{:S(2)}) copy-start(bf16[1,1,8,3,128,128]{5,4,3,2,1,0:T(8,128)(2,1)} %tiles.6) | copy-start | bytes 2359300
  2.1 6.1 %collective-permute-start = (bf16[128,256]{1,0:T(8,128)(2,1)S(1)}, bf16[128,256]{1,0:T(8,128)(2,1)S(1)}, u32[]{:S(2)}, u32[]{:S(2)}) collective-permute-start(bf16[128,256]{1,0:T(8,128)(2,1)S(1)} %get-tuple-element.28), channel_id=1, source_target_pairs={{0,4},{1,5},{2,6},{3,7},{4,0},{5,1},{6,2},{7,3},{8,12},{9,13},{10,... | collective-permute-start | bytes 196616 | tf_op jit(solution)/shard_map/ppermute | solution.py:297
  5.1 1.6 %copy-start.17 = (s32[1,1,8,3]{2,1,3,0:T(1,128)S(1)}, s32[1,1,8,3]{2,1,3,0:T(1,128)}, u32[]{:S(2)}) copy-start(s32[1,1,8,3]{2,1,3,0:T(1,128)} %param.23) | copy-start | bytes 292
  5.1 3.1 %collective-permute-start.1 = (bf16[128,256]{1,0:T(8,128)(2,1)S(1)}, bf16[128,256]{1,0:T(8,128)(2,1)S(1)}, u32[]{:S(2)}, u32[]{:S(2)}) collective-permute-start(bf16[128,256]{1,0:T(8,128)(2,1)S(1)} %get-tuple-element.29), channel_id=1, source_target_pairs={{0,1},{1,0},{2,3},{3,2},{4,8},{5,9},{6,10},{7,11},{8,4},{9,5},{10,... | collective-permute-start | bytes 196616 | tf_op jit(solution)/shard_map/ppermute | solution.py:297
  5.1 3.1 %collective-permute-start.2 = (bf16[128,256]{1,0:T(8,128)(2,1)S(1)}, bf16[128,256]{1,0:T(8,128)(2,1)S(1)}, u32[]{:S(2)}, u32[]{:S(2)}) collective-permute-start(bf16[128,256]{1,0:T(8,128)(2,1)S(1)} %get-tuple-element.30), channel_id=1, source_target_pairs={{0,1},{1,0},{2,3},{3,2},{4,5},{5,4},{6,7},{7,6},{8,9},{9,8},{10,11... | collective-permute-start | bytes 196616 | tf_op jit(solution)/shard_map/ppermute | solution.py:297
  5.6 1.2 %copy-start.18 = (s32[1,1,8,3]{2,1,3,0:T(1,128)S(1)}, s32[1,1,8,3]{2,1,3,0:T(1,128)}, u32[]{:S(2)}) copy-start(s32[1,1,8,3]{2,1,3,0:T(1,128)} %param.24) | copy-start | bytes 292
  5.6 4.2 %collective-permute-start.3 = (bf16[128,256]{1,0:T(8,128)(2,1)S(1)}, bf16[128,256]{1,0:T(8,128)(2,1)S(1)}, u32[]{:S(2)}, u32[]{:S(2)}) collective-permute-start(bf16[128,256]{1,0:T(8,128)(2,1)S(1)} %get-tuple-element.31), channel_id=1, source_target_pairs={{0,3},{1,2},{2,1},{3,0},{4,7},{5,6},{6,5},{7,4},{8,11},{9,10},{10,... | collective-permute-start | bytes 196616 | tf_op jit(solution)/shard_map/ppermute | solution.py:297
  6.9 2.9 %copy-start.3 = (bf16[2,256,256]{2,1,0:T(8,128)(2,1)S(1)}, bf16[2,256,256]{2,1,0:T(8,128)(2,1)}, u32[]{:S(2)}) copy-start(bf16[2,256,256]{2,1,0:T(8,128)(2,1)} %w_upd.3) | copy-start | bytes 786436
  6.9 2.9 %copy-start.6 = (bf16[1,1,4,128,128]{4,3,2,1,0:T(8,128)(2,1)S(1)}, bf16[1,1,4,128,128]{4,3,2,1,0:T(8,128)(2,1)}, u32[]{:S(2)}) copy-start(bf16[1,1,4,128,128]{4,3,2,1,0:T(8,128)(2,1)} %tiles.7) | copy-start | bytes 393220
  6.9 2.9 %copy-start.15 = (s32[1,1,4]{2,1,0:T(1,128)S(1)}, s32[1,1,4]{2,1,0:T(1,128)}, u32[]{:S(2)}) copy-start(s32[1,1,4]{2,1,0:T(1,128)} %block.3) | copy-start | bytes 52
  11.6 5.5 %collective-permute-start.4 = (bf16[128,256]{1,0:T(8,128)(2,1)S(1)}, bf16[128,256]{1,0:T(8,128)(2,1)S(1)}, u32[]{:S(2)}, u32[]{:S(2)}) collective-permute-start(bf16[128,256]{1,0:T(8,128)(2,1)S(1)} %get-tuple-element.34), channel_id=1, source_target_pairs={{0,4},{1,5},{2,6},{3,7},{4,0},{5,1},{6,2},{7,3},{8,12},{9,13},{10,... | collective-permute-start | bytes 196616 | tf_op jit(solution)/shard_map/ppermute | solution.py:297
  13.8 3.4 %collective-permute-start.5 = (bf16[128,256]{1,0:T(8,128)(2,1)S(1)}, bf16[128,256]{1,0:T(8,128)(2,1)S(1)}, u32[]{:S(2)}, u32[]{:S(2)}) collective-permute-start(bf16[128,256]{1,0:T(8,128)(2,1)S(1)} %get-tuple-element.35), channel_id=1, source_target_pairs={{0,1},{1,0},{2,3},{3,2},{4,8},{5,9},{6,10},{7,11},{8,4},{9,5},{10,... | collective-permute-start | bytes 196616 | tf_op jit(solution)/shard_map/ppermute | solution.py:297
  14.0 3.2 %collective-permute-start.6 = (bf16[128,256]{1,0:T(8,128)(2,1)S(1)}, bf16[128,256]{1,0:T(8,128)(2,1)S(1)}, u32[]{:S(2)}, u32[]{:S(2)}) collective-permute-start(bf16[128,256]{1,0:T(8,128)(2,1)S(1)} %get-tuple-element.36), channel_id=1, source_target_pairs={{0,1},{1,0},{2,3},{3,2},{4,5},{5,4},{6,7},{7,6},{8,9},{9,8},{10,11... | collective-permute-start | bytes 196616 | tf_op jit(solution)/shard_map/ppermute | solution.py:297
  14.3 4.1 %collective-permute-start.7 = (bf16[128,256]{1,0:T(8,128)(2,1)S(1)}, bf16[128,256]{1,0:T(8,128)(2,1)S(1)}, u32[]{:S(2)}, u32[]{:S(2)}) collective-permute-start(bf16[128,256]{1,0:T(8,128)(2,1)S(1)} %get-tuple-element.37), channel_id=1, source_target_pairs={{0,3},{1,2},{2,1},{3,0},{4,7},{5,6},{6,5},{7,4},{8,11},{9,10},{10,... | collective-permute-start | bytes 196616 | tf_op jit(solution)/shard_map/ppermute | solution.py:297
  15.6 2.8 %copy-start.8 = (bf16[256,768]{1,0:T(8,128)(2,1)S(1)}, bf16[256,768]{1,0:T(8,128)(2,1)}, u32[]{:S(2)}) copy-start(bf16[256,768]{1,0:T(8,128)(2,1)} %w_qkv.1) | copy-start | bytes 1179652
  15.6 2.8 %copy-start.11 = (s32[1,1,1024]{2,1,0:T(1,128)S(1)}, s32[1,1,1024]{2,1,0:T(1,128)}, u32[]{:S(2)}) copy-start(s32[1,1,1024]{2,1,0:T(1,128)} %refs_2_.2) | copy-start | bytes 12292
  18.4 5.3 %copy-start.4 = (bf16[256,1024]{1,0:T(8,128)(2,1)S(1)}, bf16[256,1024]{1,0:T(8,128)(2,1)}, u32[]{:S(2)}) copy-start(bf16[256,1024]{1,0:T(8,128)(2,1)} %refs_4_.1) | copy-start | bytes 1572868
  18.4 5.3 %copy-start.5 = (bf16[1024,256]{1,0:T(8,128)(2,1)S(1)}, bf16[1024,256]{1,0:T(8,128)(2,1)}, u32[]{:S(2)}) copy-start(bf16[1024,256]{1,0:T(8,128)(2,1)} %refs_5_.1) | copy-start | bytes 1572868
  18.4 5.3 %copy-start.9 = (bf16[256,256]{1,0:T(8,128)(2,1)S(1)}, bf16[256,256]{1,0:T(8,128)(2,1)}, u32[]{:S(2)}) copy-start(bf16[256,256]{1,0:T(8,128)(2,1)} %refs_3_.2) | copy-start | bytes 393220
  18.4 5.3 %copy-start.12 = (s32[1,1,1024]{2,1,0:T(1,128)S(1)}, s32[1,1,1024]{2,1,0:T(1,128)}, u32[]{:S(2)}) copy-start(s32[1,1,1024]{2,1,0:T(1,128)} %refs_1_.3) | copy-start | bytes 12292
  18.4 5.3 %copy-start.13 = (s32[1,1,1024]{2,1,0:T(1,128)S(1)}, s32[1,1,1024]{2,1,0:T(1,128)}, u32[]{:S(2)}) copy-start(s32[1,1,1024]{2,1,0:T(1,128)} %refs_2_.3) | copy-start | bytes 12292
  23.7 11.5 %copy-start.7 = (bf16[256,768]{1,0:T(8,128)(2,1)S(1)}, bf16[256,768]{1,0:T(8,128)(2,1)}, u32[]{:S(2)}) copy-start(bf16[256,768]{1,0:T(8,128)(2,1)} %refs_1_.2) | copy-start | bytes 1179652
  23.8 11.5 %copy-start.14 = (s32[1,1,4,512]{3,2,1,0:T(4,128)S(1)}, s32[1,1,4,512]{3,2,1,0:T(4,128)}, u32[]{:S(2)}) copy-start(s32[1,1,4,512]{3,2,1,0:T(4,128)} %refs_0_.1) | copy-start | bytes 24580
  27.5 7.8 %collective-permute-start.8 = (bf16[512,256]{1,0:T(8,128)(2,1)S(1)}, bf16[512,256]{1,0:T(8,128)(2,1)S(1)}, u32[]{:S(2)}, u32[]{:S(2)}) collective-permute-start(bf16[512,256]{1,0:T(8,128)(2,1)S(1)} %get-tuple-element.41), channel_id=1, source_target_pairs={{0,1},{1,2},{2,3},{3,0},{4,5},{5,6},{6,7},{7,4},{8,9},{9,10},{10,1... | collective-permute-start | bytes 786440 | tf_op jit(solution)/shard_map/ppermute | solution.py:308
  27.7 5.4 %collective-permute-start.9 = (bf16[176,256]{1,0:T(8,128)(2,1)S(1)}, bf16[176,256]{1,0:T(8,128)(2,1)S(1)}, u32[]{:S(2)}, u32[]{:S(2)}) collective-permute-start(bf16[176,256]{1,0:T(8,128)(2,1)S(1)} %get-tuple-element.43), channel_id=1, source_target_pairs={{0,2},{1,3},{2,0},{3,1},{4,6},{5,7},{6,4},{7,5},{8,10},{9,11},{10,... | collective-permute-start | bytes 270344 | tf_op jit(solution)/shard_map/ppermute | solution.py:308
  29.2 4.9 %collective-permute-start.10 = (bf16[176,256]{1,0:T(8,128)(2,1)S(1)}, bf16[176,256]{1,0:T(8,128)(2,1)S(1)}, u32[]{:S(2)}, u32[]{:S(2)}) collective-permute-start(bf16[176,256]{1,0:T(8,128)(2,1)S(1)} %get-tuple-element.44), channel_id=1, source_target_pairs={{0,3},{1,0},{2,1},{3,2},{4,7},{5,4},{6,5},{7,6},{8,11},{9,8},{10,9... | collective-permute-start | bytes 270344 | tf_op jit(solution)/shard_map/ppermute | solution.py:308
  35.3 14.5 %copy-start.10 = (bf16[256,256]{1,0:T(8,128)(2,1)S(1)}, bf16[256,256]{1,0:T(8,128)(2,1)}, u32[]{:S(2)}) copy-start(bf16[256,256]{1,0:T(8,128)(2,1)} %refs_3_.3) | copy-start | bytes 393220
  40.6 9.3 %collective-permute-start.11 = (bf16[512,256]{1,0:T(8,128)(2,1)S(1)}, bf16[512,256]{1,0:T(8,128)(2,1)S(1)}, u32[]{:S(2)}, u32[]{:S(2)}) collective-permute-start(bf16[512,256]{1,0:T(8,128)(2,1)S(1)} %get-tuple-element.45), channel_id=1, source_target_pairs={{0,3},{1,0},{2,1},{3,2},{4,7},{5,4},{6,5},{7,6},{8,11},{9,8},{10,9... | collective-permute-start | bytes 786440 | tf_op jit(solution)/shard_map/ppermute | solution.py:308
  42.6 7.3 %collective-permute-start.12 = (bf16[176,256]{1,0:T(8,128)(2,1)S(1)}, bf16[176,256]{1,0:T(8,128)(2,1)S(1)}, u32[]{:S(2)}, u32[]{:S(2)}) collective-permute-start(bf16[176,256]{1,0:T(8,128)(2,1)S(1)} %get-tuple-element.47), channel_id=1, source_target_pairs={{0,2},{1,3},{2,0},{3,1},{4,6},{5,7},{6,4},{7,5},{8,10},{9,11},{10,... | collective-permute-start | bytes 270344 | tf_op jit(solution)/shard_map/ppermute | solution.py:308
  43.1 6.7 %collective-permute-start.13 = (bf16[176,256]{1,0:T(8,128)(2,1)S(1)}, bf16[176,256]{1,0:T(8,128)(2,1)S(1)}, u32[]{:S(2)}, u32[]{:S(2)}) collective-permute-start(bf16[176,256]{1,0:T(8,128)(2,1)S(1)} %get-tuple-element.48), channel_id=1, source_target_pairs={{0,1},{1,2},{2,3},{3,0},{4,5},{5,6},{6,7},{7,4},{8,9},{9,10},{10,1... | collective-permute-start | bytes 270344 | tf_op jit(solution)/shard_map/ppermute | solution.py:308

commit v3 on v2

--- a/solution.py
+++ b/solution.py
@@ -112,6 +112,16 @@
     make_rims(messages, chosen, rims_out)
 
 
+def slots_kernel(order, peer, rank, after, slots_out, *, members, capacity, light):
+    me = lax.axis_index("rot")
+    slots = slot_of(peer[0], rank[0], me, members, capacity, light)
+    points = slots.shape[1]
+    digits = jnp.concatenate([slots // LANES, lax.rem(slots, LANES)] + [jnp.zeros_like(slots)] * 6, axis=0)
+    moved = dot(digits.astype(F32).astype(BF16), places(order[0], points)).astype(jnp.int32)
+    slots_out[0:1, :] = slots
+    slots_out[1:2, :] = moved[0:1] * LANES + moved[1:2]
+
+
 def local_kernel(messages, tiles, source, live, aggregate):
     tile = tiles.shape[-1]
     blocks, sources = tiles.shape[2], tiles.shape[3]
@@ -180,28 +190,38 @@
     attention(jnp.concatenate(balled, axis=0), w_qkv[...], store)
 
 
-def feed_kernel(
-    state, mixed, order, w_out, w_in, w_mlp_out, peer, rank, state_out, *outgoing,
-    members, capacity, light,
-):
+def feed(pieces, w_in, w_mlp_out):
+    inner = [dot(normed(piece).astype(BF16), w_in[...]) for piece in pieces]
+    return [
+        piece + dot(gelu(values).astype(BF16), w_mlp_out[...])
+        for piece, values in zip(pieces, inner)
+    ]
+
+
+def sent_kernel(state, mixed, slots, w_out, w_in, w_mlp_out, *refs, start, after):
+    outgoing = refs[after:]
+    count = sum(out.shape[0] for out in outgoing)
+    at_row = hot(iota((count, slots.shape[1]), 0) + start == slots[0:1, :])
+    at_ball = hot(iota((count, slots.shape[1]), 0) + start == slots[1:2, :])
+    back = dot(at_ball, mixed[...]).astype(BF16)
+    rows = dot(at_row, state[...].astype(BF16))
+    step = up_to(count // 2, 16)
+    cuts = [slice(0, step), slice(step, count)]
+    done = feed([rows[cut] + dot(back[cut], w_out[...]) for cut in cuts], w_in, w_mlp_out)
+    units = jnp.concatenate([normed(piece).astype(BF16) for piece in done], axis=0)
+    at = 0
+    for out in outgoing:
+        out[...] = units[at : at + out.shape[0]]
+        at += out.shape[0]
+
+
+def kept_kernel(state, mixed, order, w_out, w_in, w_mlp_out, after, state_out):
     points = state.shape[0]
     back = dot(places(order[0], points), mixed[...]).astype(BF16)
     starts = range(0, points, BALL)
     pieces = [state[at : at + BALL, :] + dot(back[at : at + BALL], w_out[...]) for at in starts]
-    inner = [dot(normed(piece).astype(BF16), w_in[...]) for piece in pieces]
-    units = []
-    for at, piece, values in zip(starts, pieces, inner):
-        piece = piece + dot(gelu(values).astype(BF16), w_mlp_out[...])
+    for at, piece in zip(starts, feed(pieces, w_in, w_mlp_out)):
         state_out[at : at + BALL, :] = piece
-        units.append(normed(piece).astype(BF16))
-    me = lax.axis_index("rot")
-    slots = slot_of(peer[0], rank[0], me, members, capacity, light)
-    total_slots = capacity + (members - 1) * light
-    sent = dot(places(slots, total_slots), jnp.concatenate(units, axis=0)).astype(BF16)
-    outgoing[0][...] = sent[:capacity]
-    for j in range(1, members):
-        at = capacity + (j - 1) * light
-        outgoing[j][...] = sent[at : at + light]
 
 
 def senders(members):
@@ -326,6 +346,9 @@
         rim_kernel, (border_rows,), [((4, rim, LANES), jnp.int32)], flops=1 << 31,
         moved=1 << 23, name="rim_rows",
     )
+    sizes = dict(members=members, capacity=capacity, light=light)
+    part_shapes = [((capacity, width), BF16)] + [((light, width), BF16)] * (members - 1)
+
     messages, *rims = call(
         first_kernel, (chosen, features, w_msg), [grid16] + rims_shape, name="first_messages"
     )
@@ -334,6 +357,10 @@
         local_kernel, (messages, local_tiles, local_src, local_live), [grid], scalars=(2, 3),
         name="local_edges",
     )
+    (slots,) = call(
+        bound(slots_kernel, **sizes), (ball_order, relay_peer, relay_rank, messages),
+        [((2, points), jnp.int32)], name="slots",
+    )
     state, messages, *rims = call(
         middle_kernel,
         (features, aggregate, *received, border_tiles, border_block, w_msg, w_upd, chosen),
@@ -344,9 +371,6 @@
         local_kernel, (messages, local_tiles, local_src, local_live), [grid], scalars=(2, 3),
         name="local_edges_again",
     )
-    sizes = dict(members=members, capacity=capacity, light=light)
-    part_shapes = [((capacity, width), BF16)] + [((light, width), BF16)] * (members - 1)
-
     state, mixed = call(
         ball_kernel,
         (
@@ -355,10 +379,18 @@
         ),
         [grid, grid16], scalars=(7,), scratch=[grid], name="ball_attention",
     )
-    state, *parts = call(
-        bound(feed_kernel, **sizes),
-        (state, mixed, ball_order, w_ball_out, w_mlp_in, w_mlp_out, relay_peer, relay_rank),
-        [grid] + part_shapes, name="feed_forward",
+    weights = (w_ball_out, w_mlp_in, w_mlp_out)
+    heavy = call(
+        bound(sent_kernel, start=0, after=0), (state, mixed, slots, *weights), part_shapes[:1],
+        name="heavy_rows",
+    )
+    lighter = call(
+        bound(sent_kernel, start=capacity, after=1), (state, mixed, slots, *weights, *heavy),
+        part_shapes[1:], name="light_rows",
+    )
+    parts = [*heavy, *lighter]
+    (state,) = call(
+        kept_kernel, (state, mixed, ball_order, *weights, lighter[0]), [grid], name="kept_rows",
     )
     parts = relay(parts, members, False)
     rows_in = ((capacity + (members - 1) * wide, width), BF16)

time: 52.1 us -> 50.4 us (0.967)
  waiting for transfers between devices: 14.7 us -> 9.06 us
  Pallas kernels: 21.7 us -> 25.4 us
    ppermute x6, waiting for transfers between devices: 11.5 us -> 6.31 us  [relay(): moved[at] = lax.ppermute(parts[at], 'rot', turn)]
    pallas_call x9 -> x12, Pallas kernels: 21.7 us -> 25.4 us  [call(): pl.pallas_call(kernel, out_shape=[jax.ShapeDtypeStruct(shape, kind) for s...]
  transfers between devices with their start and end apart: 14 -> 14, of which waited for: 8 -> 6; matrix products, arithmetic and copies ran while one was open for 0% -> 0% of each run, Pallas kernels for 5% -> 16%
where the time goes in v3:
time: 50.4 us; the launch traced here: 50.3 us
  Pallas kernels  25.4 us (50%)
  starting transfers between devices  14.4 us (29%)
  waiting for transfers between devices  9.06 us (18%)
  local copies, waits for them, and re-layouts  1.23 us (2%)
    pallas_call x12, Pallas kernels, call(): pl.pallas_call(kernel, out_shape=[jax.ShapeDtypeStruct(shape, kind) for s...  25.4 us
    ppermute x8, starting transfers between devices, exchange(): moved[i] = lax.ppermute(rims[i], ('grp', 'rot'), plan[i])  8.6 us
    ppermute x6, waiting for transfers between devices, relay(): moved[at] = lax.ppermute(parts[at], 'rot', turn)  6.31 us
    ppermute x6, starting transfers between devices, relay(): moved[at] = lax.ppermute(parts[at], 'rot', turn)  5.75 us
    ppermute x8, waiting for transfers between devices, exchange(): moved[i] = lax.ppermute(rims[i], ('grp', 'rot'), plan[i])  2.75 us
    unnamed x40, local copies, waits for them, and re-layouts  1.23 us
  transfers between devices with their start and end apart: 14, of which 6 were waited for; matrix products, arithmetic and copies ran while one was open for 0% of the time, Pallas kernels for 16%

profile of v3, /device:TPU:0, one launch (start us, length us, event | category | flops | bytes accessed | tf_op | source)
XLA Modules:
  0.0 50.3 jit_solution(747699263230813442)
XLA Ops:
  0.0 0.8 %copy-done.16 = s32[1,1,4,128]{3,2,1,0:T(4,128)S(1)} copy-done((s32[1,1,4,128]{3,2,1,0:T(4,128)S(1)}, s32[1,1,4,128]{3,2,1,0:T(4,128)}, u32[]{:S(2)}) %copy-start.16) | copy-done | bytes 2072
  0.8 0.1 rim_rows.2.chosen
  0.9 0.1 copy-done.5
  1.0 0.2 copy-done.3
  1.1 0.9 %first_messages.1 = (bf16[1024,256]{1,0:T(8,128)(2,1)S(1)}, bf16[128,256]{1,0:T(8,128)(2,1)S(1)}, bf16[128,256]{1,0:T(8,128)(2,1)S(1)}, bf16[128,256]{1,0:T(8,128)(2,1)S(1)}, bf16[128,256]{1,0:T(8,128)(2,1)S(1)}) custom-call(s32[4,128,128]{2,1,0:T(8,128)S(1)} %rim_rows.2.chosen, bf16[1024,256]{1,0:T(8,128)(2,1)S(1)} %copy-done.3, ...), custom_call_target="tpu_custom_call" | custom-call | bytes 1048576 | tf_op jit(solution)/shard_map/first_messages/pallas_call | solution.py:279
  2.1 3.0 %collective-permute-start = (bf16[128,256]{1,0:T(8,128)(2,1)S(1)}, bf16[128,256]{1,0:T(8,128)(2,1)S(1)}, u32[]{:S(2)}, u32[]{:S(2)}) collective-permute-start(bf16[128,256]{1,0:T(8,128)(2,1)S(1)} %get-tuple-element.26), channel_id=1, source_target_pairs={{0,4},{1,5},{2,6},{3,7},{4,0},{5,1},{6,2},{7,3},{8,12},{9,13},{10,... | collective-permute-start | bytes 196616 | tf_op jit(solution)/shard_map/ppermute | solution.py:317
  5.1 0.0 collective-permute-start.1
  5.1 0.5 %collective-permute-start.2 = (bf16[128,256]{1,0:T(8,128)(2,1)S(1)}, bf16[128,256]{1,0:T(8,128)(2,1)S(1)}, u32[]{:S(2)}, u32[]{:S(2)}) collective-permute-start(bf16[128,256]{1,0:T(8,128)(2,1)S(1)} %get-tuple-element.28), channel_id=1, source_target_pairs={{0,1},{1,0},{2,3},{3,2},{4,5},{5,4},{6,7},{7,6},{8,9},{9,8},{10,11... | collective-permute-start | bytes 196616 | tf_op jit(solution)/shard_map/ppermute | solution.py:317
  5.6 1.1 %collective-permute-start.3 = (bf16[128,256]{1,0:T(8,128)(2,1)S(1)}, bf16[128,256]{1,0:T(8,128)(2,1)S(1)}, u32[]{:S(2)}, u32[]{:S(2)}) collective-permute-start(bf16[128,256]{1,0:T(8,128)(2,1)S(1)} %get-tuple-element.29), channel_id=1, source_target_pairs={{0,3},{1,2},{2,1},{3,0},{4,7},{5,6},{6,5},{7,4},{8,11},{9,10},{10,... | collective-permute-start | bytes 196616 | tf_op jit(solution)/shard_map/ppermute | solution.py:317
  6.7 0.0 copy-done.17
  6.7 0.1 copy.20.source
  6.8 0.0 copy-done.18
  6.8 0.1 copy.21.live
  6.9 0.0 copy-done.2
  6.9 1.2 %local_edges.1.aggregate = f32[1024,256]{1,0:T(8,128)S(1)} custom-call(bf16[1024,256]{1,0:T(8,128)(2,1)S(1)} %get-tuple-element.25.messages.refs_3_, bf16[1,1,8,3,128,128]{5,4,3,2,1,0:T(8,128)(2,1)S(1)} %copy-done.2, s32[1,1,8,3]{3,2,1,0:T(8,128)S(1)} %copy.20.source, s32[1,1,8,3]{3,2,1,0:T(8,128)S(1)} %copy.21.live), custom_call_target="tpu_custom_call" | custom-call | bytes 1048576 | tf_op jit(solution)/shard_map/local_edges/pallas_call | solution.py:279
  8.1 0.1 collective-permute-done.rec0
  8.2 0.0 collective-permute-done.1.rec1
  8.2 0.0 collective-permute-done.2.rec2
  8.2 1.6 %collective-permute-done.3.rec3 = bf16[128,256]{1,0:T(8,128)(2,1)S(1)} collective-permute-done((bf16[128,256]{1,0:T(8,128)(2,1)S(1)}, bf16[128,256]{1,0:T(8,128)(2,1)S(1)}, u32[]{:S(2)}, u32[]{:S(2)}) %collective-permute-start.3) | collective-permute-done | bytes 65568 | tf_op jit(solution)/shard_map/ppermute | solution.py:317
  9.8 0.0 copy-done.6
  9.8 0.0 copy-done.7
  9.8 0.0 copy-done.15
  9.8 0.0 copy-start.12
  9.8 0.0 copy-start.13
  9.8 1.8 %second_messages.1 = (f32[1024,256]{1,0:T(8,128)S(1)}, bf16[1024,256]{1,0:T(8,128)(2,1)S(1)}, bf16[128,256]{1,0:T(8,128)(2,1)S(1)}, bf16[128,256]{1,0:T(8,128)(2...) custom-call(bf16[1024,256]{1,0:T(8,128)(2,1)S(1)} %copy-done.3, ...), custom_call_target="tpu_custom_call" | custom-call | bytes 1048576 | tf_op jit(solution)/shard_map/second_messages/pallas_call | solution.py:279
  11.6 0.0 copy-start.11
  11.7 2.1 %collective-permute-start.4 = (bf16[128,256]{1,0:T(8,128)(2,1)S(1)}, bf16[128,256]{1,0:T(8,128)(2,1)S(1)}, u32[]{:S(2)}, u32[]{:S(2)}) collective-permute-start(bf16[128,256]{1,0:T(8,128)(2,1)S(1)} %get-tuple-element.32), channel_id=1, source_target_pairs={{0,4},{1,5},{2,6},{3,7},{4,0},{5,1},{6,2},{7,3},{8,12},{9,13},{10,... | collective-permute-start | bytes 196616 | tf_op jit(solution)/shard_map/ppermute | solution.py:317
  13.8 0.2 collective-permute-start.5
  14.0 0.3 collective-permute-start.6
  14.3 1.3 %collective-permute-start.7 = (bf16[128,256]{1,0:T(8,128)(2,1)S(1)}, bf16[128,256]{1,0:T(8,128)(2,1)S(1)}, u32[]{:S(2)}, u32[]{:S(2)}) collective-permute-start(bf16[128,256]{1,0:T(8,128)(2,1)S(1)} %get-tuple-element.35), channel_id=1, source_target_pairs={{0,3},{1,2},{2,1},{3,0},{4,7},{5,6},{6,5},{7,4},{8,11},{9,10},{10,... | collective-permute-start | bytes 196616 | tf_op jit(solution)/shard_map/ppermute | solution.py:317
  15.6 0.0 copy-done.12
  15.6 0.0 copy-done.13
  15.6 0.0 copy-done.11
  15.6 0.5 slots.1.refs_2_
  16.1 1.2 %local_edges_again.1.aggregate = f32[1024,256]{1,0:T(8,128)S(1)} custom-call(bf16[1024,256]{1,0:T(8,128)(2,1)S(1)} %get-tuple-element.31.messages, bf16[1,1,8,3,128,128]{5,4,3,2,1,0:T(8,128)(2,1)S(1)} %copy-done.2, s32[1,1,8,3]{3,2,1,0:T(8,128)S(1)} %copy.20.source, s32[1,1,8,3]{3,2,1,0:T(8,128)S(1)} %copy.21.live), custom_call_target="tpu_custom_call" | custom-call | bytes 1048576 | tf_op jit(solution)/shard_map/local_edges_again/pallas_call | solution.py:279
  17.3 0.0 collective-permute-done.4.rec0
  17.3 0.0 collective-permute-done.5.rec1
  17.3 0.0 collective-permute-done.6.rec2
  17.4 1.1 %collective-permute-done.7.rec3 = bf16[128,256]{1,0:T(8,128)(2,1)S(1)} collective-permute-done((bf16[128,256]{1,0:T(8,128)(2,1)S(1)}, bf16[128,256]{1,0:T(8,128)(2,1)S(1)}, u32[]{:S(2)}, u32[]{:S(2)}) %collective-permute-start.7) | collective-permute-done | bytes 65568 | tf_op jit(solution)/shard_map/ppermute | solution.py:317
  18.4 0.0 copy-done.9
  18.4 5.2 %ball_attention.1 = (f32[1024,256]{1,0:T(8,128)S(1)}, bf16[1024,256]{1,0:T(8,128)(2,1)S(1)}) custom-call(f32[1024,256]{1,0:T(8,128)S(1)} %get-tuple-element.30.state, f32[1024,256]{1,0:T(8,128)S(1)} %local_edges_again.1.aggregate, bf16[128,256]{1,0:T(8,128)(2,1)S(1)} %collective-permute-done.4.rec0, bf16[128,256]{1,0:T(8,128)(2,1)S(1)} %collective-permute-done.5.rec1, ...), custom_call_target="tpu_custom_call" | custom-call | bytes 1048576 | tf_op jit(solution)/shard_map/ball_attention/pallas_call | solution.py:279
  23.7 0.0 copy-done
  23.7 0.0 copy-done.1
  23.7 0.0 copy-done.4
  23.7 1.9 %heavy_rows.1.refs_6_ = bf16[512,256]{1,0:T(8,128)(2,1)S(1)} custom-call(f32[1024,256]{1,0:T(8,128)S(1)} %get-tuple-element.36.refs_0_.state, bf16[1024,256]{1,0:T(8,128)(2,1)S(1)} %get-tuple-element.37.refs_1_.mixed, s32[2,1024]{1,0:T(2,128)S(1)} %slots.1.refs_2_, bf16[256,256]{1,0:T(8,128)(2,1)S(1)} %copy-done.4, bf16[256,1024]{1,0:T(8,128)(2,1)S(1)} %copy-done, ...), custom_call_target="tpu_custom_call" | custom-call | bytes 1048576 | tf_op jit(solution)/shard_map/heavy_rows/pallas_call | solution.py:279
  25.6 0.0 copy-start.8
  25.6 0.4 collective-permute-start.8
  26.0 2.0 %light_rows.1 = (bf16[176,256]{1,0:T(8,128)(2,1)S(1)}, bf16[176,256]{1,0:T(8,128)(2,1)S(1)}, bf16[176,256]{1,0:T(8,128)(2,1)S(1)}) custom-call(f32[1024,256]{1,0:T(8,128)S(1)} %get-tuple-element.36.refs_0_.state, bf16[1024,256]{1,0:T(8,128)(2,1)S(1)} %get-tuple-element.37.refs_1_.mixed, s32[2,1024]{1,0:T(2,128)S(1)} %slots.1.refs_2_, ...), custom_call_target="tpu_custom_call" | custom-call | bytes 1048576 | tf_op jit(solution)/shard_map/light_rows/pallas_call | solution.py:279
  28.0 1.6 %collective-permute-start.9 = (bf16[176,256]{1,0:T(8,128)(2,1)S(1)}, bf16[176,256]{1,0:T(8,128)(2,1)S(1)}, u32[]{:S(2)}, u32[]{:S(2)}) collective-permute-start(bf16[176,256]{1,0:T(8,128)(2,1)S(1)} %get-tuple-element.39), channel_id=1, source_target_pairs={{0,2},{1,3},{2,0},{3,1},{4,6},{5,7},{6,4},{7,5},{8,10},{9,11},{10,... | collective-permute-start | bytes 270344 | tf_op jit(solution)/shard_map/ppermute | solution.py:328
  29.6 1.3 %collective-permute-start.10 = (bf16[176,256]{1,0:T(8,128)(2,1)S(1)}, bf16[176,256]{1,0:T(8,128)(2,1)S(1)}, u32[]{:S(2)}, u32[]{:S(2)}) collective-permute-start(bf16[176,256]{1,0:T(8,128)(2,1)S(1)} %get-tuple-element.40), channel_id=1, source_target_pairs={{0,3},{1,0},{2,1},{3,2},{4,7},{5,4},{6,5},{7,6},{8,11},{9,8},{10,9... | collective-permute-start | bytes 270344 | tf_op jit(solution)/shard_map/ppermute | solution.py:328
  30.9 2.3 %collective-permute-done.9.refs_4_ = bf16[176,256]{1,0:T(8,128)(2,1)S(1)} collective-permute-done((bf16[176,256]{1,0:T(8,128)(2,1)S(1)}, bf16[176,256]{1,0:T(8,128)(2,1)S(1)}, u32[]{:S(2)}, u32[]{:S(2)}) %collective-permute-start.9) | collective-permute-done | bytes 90144 | tf_op jit(solution)/shard_map/ppermute | solution.py:328
  33.2 0.4 collective-permute-done.10.refs_5_
  33.6 0.0 collective-permute-done.8.refs_2_
  33.6 0.0 copy-done.8
  33.6 0.0 copy-done.14
  33.6 5.3 %owner_layer.1 = (bf16[512,256]{1,0:T(8,128)(2,1)S(1)}, bf16[176,256]{1,0:T(8,128)(2,1)S(1)}, bf16[176,256]{1,0:T(8,128)(2,1)S(1)}, bf16[176,256]{1,0:T(8,128)(2,1)S(1)}) custom-call(s32[1,1,4,512]{3,2,1,0:T(4,128)S(1)} %copy-done.14, bf16[256,768]{1,0:T(8,128)(2,1)S(1)} %copy-done.8, bf16[512,256]{1,0:T(8,128)(2,1)S(1)} %collective-permute-done.8.refs_2_, ...), custom_call_target="tpu_custom_call" | custom-call | bytes 1048576 | tf_op jit(solution)/shard_map/owner_layer/pallas_call | solution.py:279
  38.9 2.0 %collective-permute-start.11 = (bf16[512,256]{1,0:T(8,128)(2,1)S(1)}, bf16[512,256]{1,0:T(8,128)(2,1)S(1)}, u32[]{:S(2)}, u32[]{:S(2)}) collective-permute-start(bf16[512,256]{1,0:T(8,128)(2,1)S(1)} %get-tuple-element.41), channel_id=1, source_target_pairs={{0,3},{1,0},{2,1},{3,2},{4,7},{5,4},{6,5},{7,6},{8,11},{9,8},{10,9... | collective-permute-start | bytes 786440 | tf_op jit(solution)/shard_map/ppermute | solution.py:328
  40.9 0.5 collective-permute-start.12
  41.4 0.0 collective-permute-start.13
  41.4 3.1 %kept_rows.1.refs_0_ = f32[1024,256]{1,0:T(8,128)S(1)} custom-call(f32[1024,256]{1,0:T(8,128)S(1)} %get-tuple-element.36.refs_0_.state, bf16[1024,256]{1,0:T(8,128)(2,1)S(1)} %get-tuple-element.37.refs_1_.mixed, s32[1,1,1024]{2,1,0:T(1,128)S(1)} %copy-done.11, bf16[256,256]{1,0:T(8,128)(2,1)S(1)} %copy-done.4, bf16[256,1024]{1,0:T(8,128)(2,1)S(1)} %copy-done, ...), custom_call_target="tpu_custom_call" | custom-call | bytes 1048576 | tf_op jit(solution)/shard_map/kept_rows/pallas_call | solution.py:279
  44.5 3.6 %collective-permute-done.12.refs_6_ = bf16[176,256]{1,0:T(8,128)(2,1)S(1)} collective-permute-done((bf16[176,256]{1,0:T(8,128)(2,1)S(1)}, bf16[176,256]{1,0:T(8,128)(2,1)S(1)}, u32[]{:S(2)}, u32[]{:S(2)}) %collective-permute-start.12) | collective-permute-done | bytes 90144 | tf_op jit(solution)/shard_map/ppermute | solution.py:328
  48.1 0.0 collective-permute-done.13.refs_7_
  48.1 0.0 collective-permute-done.11.refs_4_
  48.1 2.1 %relayed_changes.1 = f32[1024,256]{1,0:T(8,128)} custom-call(f32[1024,256]{1,0:T(8,128)S(1)} %kept_rows.1.refs_0_, s32[1,1,1024]{2,1,0:T(1,128)S(1)} %copy-done.12, s32[1,1,1024]{2,1,0:T(1,128)S(1)} %copy-done.13, bf16[256,256]{1,0:T(8,128)(2,1)S(1)} %copy-done.10, bf16[512,256]{1,0:T(8,128)(2,1)S(1)} %collective-permute-done.11.refs_4_, ...), custom_call_target="tpu_custom_call" | custom-call | bytes 1048576 | tf_op jit(solution)/shard_map/relayed_changes/pallas_call | solution.py:279
  (16 shorter events, 0.0 us)
Async XLA Ops:
  0.0 1.0 %copy-start.5 = (bf16[2,256,256]{2,1,0:T(8,128)(2,1)S(1)}, bf16[2,256,256]{2,1,0:T(8,128)(2,1)}, u32[]{:S(2)}) copy-start(bf16[2,256,256]{2,1,0:T(8,128)(2,1)} %w_msg.3) | copy-start | bytes 786436
  0.0 1.1 %copy-start.3 = (bf16[1024,256]{1,0:T(8,128)(2,1)S(1)}, bf16[1024,256]{1,0:T(8,128)(2,1)}, u32[]{:S(2)}) copy-start(bf16[1024,256]{1,0:T(8,128)(2,1)} %state.1) | copy-start | bytes 1572868
  0.0 0.8 %copy-start.16 = (s32[1,1,4,128]{3,2,1,0:T(4,128)S(1)}, s32[1,1,4,128]{3,2,1,0:T(4,128)}, u32[]{:S(2)}) copy-start(s32[1,1,4,128]{3,2,1,0:T(4,128)} %rim_rows.3) | copy-start | bytes 6148
  1.1 5.7 %copy-start.2 = (bf16[1,1,8,3,128,128]{5,4,3,2,1,0:T(8,128)(2,1)S(1)}, bf16[1,1,8,3,128,128]{5,4,3,2,1,0:T(8,128)(2,1)}, u32[]{:S(2)}) copy-start(bf16[1,1,8,3,128,128]{5,4,3,2,1,0:T(8,128)(2,1)} %tiles.6) | copy-start | bytes 2359300
  2.1 6.1 %collective-permute-start = (bf16[128,256]{1,0:T(8,128)(2,1)S(1)}, bf16[128,256]{1,0:T(8,128)(2,1)S(1)}, u32[]{:S(2)}, u32[]{:S(2)}) collective-permute-start(bf16[128,256]{1,0:T(8,128)(2,1)S(1)} %get-tuple-element.26), channel_id=1, source_target_pairs={{0,4},{1,5},{2,6},{3,7},{4,0},{5,1},{6,2},{7,3},{8,12},{9,13},{10,... | collective-permute-start | bytes 196616 | tf_op jit(solution)/shard_map/ppermute | solution.py:317
  5.1 1.6 %copy-start.17 = (s32[1,1,8,3]{2,1,3,0:T(1,128)S(1)}, s32[1,1,8,3]{2,1,3,0:T(1,128)}, u32[]{:S(2)}) copy-start(s32[1,1,8,3]{2,1,3,0:T(1,128)} %param.23) | copy-start | bytes 292
  5.1 3.1 %collective-permute-start.1 = (bf16[128,256]{1,0:T(8,128)(2,1)S(1)}, bf16[128,256]{1,0:T(8,128)(2,1)S(1)}, u32[]{:S(2)}, u32[]{:S(2)}) collective-permute-start(bf16[128,256]{1,0:T(8,128)(2,1)S(1)} %get-tuple-element.27), channel_id=1, source_target_pairs={{0,1},{1,0},{2,3},{3,2},{4,8},{5,9},{6,10},{7,11},{8,4},{9,5},{10,... | collective-permute-start | bytes 196616 | tf_op jit(solution)/shard_map/ppermute | solution.py:317
  5.1 3.1 %collective-permute-start.2 = (bf16[128,256]{1,0:T(8,128)(2,1)S(1)}, bf16[128,256]{1,0:T(8,128)(2,1)S(1)}, u32[]{:S(2)}, u32[]{:S(2)}) collective-permute-start(bf16[128,256]{1,0:T(8,128)(2,1)S(1)} %get-tuple-element.28), channel_id=1, source_target_pairs={{0,1},{1,0},{2,3},{3,2},{4,5},{5,4},{6,7},{7,6},{8,9},{9,8},{10,11... | collective-permute-start | bytes 196616 | tf_op jit(solution)/shard_map/ppermute | solution.py:317
  5.6 1.2 %copy-start.18 = (s32[1,1,8,3]{2,1,3,0:T(1,128)S(1)}, s32[1,1,8,3]{2,1,3,0:T(1,128)}, u32[]{:S(2)}) copy-start(s32[1,1,8,3]{2,1,3,0:T(1,128)} %param.24) | copy-start | bytes 292
  5.6 4.2 %collective-permute-start.3 = (bf16[128,256]{1,0:T(8,128)(2,1)S(1)}, bf16[128,256]{1,0:T(8,128)(2,1)S(1)}, u32[]{:S(2)}, u32[]{:S(2)}) collective-permute-start(bf16[128,256]{1,0:T(8,128)(2,1)S(1)} %get-tuple-element.29), channel_id=1, source_target_pairs={{0,3},{1,2},{2,1},{3,0},{4,7},{5,6},{6,5},{7,4},{8,11},{9,10},{10,... | collective-permute-start | bytes 196616 | tf_op jit(solution)/shard_map/ppermute | solution.py:317
  6.9 2.9 %copy-start.6 = (bf16[2,256,256]{2,1,0:T(8,128)(2,1)S(1)}, bf16[2,256,256]{2,1,0:T(8,128)(2,1)}, u32[]{:S(2)}) copy-start(bf16[2,256,256]{2,1,0:T(8,128)(2,1)} %w_upd.3) | copy-start | bytes 786436
  6.9 2.9 %copy-start.7 = (bf16[1,1,4,128,128]{4,3,2,1,0:T(8,128)(2,1)S(1)}, bf16[1,1,4,128,128]{4,3,2,1,0:T(8,128)(2,1)}, u32[]{:S(2)}) copy-start(bf16[1,1,4,128,128]{4,3,2,1,0:T(8,128)(2,1)} %tiles.7) | copy-start | bytes 393220
  6.9 2.9 %copy-start.15 = (s32[1,1,4]{2,1,0:T(1,128)S(1)}, s32[1,1,4]{2,1,0:T(1,128)}, u32[]{:S(2)}) copy-start(s32[1,1,4]{2,1,0:T(1,128)} %block.3) | copy-start | bytes 52
  9.8 5.8 %copy-start.12 = (s32[1,1,1024]{2,1,0:T(1,128)S(1)}, s32[1,1,1024]{2,1,0:T(1,128)}, u32[]{:S(2)}) copy-start(s32[1,1,1024]{2,1,0:T(1,128)} %refs_1_.5) | copy-start | bytes 12292
  9.8 5.8 %copy-start.13 = (s32[1,1,1024]{2,1,0:T(1,128)S(1)}, s32[1,1,1024]{2,1,0:T(1,128)}, u32[]{:S(2)}) copy-start(s32[1,1,1024]{2,1,0:T(1,128)} %refs_2_.3) | copy-start | bytes 12292
  11.6 4.0 %copy-start.11 = (s32[1,1,1024]{2,1,0:T(1,128)S(1)}, s32[1,1,1024]{2,1,0:T(1,128)}, u32[]{:S(2)}) copy-start(s32[1,1,1024]{2,1,0:T(1,128)} %order.3) | copy-start | bytes 12292
  11.7 5.7 %collective-permute-start.4 = (bf16[128,256]{1,0:T(8,128)(2,1)S(1)}, bf16[128,256]{1,0:T(8,128)(2,1)S(1)}, u32[]{:S(2)}, u32[]{:S(2)}) collective-permute-start(bf16[128,256]{1,0:T(8,128)(2,1)S(1)} %get-tuple-element.32), channel_id=1, source_target_pairs={{0,4},{1,5},{2,6},{3,7},{4,0},{5,1},{6,2},{7,3},{8,12},{9,13},{10,... | collective-permute-start | bytes 196616 | tf_op jit(solution)/shard_map/ppermute | solution.py:317
  13.8 3.5 %collective-permute-start.5 = (bf16[128,256]{1,0:T(8,128)(2,1)S(1)}, bf16[128,256]{1,0:T(8,128)(2,1)S(1)}, u32[]{:S(2)}, u32[]{:S(2)}) collective-permute-start(bf16[128,256]{1,0:T(8,128)(2,1)S(1)} %get-tuple-element.33), channel_id=1, source_target_pairs={{0,1},{1,0},{2,3},{3,2},{4,8},{5,9},{6,10},{7,11},{8,4},{9,5},{10,... | collective-permute-start | bytes 196616 | tf_op jit(solution)/shard_map/ppermute | solution.py:317
  14.0 3.4 %collective-permute-start.6 = (bf16[128,256]{1,0:T(8,128)(2,1)S(1)}, bf16[128,256]{1,0:T(8,128)(2,1)S(1)}, u32[]{:S(2)}, u32[]{:S(2)}) collective-permute-start(bf16[128,256]{1,0:T(8,128)(2,1)S(1)} %get-tuple-element.34), channel_id=1, source_target_pairs={{0,1},{1,0},{2,3},{3,2},{4,5},{5,4},{6,7},{7,6},{8,9},{9,8},{10,11... | collective-permute-start | bytes 196616 | tf_op jit(solution)/shard_map/ppermute | solution.py:317
  14.3 4.1 %collective-permute-start.7 = (bf16[128,256]{1,0:T(8,128)(2,1)S(1)}, bf16[128,256]{1,0:T(8,128)(2,1)S(1)}, u32[]{:S(2)}, u32[]{:S(2)}) collective-permute-start(bf16[128,256]{1,0:T(8,128)(2,1)S(1)} %get-tuple-element.35), channel_id=1, source_target_pairs={{0,3},{1,2},{2,1},{3,0},{4,7},{5,6},{6,5},{7,4},{8,11},{9,10},{10,... | collective-permute-start | bytes 196616 | tf_op jit(solution)/shard_map/ppermute | solution.py:317
  16.1 2.3 %copy-start.9 = (bf16[256,768]{1,0:T(8,128)(2,1)S(1)}, bf16[256,768]{1,0:T(8,128)(2,1)}, u32[]{:S(2)}) copy-start(bf16[256,768]{1,0:T(8,128)(2,1)} %w_qkv.1) | copy-start | bytes 1179652
  18.4 5.2 %copy-start = (bf16[256,1024]{1,0:T(8,128)(2,1)S(1)}, bf16[256,1024]{1,0:T(8,128)(2,1)}, u32[]{:S(2)}) copy-start(bf16[256,1024]{1,0:T(8,128)(2,1)} %w_in.1) | copy-start | bytes 1572868
  18.4 5.3 %copy-start.1 = (bf16[1024,256]{1,0:T(8,128)(2,1)S(1)}, bf16[1024,256]{1,0:T(8,128)(2,1)}, u32[]{:S(2)}) copy-start(bf16[1024,256]{1,0:T(8,128)(2,1)} %w_mlp_out.1) | copy-start | bytes 1572868
  18.4 5.3 %copy-start.4 = (bf16[256,256]{1,0:T(8,128)(2,1)S(1)}, bf16[256,256]{1,0:T(8,128)(2,1)}, u32[]{:S(2)}) copy-start(bf16[256,256]{1,0:T(8,128)(2,1)} %w_out.1) | copy-start | bytes 393220
  25.6 8.0 %copy-start.8 = (bf16[256,768]{1,0:T(8,128)(2,1)S(1)}, bf16[256,768]{1,0:T(8,128)(2,1)}, u32[]{:S(2)}) copy-start(bf16[256,768]{1,0:T(8,128)(2,1)} %refs_1_.4) | copy-start | bytes 1179652
  25.6 8.0 %collective-permute-start.8 = (bf16[512,256]{1,0:T(8,128)(2,1)S(1)}, bf16[512,256]{1,0:T(8,128)(2,1)S(1)}, u32[]{:S(2)}, u32[]{:S(2)}) collective-permute-start(bf16[512,256]{1,0:T(8,128)(2,1)S(1)} %heavy_rows.1.refs_6_), channel_id=1, source_target_pairs={{0,1},{1,2},{2,3},{3,0},{4,5},{5,6},{6,7},{7,4},{8,9},{9,10},{10,1... | collective-permute-start | bytes 786440 | tf_op jit(solution)/shard_map/ppermute | solution.py:328
  26.0 7.6 %copy-start.14 = (s32[1,1,4,512]{3,2,1,0:T(4,128)S(1)}, s32[1,1,4,512]{3,2,1,0:T(4,128)}, u32[]{:S(2)}) copy-start(s32[1,1,4,512]{3,2,1,0:T(4,128)} %refs_0_.3) | copy-start | bytes 24580
  28.0 5.2 %collective-permute-start.9 = (bf16[176,256]{1,0:T(8,128)(2,1)S(1)}, bf16[176,256]{1,0:T(8,128)(2,1)S(1)}, u32[]{:S(2)}, u32[]{:S(2)}) collective-permute-start(bf16[176,256]{1,0:T(8,128)(2,1)S(1)} %get-tuple-element.39), channel_id=1, source_target_pairs={{0,2},{1,3},{2,0},{3,1},{4,6},{5,7},{6,4},{7,5},{8,10},{9,11},{10,... | collective-permute-start | bytes 270344 | tf_op jit(solution)/shard_map/ppermute | solution.py:328
  29.6 4.0 %collective-permute-start.10 = (bf16[176,256]{1,0:T(8,128)(2,1)S(1)}, bf16[176,256]{1,0:T(8,128)(2,1)S(1)}, u32[]{:S(2)}, u32[]{:S(2)}) collective-permute-start(bf16[176,256]{1,0:T(8,128)(2,1)S(1)} %get-tuple-element.40), channel_id=1, source_target_pairs={{0,3},{1,0},{2,1},{3,2},{4,7},{5,4},{6,5},{7,6},{8,11},{9,8},{10,9... | collective-permute-start | bytes 270344 | tf_op jit(solution)/shard_map/ppermute | solution.py:328
  38.9 9.2 %collective-permute-start.11 = (bf16[512,256]{1,0:T(8,128)(2,1)S(1)}, bf16[512,256]{1,0:T(8,128)(2,1)S(1)}, u32[]{:S(2)}, u32[]{:S(2)}) collective-permute-start(bf16[512,256]{1,0:T(8,128)(2,1)S(1)} %get-tuple-element.41), channel_id=1, source_target_pairs={{0,3},{1,0},{2,1},{3,2},{4,7},{5,4},{6,5},{7,6},{8,11},{9,8},{10,9... | collective-permute-start | bytes 786440 | tf_op jit(solution)/shard_map/ppermute | solution.py:328
  40.9 7.2 %collective-permute-start.12 = (bf16[176,256]{1,0:T(8,128)(2,1)S(1)}, bf16[176,256]{1,0:T(8,128)(2,1)S(1)}, u32[]{:S(2)}, u32[]{:S(2)}) collective-permute-start(bf16[176,256]{1,0:T(8,128)(2,1)S(1)} %get-tuple-element.43), channel_id=1, source_target_pairs={{0,2},{1,3},{2,0},{3,1},{4,6},{5,7},{6,4},{7,5},{8,10},{9,11},{10,... | collective-permute-start | bytes 270344 | tf_op jit(solution)/shard_map/ppermute | solution.py:328
  41.4 6.8 %copy-start.10 = (bf16[256,256]{1,0:T(8,128)(2,1)S(1)}, bf16[256,256]{1,0:T(8,128)(2,1)}, u32[]{:S(2)}) copy-start(bf16[256,256]{1,0:T(8,128)(2,1)} %refs_3_.5) | copy-start | bytes 393220
  41.4 6.7 %collective-permute-start.13 = (bf16[176,256]{1,0:T(8,128)(2,1)S(1)}, bf16[176,256]{1,0:T(8,128)(2,1)S(1)}, u32[]{:S(2)}, u32[]{:S(2)}) collective-permute-start(bf16[176,256]{1,0:T(8,128)(2,1)S(1)} %get-tuple-element.44), channel_id=1, source_target_pairs={{0,1},{1,2},{2,3},{3,0},{4,5},{5,6},{6,7},{7,4},{8,9},{9,10},{10,1... | collective-permute-start | bytes 270344 | tf_op jit(solution)/shard_map/ppermute | solution.py:328

commit v4 on v3

--- a/solution.py
+++ b/solution.py
@@ -13,6 +13,7 @@
 F32 = jnp.float32
 BF16 = jnp.bfloat16
 LANES = 128
+DIGIT = 32
 
 
 def up_to(count, unit):
@@ -79,7 +80,8 @@
         query, keys, values = own[:, :width], own[:, width : 2 * width], own[:, 2 * width :]
         weights = []
         for h in range(HEADS):
-            scores = dot_rows(query * masks[h], keys)
+            near = slice(h * head // LANES * LANES, (h * head // LANES + 1) * LANES)
+            scores = dot_rows(query[:, near] * masks[h][:, near], keys[:, near])
             top = jnp.max(scores, axis=-1, keepdims=True)
             raw = jnp.exp2((scores - top) * scale)
             weights.append((raw * (1.0 / jnp.sum(raw, axis=-1, keepdims=True))).astype(BF16))
@@ -103,16 +105,29 @@
 
 def make_rims(messages, chosen, out_refs):
     for at, out in enumerate(out_refs):
-        out[...] = dot(picks_by(chosen[at], messages.shape[0]), messages).astype(BF16)
-
-
-def first_kernel(chosen, features, w_msg, messages_out, *rims_out):
-    messages = dot(normed(features[...].astype(F32)).astype(BF16), w_msg[0]).astype(BF16)
+        out[: chosen.shape[1], :] = dot(picks_by(chosen[at], messages.shape[0]), messages).astype(BF16)
+
+
+def first_kernel(chosen, features, w_msg, inbox, messages_out, *rims_out):
+    points, width = features.shape
+    messages = [
+        dot(normed(features[at : at + BALL, :].astype(F32)).astype(BF16), w_msg[0]).astype(BF16)
+        for at in range(0, points, BALL)
+    ]
+    messages = jnp.concatenate(messages, axis=0)
     messages_out[...] = messages
     make_rims(messages, chosen, rims_out)
-
-
-def slots_kernel(order, peer, rank, after, slots_out, *, members, capacity, light):
+    table = inbox[0, 0]
+    pieces = [table[:, at : at + width] for at in range(0, table.shape[1], width)]
+    digits = [piece // DIGIT for piece in pieces] + [lax.rem(piece, DIGIT) for piece in pieces]
+    digits = jnp.concatenate(digits, axis=0).astype(F32).astype(BF16)
+    for out in rims_out[2:]:
+        out[chosen.shape[1] :, :] = digits
+
+
+def slots_kernel(
+    order, peer, rank, rec2, rec3, after, slots_out, inbox_out, *, members, capacity, light, rim
+):
     me = lax.axis_index("rot")
     slots = slot_of(peer[0], rank[0], me, members, capacity, light)
     points = slots.shape[1]
@@ -120,6 +135,14 @@
     moved = dot(digits.astype(F32).astype(BF16), places(order[0], points)).astype(jnp.int32)
     slots_out[0:1, :] = slots
     slots_out[1:2, :] = moved[0:1] * LANES + moved[1:2]
+    even = (lax.rem(me, 2) == 0).astype(F32)
+    table = rec2[rim:, :].astype(F32) * even + rec3[rim:, :].astype(F32) * (1.0 - even)
+    half = table.shape[0] // 2
+    table = (table[:half] * DIGIT + table[half:]).astype(jnp.int32)
+    width = table.shape[1]
+    for at in range(0, capacity, width):
+        first = at // width * members
+        inbox_out[:, at : at + width] = table[first : first + members]
 
 
 def local_kernel(messages, tiles, source, live, aggregate):
@@ -145,7 +168,7 @@
         count = jnp.where(side < 2, lax.axis_size("grp"), lax.axis_size("rot"))
         above = lax.rem(side, 2) == 1
         inside = jnp.where(above, index + 1 < count, index > 0)
-        part = dot(tiles[0, 0, pl.ds(side, 1)][0], rows[...]) * inside.astype(F32)
+        part = dot(tiles[0, 0, pl.ds(side, 1)][0], rows[: tiles.shape[-1], :]) * inside.astype(F32)
         at = pl.ds(pl.multiple_of(block[0, 0, side] * size, size), size)
         total[at, :] += part
 
@@ -164,9 +187,8 @@
 
 
 def slot_of(peer, rank, me, members, capacity, light):
-    away = lax.rem(peer - me + members, members)
-    base = jnp.where(away == 1, 0, capacity + light * jnp.where(away == 0, 0, away - 1))
-    return base + rank
+    away = lax.rem(peer - me - 1 + 2 * members, members)
+    return jnp.where(away == 0, 0, capacity + light * (away - 1)) + rank
 
 
 def ball_kernel(
@@ -215,34 +237,26 @@
         at += out.shape[0]
 
 
-def kept_kernel(state, mixed, order, w_out, w_in, w_mlp_out, after, state_out):
-    points = state.shape[0]
-    back = dot(places(order[0], points), mixed[...]).astype(BF16)
-    starts = range(0, points, BALL)
-    pieces = [state[at : at + BALL, :] + dot(back[at : at + BALL], w_out[...]) for at in starts]
-    for at, piece in zip(starts, feed(pieces, w_in, w_mlp_out)):
-        state_out[at : at + BALL, :] = piece
-
-
-def senders(members):
-    return [1, 0] + list(range(2, members))
-
-
-def owner_kernel(inbox, w_qkv, *refs, members, capacity, light, wide):
-    incoming, returned = refs[:members], refs[members : 2 * members]
-    rows_in, mixed = refs[2 * members :]
+def kept_kernel(state, mixed, order, w_out, after, state_out):
+    back = dot(places(order[0], state.shape[0]), mixed[...]).astype(BF16)
+    state_out[...] = state[...] + dot(back, w_out[...])
+
+
+def owner_kernel(after, inbox, w_qkv, *refs, members, capacity, light, wide):
+    incoming, returned = refs[:members], refs[members : 2 * members - 1]
+    mixed, rows_in = refs[2 * members - 1 :]
     me = lax.axis_index("rot")
     points = mixed.shape[0]
     indices = []
     at = 0
-    for away, rows in zip(senders(members), incoming):
-        height = capacity if away == 1 else light
-        span = capacity if away == 1 else wide
+    for away, rows in enumerate(incoming):
+        height = rows.shape[0]
+        span = capacity if away == 0 else wide
         sender = lax.rem(me - away + members, members)
         rows_in[at : at + height, :] = rows[...]
         if span > height:
             rows_in[at + height : at + span, :] = jnp.zeros((span - height, rows_in.shape[1]), BF16)
-        indices.append(inbox[0, 0, pl.ds(sender, 1), :][:, :span])
+        indices.append(inbox[pl.ds(sender, 1), :][:, :span])
         at += span
     index_row = jnp.concatenate(indices, axis=1)
     owned = dot(places(index_row, points), rows_in[...]).astype(BF16)
@@ -251,22 +265,34 @@
         mixed[ball * BALL : (ball + 1) * BALL, :] = value
 
     attention(owned, w_qkv[...], store)
-    for index, out in zip(indices, returned):
+    for index, out in zip(indices[1:], returned):
         out[...] = dot(picks(index, points), mixed[...])[: out.shape[0]].astype(BF16)
 
 
+def stayed_kernel(
+    state, mixed, inbox, peer, rank, w_in, w_mlp_out, w_out, after, out,
+    *, members, capacity, light,
+):
+    me = lax.axis_index("rot")
+    back = dot(picks(inbox[pl.ds(me, 1), :], mixed.shape[0]), mixed[...]).astype(BF16)
+    slots = slot_of(peer[0], rank[0], me, members, capacity, light)
+    update = dot(picks(slots, capacity), back).astype(BF16)
+    starts = range(0, state.shape[0], BALL)
+    pieces = feed([state[at : at + BALL, :] for at in starts], w_in, w_mlp_out)
+    for at, piece in zip(starts, pieces):
+        out[at : at + BALL, :] = piece + dot(update[at : at + BALL], w_out[...])
+
+
 def last_kernel(state, peer, rank, w_out, *refs, members, capacity, light, wide):
-    returned, out, rows_in = refs[:members], *refs[members:]
+    returned, out, rows_in = refs[: members - 1], *refs[members - 1 :]
     me = lax.axis_index("rot")
-    at = 0
-    for away, rows in zip(senders(members), returned):
-        height = capacity if away == 1 else light
-        span = capacity if away == 1 else wide
-        rows_in[at : at + height, :] = rows[...]
-        if span > height:
-            rows_in[at + height : at + span, :] = jnp.zeros((span - height, rows_in.shape[1]), BF16)
-        at += span
-    slots = slot_of(peer[0], rank[0], me, members, capacity, wide)
+    for at, rows in enumerate(returned):
+        rows_in[at * wide : at * wide + light, :] = rows[...]
+        if wide > light:
+            rows_in[at * wide + light : (at + 1) * wide, :] = jnp.zeros(
+                (wide - light, rows_in.shape[1]), BF16
+            )
+    slots = slot_of(peer[0], rank[0], me, members, capacity, wide) - capacity
     update = dot(picks(slots, rows_in.shape[0]), rows_in[...]).astype(BF16)
     out[...] = state[...] + dot(update, w_out[...])
 
@@ -319,13 +345,11 @@
 
 
 def relay(parts, members, back):
-    moved = list(parts)
-    for at, away in reversed(list(enumerate(senders(members)))):
-        if away == 0:
-            continue
-        step = members - away if back else away
+    moved = []
+    for at, rows in enumerate(parts):
+        step = members - 1 - at if back else at + 1
         turn = [(i, (i + step) % members) for i in range(members)]
-        moved[at] = lax.ppermute(parts[at], "rot", turn)
+        moved.append(lax.ppermute(rows, "rot", turn))
     return moved
 
 
@@ -339,7 +363,9 @@
     rim = border_rows.shape[-1]
     most = up_to(points - capacity, members - 1) // (members - 1)
     light, wide = up_to(most, 16), up_to(most, LANES)
+    digits = 2 * members * (capacity // width)
     rims_shape = [((rim, width), BF16)] * 4
+    first_shape = rims_shape[:2] + [((rim + digits, width), BF16)] * 2
     grid, grid16 = ((points, width), F32), ((points, width), BF16)
 
     (chosen,) = call(
@@ -350,21 +376,23 @@
     part_shapes = [((capacity, width), BF16)] + [((light, width), BF16)] * (members - 1)
 
     messages, *rims = call(
-        first_kernel, (chosen, features, w_msg), [grid16] + rims_shape, name="first_messages"
+        first_kernel, (chosen, features, w_msg, relay_inbox), [grid16] + first_shape,
+        name="first_messages",
     )
     received = exchange(rims)
     (aggregate,) = call(
         local_kernel, (messages, local_tiles, local_src, local_live), [grid], scalars=(2, 3),
         name="local_edges",
     )
-    (slots,) = call(
-        bound(slots_kernel, **sizes), (ball_order, relay_peer, relay_rank, messages),
-        [((2, points), jnp.int32)], name="slots",
-    )
     state, messages, *rims = call(
         middle_kernel,
         (features, aggregate, *received, border_tiles, border_block, w_msg, w_upd, chosen),
         [grid, grid16] + rims_shape, scalars=(7,), scratch=[grid], name="second_messages",
+    )
+    slots, inbox = call(
+        bound(slots_kernel, rim=rim, **sizes),
+        (ball_order, relay_peer, relay_rank, received[2], received[3], messages),
+        [((2, points), jnp.int32), ((members, capacity), jnp.int32)], name="slots",
     )
     received = exchange(rims)
     (aggregate,) = call(
@@ -380,25 +408,32 @@
         [grid, grid16], scalars=(7,), scratch=[grid], name="ball_attention",
     )
     weights = (w_ball_out, w_mlp_in, w_mlp_out)
+    parts = call(
+        bound(sent_kernel, start=capacity, after=0), (state, mixed, slots, *weights),
+        part_shapes[1:], name="light_rows",
+    )
     heavy = call(
-        bound(sent_kernel, start=0, after=0), (state, mixed, slots, *weights), part_shapes[:1],
-        name="heavy_rows",
-    )
-    lighter = call(
-        bound(sent_kernel, start=capacity, after=1), (state, mixed, slots, *weights, *heavy),
-        part_shapes[1:], name="light_rows",
-    )
-    parts = [*heavy, *lighter]
+        bound(sent_kernel, start=0, after=1), (state, mixed, slots, *weights, parts[0]),
+        part_shapes[:1], name="heavy_rows",
+    )
     (state,) = call(
-        kept_kernel, (state, mixed, ball_order, *weights, lighter[0]), [grid], name="kept_rows",
+        kept_kernel, (state, mixed, ball_order, w_ball_out, heavy[0]), [grid], name="kept_rows"
     )
     parts = relay(parts, members, False)
     rows_in = ((capacity + (members - 1) * wide, width), BF16)
-    parts = call(
-        bound(owner_kernel, wide=wide, **sizes), (relay_inbox, w_rot_qkv, *parts), part_shapes,
-        scratch=[rows_in, grid16], name="owner_layer",
+    *parts, mixed = call(
+        bound(owner_kernel, wide=wide, **sizes), (state, inbox, w_rot_qkv, *heavy, *parts),
+        part_shapes[1:] + [grid16], scratch=[rows_in], name="owner_layer",
+    )
+    (state,) = call(
+        bound(stayed_kernel, **sizes),
+        (
+            state, mixed, inbox, relay_peer, relay_rank, w_mlp_in, w_mlp_out, w_rot_out, parts[0],
+        ),
+        [grid], name="stayed_changes",
     )
     parts = relay(parts, members, True)
+    rows_in = (((members - 1) * wide, width), BF16)
     (out,) = call(
         bound(last_kernel, wide=wide, **sizes), (state, relay_peer, relay_rank, w_rot_out, *parts),
         [grid], scratch=[rows_in], name="relayed_changes",

time: 50.4 us -> 45.8 us (0.909)
  waiting for transfers between devices: 9.06 us -> 5.6 us
  starting transfers between devices: 14.4 us -> 12.1 us
  local copies, waits for them, and re-layouts: 1.23 us -> 1.81 us
    ppermute x6, waiting for transfers between devices: 6.31 us -> 2.46 us  [relay(): moved.append(lax.ppermute(rows, 'rot', turn))]
    ppermute x6, starting transfers between devices: 5.75 us -> 3.92 us  [relay(): moved.append(lax.ppermute(rows, 'rot', turn))]
    unnamed x40, local copies, waits for them, and re-layouts: 1.23 us -> 1.81 us
    pallas_call x12 -> x13, Pallas kernels: 25.4 us -> 25.5 us  [call(): pl.pallas_call(kernel, out_shape=[jax.ShapeDtypeStruct(shape, kind) for s...]
  transfers between devices with their start and end apart: 14 -> 14, of which waited for: 6 -> 6; matrix products, arithmetic and copies ran while one was open for 0% -> 0% of each run, Pallas kernels for 16% -> 19%
where the time goes in v4:
time: 45.8 us; the launch traced here: 45.3 us
  Pallas kernels  25.5 us (56%)
  starting transfers between devices  12.1 us (26%)
  waiting for transfers between devices  5.6 us (12%)
  local copies, waits for them, and re-layouts  1.81 us (4%)
    pallas_call x13, Pallas kernels, call(): pl.pallas_call(kernel, out_shape=[jax.ShapeDtypeStruct(shape, kind) for s...  25.5 us
    ppermute x8, starting transfers between devices, exchange(): moved[i] = lax.ppermute(rims[i], ('grp', 'rot'), plan[i])  8.23 us
    ppermute x6, starting transfers between devices, relay(): moved.append(lax.ppermute(rows, 'rot', turn))  3.92 us
    ppermute x8, waiting for transfers between devices, exchange(): moved[i] = lax.ppermute(rims[i], ('grp', 'rot'), plan[i])  3.14 us
    ppermute x6, waiting for transfers between devices, relay(): moved.append(lax.ppermute(rows, 'rot', turn))  2.46 us
    unnamed x40, local copies, waits for them, and re-layouts  1.81 us
  transfers between devices with their start and end apart: 14, of which 6 were waited for; matrix products, arithmetic and copies ran while one was open for 0% of the time, Pallas kernels for 19%

profile of v4, /device:TPU:0, one launch (start us, length us, event | category | flops | bytes accessed | tf_op | source)
XLA Modules:
  0.0 45.3 jit_solution(3375941004012293350)
XLA Ops:
  0.0 0.8 %copy-done.16 = s32[1,1,4,128]{3,2,1,0:T(4,128)S(1)} copy-done((s32[1,1,4,128]{3,2,1,0:T(4,128)S(1)}, s32[1,1,4,128]{3,2,1,0:T(4,128)}, u32[]{:S(2)}) %copy-start.16) | copy-done | bytes 2072
  0.8 0.1 rim_rows.2.chosen
  0.9 0.1 copy-done.5
  1.0 0.2 copy-done.3
  1.1 0.0 copy-done.14
  1.1 0.7 %first_messages.1 = (bf16[1024,256]{1,0:T(8,128)(2,1)S(1)}, bf16[128,256]{1,0:T(8,128)(2,1)S(1)}, bf16[128,256]{1,0:T(8,128)(2,1)S(1)}, bf16[144,256]{1,0:T(8,128)(2,1)S(1)}, bf16[144,256]{1,0:T(8,128)(2,1)S(1)}) custom-call(s32[4,128,128]{2,1,0:T(8,128)S(1)} %rim_rows.2.chosen, bf16[1024,256]{1,0:T(8,128)(2,1)S(1)} %copy-done.3, ...), custom_call_target="tpu_custom_call" | custom-call | bytes 1048576 | tf_op jit(solution)/shard_map/first_messages/pallas_call | solution.py:305
  1.9 0.5 %collective-permute-start.2 = (bf16[144,256]{1,0:T(8,128)(2,1)S(1)}, bf16[144,256]{1,0:T(8,128)(2,1)S(1)}, u32[]{:S(2)}, u32[]{:S(2)}) collective-permute-start(bf16[144,256]{1,0:T(8,128)(2,1)S(1)} %get-tuple-element.30), channel_id=1, source_target_pairs={{0,1},{1,0},{2,3},{3,2},{4,5},{5,4},{6,7},{7,6},{8,9},{9,8},{10,11... | collective-permute-start | bytes 221192 | tf_op jit(solution)/shard_map/ppermute | solution.py:343
  2.4 2.6 %collective-permute-start.3 = (bf16[144,256]{1,0:T(8,128)(2,1)S(1)}, bf16[144,256]{1,0:T(8,128)(2,1)S(1)}, u32[]{:S(2)}, u32[]{:S(2)}) collective-permute-start(bf16[144,256]{1,0:T(8,128)(2,1)S(1)} %get-tuple-element.31), channel_id=1, source_target_pairs={{0,3},{1,2},{2,1},{3,0},{4,7},{5,6},{6,5},{7,4},{8,11},{9,10},{10,... | collective-permute-start | bytes 221192 | tf_op jit(solution)/shard_map/ppermute | solution.py:343
  5.0 1.5 %collective-permute-start = (bf16[128,256]{1,0:T(8,128)(2,1)S(1)}, bf16[128,256]{1,0:T(8,128)(2,1)S(1)}, u32[]{:S(2)}, u32[]{:S(2)}) collective-permute-start(bf16[128,256]{1,0:T(8,128)(2,1)S(1)} %get-tuple-element.28), channel_id=1, source_target_pairs={{0,4},{1,5},{2,6},{3,7},{4,0},{5,1},{6,2},{7,3},{8,12},{9,13},{10,... | collective-permute-start | bytes 196616 | tf_op jit(solution)/shard_map/ppermute | solution.py:343
  6.5 0.0 collective-permute-start.1
  6.5 0.0 copy-done.17
  6.5 0.1 copy.20.source
  6.6 0.6 %copy-done.18 = s32[1,1,8,3]{2,1,3,0:T(1,128)S(1)} copy-done((s32[1,1,8,3]{2,1,3,0:T(1,128)S(1)}, s32[1,1,8,3]{2,1,3,0:T(1,128)}, u32[]{:S(2)}) %copy-start.18) | copy-done | bytes 120
  7.2 0.1 copy.21.live
  7.3 0.0 copy-done.2
  7.3 1.2 %local_edges.1.aggregate = f32[1024,256]{1,0:T(8,128)S(1)} custom-call(bf16[1024,256]{1,0:T(8,128)(2,1)S(1)} %get-tuple-element.27.messages, bf16[1,1,8,3,128,128]{5,4,3,2,1,0:T(8,128)(2,1)S(1)} %copy-done.2, s32[1,1,8,3]{3,2,1,0:T(8,128)S(1)} %copy.20.source, s32[1,1,8,3]{3,2,1,0:T(8,128)S(1)} %copy.21.live), custom_call_target="tpu_custom_call" | custom-call | bytes 1048576 | tf_op jit(solution)/shard_map/local_edges/pallas_call | solution.py:305
  8.5 0.8 %collective-permute-done.rec0 = bf16[128,256]{1,0:T(8,128)(2,1)S(1)} collective-permute-done((bf16[128,256]{1,0:T(8,128)(2,1)S(1)}, bf16[128,256]{1,0:T(8,128)(2,1)S(1)}, u32[]{:S(2)}, u32[]{:S(2)}) %collective-permute-start) | collective-permute-done | bytes 65568 | tf_op jit(solution)/shard_map/ppermute | solution.py:343
  9.3 0.0 collective-permute-done.1.rec1
  9.3 0.0 collective-permute-done.2.rec2.refs_3_
  9.3 0.0 collective-permute-done.3.rec3.refs_4_
  9.3 0.0 copy-done.6
  9.3 0.0 copy-done.7
  9.3 0.0 copy-done.15
  9.3 1.8 %second_messages.1 = (f32[1024,256]{1,0:T(8,128)S(1)}, bf16[1024,256]{1,0:T(8,128)(2,1)S(1)}, bf16[128,256]{1,0:T(8,128)(2,1)S(1)}, bf16[128,256]{1,0:T(8,128)(2...) custom-call(bf16[1024,256]{1,0:T(8,128)(2,1)S(1)} %copy-done.3, ...), custom_call_target="tpu_custom_call" | custom-call | bytes 1048576 | tf_op jit(solution)/shard_map/second_messages/pallas_call | solution.py:305
  11.2 3.0 %collective-permute-start.4 = (bf16[128,256]{1,0:T(8,128)(2,1)S(1)}, bf16[128,256]{1,0:T(8,128)(2,1)S(1)}, u32[]{:S(2)}, u32[]{:S(2)}) collective-permute-start(bf16[128,256]{1,0:T(8,128)(2,1)S(1)} %get-tuple-element.34), channel_id=1, source_target_pairs={{0,4},{1,5},{2,6},{3,7},{4,0},{5,1},{6,2},{7,3},{8,12},{9,13},{10,... | collective-permute-start | bytes 196616 | tf_op jit(solution)/shard_map/ppermute | solution.py:343
  14.1 0.0 collective-permute-start.5
  14.1 0.5 %collective-permute-start.6 = (bf16[128,256]{1,0:T(8,128)(2,1)S(1)}, bf16[128,256]{1,0:T(8,128)(2,1)S(1)}, u32[]{:S(2)}, u32[]{:S(2)}) collective-permute-start(bf16[128,256]{1,0:T(8,128)(2,1)S(1)} %get-tuple-element.36), channel_id=1, source_target_pairs={{0,1},{1,0},{2,3},{3,2},{4,5},{5,4},{6,7},{7,6},{8,9},{9,8},{10,11... | collective-permute-start | bytes 196616 | tf_op jit(solution)/shard_map/ppermute | solution.py:343
  14.7 0.1 collective-permute-start.7
  14.8 1.2 %local_edges_again.1.aggregate = f32[1024,256]{1,0:T(8,128)S(1)} custom-call(bf16[1024,256]{1,0:T(8,128)(2,1)S(1)} %get-tuple-element.33.messages.refs_5_, bf16[1,1,8,3,128,128]{5,4,3,2,1,0:T(8,128)(2,1)S(1)} %copy-done.2, s32[1,1,8,3]{3,2,1,0:T(8,128)S(1)} %copy.20.source, s32[1,1,8,3]{3,2,1,0:T(8,128)S(1)} %copy.21.live), custom_call_target="tpu_custom_call" | custom-call | bytes 1048576 | tf_op jit(solution)/shard_map/local_edges_again/pallas_call | solution.py:305
  16.0 0.0 copy-done.11
  16.0 0.0 copy-done.12
  16.0 0.0 copy-done.13
  16.0 0.0 copy-start.9
  16.0 0.5 %slots.1 = (s32[2,1024]{1,0:T(2,128)S(1)}, s32[4,512]{1,0:T(4,128)S(1)}) custom-call(s32[1,1,1024]{2,1,0:T(1,128)S(1)} %copy-done.11, s32[1,1,1024]{2,1,0:T(1,128)S(1)} %copy-done.12, s32[1,1,1024]{2,1,0:T(1,128)S(1)} %copy-done.13, bf16[144,256]{1,0:T(8,128)(2,1)S(1)} %collective-permute-done.2.rec2.refs_3_, ...), custom_call_target="tpu_custom_call" | custom-call | bytes 1048576 | tf_op jit(solution)/shard_map/slots/pallas_call | solution.py:305
  16.5 0.0 collective-permute-done.4.rec0
  16.5 0.0 collective-permute-done.5.rec1
  16.5 0.0 collective-permute-done.6.rec2
  16.5 2.3 %collective-permute-done.7.rec3 = bf16[128,256]{1,0:T(8,128)(2,1)S(1)} collective-permute-done((bf16[128,256]{1,0:T(8,128)(2,1)S(1)}, bf16[128,256]{1,0:T(8,128)(2,1)S(1)}, u32[]{:S(2)}, u32[]{:S(2)}) %collective-permute-start.7) | collective-permute-done | bytes 65568 | tf_op jit(solution)/shard_map/ppermute | solution.py:343
  18.9 0.0 copy-done.9
  18.9 5.2 %ball_attention.1 = (f32[1024,256]{1,0:T(8,128)S(1)}, bf16[1024,256]{1,0:T(8,128)(2,1)S(1)}) custom-call(f32[1024,256]{1,0:T(8,128)S(1)} %get-tuple-element.32.state, f32[1024,256]{1,0:T(8,128)S(1)} %local_edges_again.1.aggregate, bf16[128,256]{1,0:T(8,128)(2,1)S(1)} %collective-permute-done.4.rec0, bf16[128,256]{1,0:T(8,128)(2,1)S(1)} %collective-permute-done.5.rec1, ...), custom_call_target="tpu_custom_call" | custom-call | bytes 1048576 | tf_op jit(solution)/shard_map/ball_attention/pallas_call | solution.py:305
  24.1 0.0 copy-done
  24.1 0.0 copy-done.1
  24.1 0.0 copy-done.4
  24.1 2.0 %light_rows.1 = (bf16[176,256]{1,0:T(8,128)(2,1)S(1)}, bf16[176,256]{1,0:T(8,128)(2,1)S(1)}, bf16[176,256]{1,0:T(8,128)(2,1)S(1)}) custom-call(f32[1024,256]{1,0:T(8,128)S(1)} %get-tuple-element.38.refs_0_.state, bf16[1024,256]{1,0:T(8,128)(2,1)S(1)} %get-tuple-element.39.refs_1_.mixed, s32[2,1024]{1,0:T(2,128)S(1)} %get-tuple-element.40.refs_2_, ...), custom_call_target="tpu_custom_call" | custom-call | bytes 1048576 | tf_op jit(solution)/shard_map/light_rows/pallas_call | solution.py:305
  26.1 0.5 %collective-permute-start.9 = (bf16[176,256]{1,0:T(8,128)(2,1)S(1)}, bf16[176,256]{1,0:T(8,128)(2,1)S(1)}, u32[]{:S(2)}, u32[]{:S(2)}) collective-permute-start(bf16[176,256]{1,0:T(8,128)(2,1)S(1)} %get-tuple-element.43), channel_id=1, source_target_pairs={{0,2},{1,3},{2,0},{3,1},{4,6},{5,7},{6,4},{7,5},{8,10},{9,11},{10,... | collective-permute-start | bytes 270344 | tf_op jit(solution)/shard_map/ppermute | solution.py:352
  26.6 1.0 %collective-permute-start.10 = (bf16[176,256]{1,0:T(8,128)(2,1)S(1)}, bf16[176,256]{1,0:T(8,128)(2,1)S(1)}, u32[]{:S(2)}, u32[]{:S(2)}) collective-permute-start(bf16[176,256]{1,0:T(8,128)(2,1)S(1)} %get-tuple-element.44), channel_id=1, source_target_pairs={{0,3},{1,0},{2,1},{3,2},{4,7},{5,4},{6,5},{7,6},{8,11},{9,8},{10,9... | collective-permute-start | bytes 270344 | tf_op jit(solution)/shard_map/ppermute | solution.py:352
  27.6 0.0 collective-permute-start.8
  27.6 1.9 %heavy_rows.1.after.refs_3_ = bf16[512,256]{1,0:T(8,128)(2,1)S(1)} custom-call(f32[1024,256]{1,0:T(8,128)S(1)} %get-tuple-element.38.refs_0_.state, bf16[1024,256]{1,0:T(8,128)(2,1)S(1)} %get-tuple-element.39.refs_1_.mixed, s32[2,1024]{1,0:T(2,128)S(1)} %get-tuple-element.40.refs_2_, bf16[256,256]{1,0:T(8,128)(2,1)S(1)} %copy-done.4, ...), custom_call_target="tpu_custom_call" | custom-call | bytes 1048576 | tf_op jit(solution)/shard_map/heavy_rows/pallas_call | solution.py:305
  29.5 0.0 copy-start.10
  29.5 1.0 %kept_rows.1.refs_0_ = f32[1024,256]{1,0:T(8,128)S(1)} custom-call(f32[1024,256]{1,0:T(8,128)S(1)} %get-tuple-element.38.refs_0_.state, bf16[1024,256]{1,0:T(8,128)(2,1)S(1)} %get-tuple-element.39.refs_1_.mixed, s32[1,1,1024]{2,1,0:T(1,128)S(1)} %copy-done.11, bf16[256,256]{1,0:T(8,128)(2,1)S(1)} %copy-done.4, bf16[512,256]{1,0:T(8,128)(2,1)S(1)} %heavy_rows.1.after.refs_3_), custom_call_target="tpu_custom_call" | custom-call | bytes 1048576 | tf_op jit(solution)/shard_map/kept_rows/pallas_call | solution.py:305
  30.5 0.5 %collective-permute-done.9.refs_5_ = bf16[176,256]{1,0:T(8,128)(2,1)S(1)} collective-permute-done((bf16[176,256]{1,0:T(8,128)(2,1)S(1)}, bf16[176,256]{1,0:T(8,128)(2,1)S(1)}, u32[]{:S(2)}, u32[]{:S(2)}) %collective-permute-start.9) | collective-permute-done | bytes 90144 | tf_op jit(solution)/shard_map/ppermute | solution.py:352
  31.0 0.0 collective-permute-done.10.refs_6_
  31.0 1.5 %collective-permute-done.8.refs_4_ = bf16[176,256]{1,0:T(8,128)(2,1)S(1)} collective-permute-done((bf16[176,256]{1,0:T(8,128)(2,1)S(1)}, bf16[176,256]{1,0:T(8,128)(2,1)S(1)}, u32[]{:S(2)}, u32[]{:S(2)}) %collective-permute-start.8) | collective-permute-done | bytes 90144 | tf_op jit(solution)/shard_map/ppermute | solution.py:352
  32.5 0.0 copy-done.10
  32.5 5.1 %owner_layer.1 = (bf16[176,256]{1,0:T(8,128)(2,1)S(1)}, bf16[176,256]{1,0:T(8,128)(2,1)S(1)}, bf16[176,256]{1,0:T(8,128)(2,1)S(1)}, bf16[1024,256]{1,0:T(8,128)(2,1)S(1)}) custom-call(f32[1024,256]{1,0:T(8,128)S(1)} %kept_rows.1.refs_0_, s32[4,512]{1,0:T(4,128)S(1)} %get-tuple-element.42.refs_1_.refs_2_, bf16[256,768]{1,0:T(8,128)(2,1)S(1)} %copy-done.10, ...), custom_call_target="tpu_custom_call" | custom-call | bytes 1048576 | tf_op jit(solution)/shard_map/owner_layer/pallas_call | solution.py:305
  37.6 0.6 %collective-permute-start.12 = (bf16[176,256]{1,0:T(8,128)(2,1)S(1)}, bf16[176,256]{1,0:T(8,128)(2,1)S(1)}, u32[]{:S(2)}, u32[]{:S(2)}) collective-permute-start(bf16[176,256]{1,0:T(8,128)(2,1)S(1)} %get-tuple-element.47), channel_id=1, source_target_pairs={{0,2},{1,3},{2,0},{3,1},{4,6},{5,7},{6,4},{7,5},{8,10},{9,11},{10,... | collective-permute-start | bytes 270344 | tf_op jit(solution)/shard_map/ppermute | solution.py:352
  38.3 0.0 collective-permute-start.13
  38.3 1.7 %collective-permute-start.11 = (bf16[176,256]{1,0:T(8,128)(2,1)S(1)}, bf16[176,256]{1,0:T(8,128)(2,1)S(1)}, u32[]{:S(2)}, u32[]{:S(2)}) collective-permute-start(bf16[176,256]{1,0:T(8,128)(2,1)S(1)} %get-tuple-element.46.refs_8_), channel_id=1, source_target_pairs={{0,3},{1,0},{2,1},{3,2},{4,7},{5,4},{6,5},{7,6},{8,11},{9,8},{10,9... | collective-permute-start | bytes 270344 | tf_op jit(solution)/shard_map/ppermute | solution.py:352
  40.0 0.0 copy-done.8
  40.0 3.0 %stayed_changes.1.refs_0_ = f32[1024,256]{1,0:T(8,128)S(1)} custom-call(f32[1024,256]{1,0:T(8,128)S(1)} %kept_rows.1.refs_0_, bf16[1024,256]{1,0:T(8,128)(2,1)S(1)} %get-tuple-element.45.refs_1_, s32[4,512]{1,0:T(4,128)S(1)} %get-tuple-element.42.refs_1_.refs_2_, s32[1,1,1024]{2,1,0:T(1,128)S(1)} %copy-done.12, s32[1,1,1024]{2,1,0:T(1,128)S(1)} %copy-done.13, ...), custom_call_target="tpu_custom_call" | custom-call | bytes 1048576 | tf_op jit(solution)/shard_map/stayed_changes/pallas_call | solution.py:305
  43.0 0.2 collective-permute-done.12.refs_5_
  43.2 0.3 collective-permute-done.13.refs_6_
  43.4 0.0 collective-permute-done.11.refs_4_
  43.4 1.9 %relayed_changes.1 = f32[1024,256]{1,0:T(8,128)} custom-call(f32[1024,256]{1,0:T(8,128)S(1)} %stayed_changes.1.refs_0_, s32[1,1,1024]{2,1,0:T(1,128)S(1)} %copy-done.12, s32[1,1,1024]{2,1,0:T(1,128)S(1)} %copy-done.13, bf16[256,256]{1,0:T(8,128)(2,1)S(1)} %copy-done.8, bf16[176,256]{1,0:T(8,128)(2,1)S(1)} %collective-permute-done.11.refs_4_, ...), custom_call_target="tpu_custom_call" | custom-call | bytes 1048576 | tf_op jit(solution)/shard_map/relayed_changes/pallas_call | solution.py:305
  (17 shorter events, 0.0 us)
Async XLA Ops:
  0.0 0.9 %copy-start.5 = (bf16[2,256,256]{2,1,0:T(8,128)(2,1)S(1)}, bf16[2,256,256]{2,1,0:T(8,128)(2,1)}, u32[]{:S(2)}) copy-start(bf16[2,256,256]{2,1,0:T(8,128)(2,1)} %w_msg.3) | copy-start | bytes 786436
  0.0 1.1 %copy-start.3 = (bf16[1024,256]{1,0:T(8,128)(2,1)S(1)}, bf16[1024,256]{1,0:T(8,128)(2,1)}, u32[]{:S(2)}) copy-start(bf16[1024,256]{1,0:T(8,128)(2,1)} %state.1) | copy-start | bytes 1572868
  0.0 1.1 %copy-start.14 = (s32[1,1,4,512]{3,2,1,0:T(4,128)S(1)}, s32[1,1,4,512]{3,2,1,0:T(4,128)}, u32[]{:S(2)}) copy-start(s32[1,1,4,512]{3,2,1,0:T(4,128)} %inbox.1) | copy-start | bytes 24580
  0.0 0.8 %copy-start.16 = (s32[1,1,4,128]{3,2,1,0:T(4,128)S(1)}, s32[1,1,4,128]{3,2,1,0:T(4,128)}, u32[]{:S(2)}) copy-start(s32[1,1,4,128]{3,2,1,0:T(4,128)} %rim_rows.3) | copy-start | bytes 6148
  1.1 6.1 %copy-start.2 = (bf16[1,1,8,3,128,128]{5,4,3,2,1,0:T(8,128)(2,1)S(1)}, bf16[1,1,8,3,128,128]{5,4,3,2,1,0:T(8,128)(2,1)}, u32[]{:S(2)}) copy-start(bf16[1,1,8,3,128,128]{5,4,3,2,1,0:T(8,128)(2,1)} %tiles.6) | copy-start | bytes 2359300
  1.9 7.4 %collective-permute-start.2 = (bf16[144,256]{1,0:T(8,128)(2,1)S(1)}, bf16[144,256]{1,0:T(8,128)(2,1)S(1)}, u32[]{:S(2)}, u32[]{:S(2)}) collective-permute-start(bf16[144,256]{1,0:T(8,128)(2,1)S(1)} %get-tuple-element.30), channel_id=1, source_target_pairs={{0,1},{1,0},{2,3},{3,2},{4,5},{5,4},{6,7},{7,6},{8,9},{9,8},{10,11... | collective-permute-start | bytes 221192 | tf_op jit(solution)/shard_map/ppermute | solution.py:343
  2.4 4.1 %copy-start.17 = (s32[1,1,8,3]{2,1,3,0:T(1,128)S(1)}, s32[1,1,8,3]{2,1,3,0:T(1,128)}, u32[]{:S(2)}) copy-start(s32[1,1,8,3]{2,1,3,0:T(1,128)} %param.23) | copy-start | bytes 292
  2.4 6.9 %collective-permute-start.3 = (bf16[144,256]{1,0:T(8,128)(2,1)S(1)}, bf16[144,256]{1,0:T(8,128)(2,1)S(1)}, u32[]{:S(2)}, u32[]{:S(2)}) collective-permute-start(bf16[144,256]{1,0:T(8,128)(2,1)S(1)} %get-tuple-element.31), channel_id=1, source_target_pairs={{0,3},{1,2},{2,1},{3,0},{4,7},{5,6},{6,5},{7,4},{8,11},{9,10},{10,... | collective-permute-start | bytes 221192 | tf_op jit(solution)/shard_map/ppermute | solution.py:343
  5.0 4.3 %collective-permute-start = (bf16[128,256]{1,0:T(8,128)(2,1)S(1)}, bf16[128,256]{1,0:T(8,128)(2,1)S(1)}, u32[]{:S(2)}, u32[]{:S(2)}) collective-permute-start(bf16[128,256]{1,0:T(8,128)(2,1)S(1)} %get-tuple-element.28), channel_id=1, source_target_pairs={{0,4},{1,5},{2,6},{3,7},{4,0},{5,1},{6,2},{7,3},{8,12},{9,13},{10,... | collective-permute-start | bytes 196616 | tf_op jit(solution)/shard_map/ppermute | solution.py:343
  6.5 0.7 %copy-start.18 = (s32[1,1,8,3]{2,1,3,0:T(1,128)S(1)}, s32[1,1,8,3]{2,1,3,0:T(1,128)}, u32[]{:S(2)}) copy-start(s32[1,1,8,3]{2,1,3,0:T(1,128)} %param.24) | copy-start | bytes 292
  6.5 2.8 %collective-permute-start.1 = (bf16[128,256]{1,0:T(8,128)(2,1)S(1)}, bf16[128,256]{1,0:T(8,128)(2,1)S(1)}, u32[]{:S(2)}, u32[]{:S(2)}) collective-permute-start(bf16[128,256]{1,0:T(8,128)(2,1)S(1)} %get-tuple-element.29), channel_id=1, source_target_pairs={{0,1},{1,0},{2,3},{3,2},{4,8},{5,9},{6,10},{7,11},{8,4},{9,5},{10,... | collective-permute-start | bytes 196616 | tf_op jit(solution)/shard_map/ppermute | solution.py:343
  7.3 2.0 %copy-start.6 = (bf16[2,256,256]{2,1,0:T(8,128)(2,1)S(1)}, bf16[2,256,256]{2,1,0:T(8,128)(2,1)}, u32[]{:S(2)}) copy-start(bf16[2,256,256]{2,1,0:T(8,128)(2,1)} %w_upd.3) | copy-start | bytes 786436
  7.3 2.0 %copy-start.7 = (bf16[1,1,4,128,128]{4,3,2,1,0:T(8,128)(2,1)S(1)}, bf16[1,1,4,128,128]{4,3,2,1,0:T(8,128)(2,1)}, u32[]{:S(2)}) copy-start(bf16[1,1,4,128,128]{4,3,2,1,0:T(8,128)(2,1)} %tiles.7) | copy-start | bytes 393220
  7.3 2.0 %copy-start.15 = (s32[1,1,4]{2,1,0:T(1,128)S(1)}, s32[1,1,4]{2,1,0:T(1,128)}, u32[]{:S(2)}) copy-start(s32[1,1,4]{2,1,0:T(1,128)} %block.3) | copy-start | bytes 52
  11.2 5.3 %collective-permute-start.4 = (bf16[128,256]{1,0:T(8,128)(2,1)S(1)}, bf16[128,256]{1,0:T(8,128)(2,1)S(1)}, u32[]{:S(2)}, u32[]{:S(2)}) collective-permute-start(bf16[128,256]{1,0:T(8,128)(2,1)S(1)} %get-tuple-element.34), channel_id=1, source_target_pairs={{0,4},{1,5},{2,6},{3,7},{4,0},{5,1},{6,2},{7,3},{8,12},{9,13},{10,... | collective-permute-start | bytes 196616 | tf_op jit(solution)/shard_map/ppermute | solution.py:343
  14.1 2.4 %collective-permute-start.5 = (bf16[128,256]{1,0:T(8,128)(2,1)S(1)}, bf16[128,256]{1,0:T(8,128)(2,1)S(1)}, u32[]{:S(2)}, u32[]{:S(2)}) collective-permute-start(bf16[128,256]{1,0:T(8,128)(2,1)S(1)} %get-tuple-element.35), channel_id=1, source_target_pairs={{0,1},{1,0},{2,3},{3,2},{4,8},{5,9},{6,10},{7,11},{8,4},{9,5},{10,... | collective-permute-start | bytes 196616 | tf_op jit(solution)/shard_map/ppermute | solution.py:343
  14.1 2.4 %collective-permute-start.6 = (bf16[128,256]{1,0:T(8,128)(2,1)S(1)}, bf16[128,256]{1,0:T(8,128)(2,1)S(1)}, u32[]{:S(2)}, u32[]{:S(2)}) collective-permute-start(bf16[128,256]{1,0:T(8,128)(2,1)S(1)} %get-tuple-element.36), channel_id=1, source_target_pairs={{0,1},{1,0},{2,3},{3,2},{4,5},{5,4},{6,7},{7,6},{8,9},{9,8},{10,11... | collective-permute-start | bytes 196616 | tf_op jit(solution)/shard_map/ppermute | solution.py:343
  14.7 4.2 %collective-permute-start.7 = (bf16[128,256]{1,0:T(8,128)(2,1)S(1)}, bf16[128,256]{1,0:T(8,128)(2,1)S(1)}, u32[]{:S(2)}, u32[]{:S(2)}) collective-permute-start(bf16[128,256]{1,0:T(8,128)(2,1)S(1)} %get-tuple-element.37), channel_id=1, source_target_pairs={{0,3},{1,2},{2,1},{3,0},{4,7},{5,6},{6,5},{7,4},{8,11},{9,10},{10,... | collective-permute-start | bytes 196616 | tf_op jit(solution)/shard_map/ppermute | solution.py:343
  14.7 1.2 %copy-start.11 = (s32[1,1,1024]{2,1,0:T(1,128)S(1)}, s32[1,1,1024]{2,1,0:T(1,128)}, u32[]{:S(2)}) copy-start(s32[1,1,1024]{2,1,0:T(1,128)} %order.3) | copy-start | bytes 12292
  14.7 1.2 %copy-start.12 = (s32[1,1,1024]{2,1,0:T(1,128)S(1)}, s32[1,1,1024]{2,1,0:T(1,128)}, u32[]{:S(2)}) copy-start(s32[1,1,1024]{2,1,0:T(1,128)} %refs_1_.3) | copy-start | bytes 12292
  14.8 1.2 %copy-start.13 = (s32[1,1,1024]{2,1,0:T(1,128)S(1)}, s32[1,1,1024]{2,1,0:T(1,128)}, u32[]{:S(2)}) copy-start(s32[1,1,1024]{2,1,0:T(1,128)} %refs_2_.5) | copy-start | bytes 12292
  16.0 2.9 %copy-start.9 = (bf16[256,768]{1,0:T(8,128)(2,1)S(1)}, bf16[256,768]{1,0:T(8,128)(2,1)}, u32[]{:S(2)}) copy-start(bf16[256,768]{1,0:T(8,128)(2,1)} %w_qkv.1) | copy-start | bytes 1179652
  18.9 5.2 %copy-start = (bf16[256,1024]{1,0:T(8,128)(2,1)S(1)}, bf16[256,1024]{1,0:T(8,128)(2,1)}, u32[]{:S(2)}) copy-start(bf16[256,1024]{1,0:T(8,128)(2,1)} %refs_5_.5) | copy-start | bytes 1572868
  18.9 5.2 %copy-start.1 = (bf16[1024,256]{1,0:T(8,128)(2,1)S(1)}, bf16[1024,256]{1,0:T(8,128)(2,1)}, u32[]{:S(2)}) copy-start(bf16[1024,256]{1,0:T(8,128)(2,1)} %refs_6_.1) | copy-start | bytes 1572868
  18.9 5.2 %copy-start.4 = (bf16[256,256]{1,0:T(8,128)(2,1)S(1)}, bf16[256,256]{1,0:T(8,128)(2,1)}, u32[]{:S(2)}) copy-start(bf16[256,256]{1,0:T(8,128)(2,1)} %w_out.1) | copy-start | bytes 393220
  26.1 4.9 %collective-permute-start.9 = (bf16[176,256]{1,0:T(8,128)(2,1)S(1)}, bf16[176,256]{1,0:T(8,128)(2,1)S(1)}, u32[]{:S(2)}, u32[]{:S(2)}) collective-permute-start(bf16[176,256]{1,0:T(8,128)(2,1)S(1)} %get-tuple-element.43), channel_id=1, source_target_pairs={{0,2},{1,3},{2,0},{3,1},{4,6},{5,7},{6,4},{7,5},{8,10},{9,11},{10,... | collective-permute-start | bytes 270344 | tf_op jit(solution)/shard_map/ppermute | solution.py:352
  26.6 4.4 %collective-permute-start.10 = (bf16[176,256]{1,0:T(8,128)(2,1)S(1)}, bf16[176,256]{1,0:T(8,128)(2,1)S(1)}, u32[]{:S(2)}, u32[]{:S(2)}) collective-permute-start(bf16[176,256]{1,0:T(8,128)(2,1)S(1)} %get-tuple-element.44), channel_id=1, source_target_pairs={{0,3},{1,0},{2,1},{3,2},{4,7},{5,4},{6,5},{7,6},{8,11},{9,8},{10,9... | collective-permute-start | bytes 270344 | tf_op jit(solution)/shard_map/ppermute | solution.py:352
  27.6 4.9 %collective-permute-start.8 = (bf16[176,256]{1,0:T(8,128)(2,1)S(1)}, bf16[176,256]{1,0:T(8,128)(2,1)S(1)}, u32[]{:S(2)}, u32[]{:S(2)}) collective-permute-start(bf16[176,256]{1,0:T(8,128)(2,1)S(1)} %get-tuple-element.41.refs_6_), channel_id=1, source_target_pairs={{0,1},{1,2},{2,3},{3,0},{4,5},{5,6},{6,7},{7,4},{8,9},{9,10},{10,1... | collective-permute-start | bytes 270344 | tf_op jit(solution)/shard_map/ppermute | solution.py:352
  29.5 3.0 %copy-start.10 = (bf16[256,768]{1,0:T(8,128)(2,1)S(1)}, bf16[256,768]{1,0:T(8,128)(2,1)}, u32[]{:S(2)}) copy-start(bf16[256,768]{1,0:T(8,128)(2,1)} %refs_2_.4) | copy-start | bytes 1179652
  32.5 7.5 %copy-start.8 = (bf16[256,256]{1,0:T(8,128)(2,1)S(1)}, bf16[256,256]{1,0:T(8,128)(2,1)}, u32[]{:S(2)}) copy-start(bf16[256,256]{1,0:T(8,128)(2,1)} %refs_3_.7) | copy-start | bytes 393220
  37.6 5.5 %collective-permute-start.12 = (bf16[176,256]{1,0:T(8,128)(2,1)S(1)}, bf16[176,256]{1,0:T(8,128)(2,1)S(1)}, u32[]{:S(2)}, u32[]{:S(2)}) collective-permute-start(bf16[176,256]{1,0:T(8,128)(2,1)S(1)} %get-tuple-element.47), channel_id=1, source_target_pairs={{0,2},{1,3},{2,0},{3,1},{4,6},{5,7},{6,4},{7,5},{8,10},{9,11},{10,... | collective-permute-start | bytes 270344 | tf_op jit(solution)/shard_map/ppermute | solution.py:352
  38.3 5.2 %collective-permute-start.13 = (bf16[176,256]{1,0:T(8,128)(2,1)S(1)}, bf16[176,256]{1,0:T(8,128)(2,1)S(1)}, u32[]{:S(2)}, u32[]{:S(2)}) collective-permute-start(bf16[176,256]{1,0:T(8,128)(2,1)S(1)} %get-tuple-element.48), channel_id=1, source_target_pairs={{0,1},{1,2},{2,3},{3,0},{4,5},{5,6},{6,7},{7,4},{8,9},{9,10},{10,1... | collective-permute-start | bytes 270344 | tf_op jit(solution)/shard_map/ppermute | solution.py:352
  38.3 5.2 %collective-permute-start.11 = (bf16[176,256]{1,0:T(8,128)(2,1)S(1)}, bf16[176,256]{1,0:T(8,128)(2,1)S(1)}, u32[]{:S(2)}, u32[]{:S(2)}) collective-permute-start(bf16[176,256]{1,0:T(8,128)(2,1)S(1)} %get-tuple-element.46.refs_8_), channel_id=1, source_target_pairs={{0,3},{1,0},{2,1},{3,2},{4,7},{5,4},{6,5},{7,6},{8,11},{9,8},{10,9... | collective-permute-start | bytes 270344 | tf_op jit(solution)/shard_map/ppermute | solution.py:352

commit v5 on v4

--- a/solution.py
+++ b/solution.py
@@ -121,7 +121,7 @@
     pieces = [table[:, at : at + width] for at in range(0, table.shape[1], width)]
     digits = [piece // DIGIT for piece in pieces] + [lax.rem(piece, DIGIT) for piece in pieces]
     digits = jnp.concatenate(digits, axis=0).astype(F32).astype(BF16)
-    for out in rims_out[2:]:
+    for out in rims_out:
         out[chosen.shape[1] :, :] = digits
 
 
@@ -186,8 +186,13 @@
     make_rims(messages, chosen, (rim0, rim1, rim2, rim3))
 
 
+def partner(me, step, members):
+    return me ^ step if members & (members - 1) == 0 else (me + step) % members
+
+
 def slot_of(peer, rank, me, members, capacity, light):
-    away = lax.rem(peer - me - 1 + 2 * members, members)
+    worker = lax.rem(peer - 1 + members, members)
+    away = me ^ worker if members & (members - 1) == 0 else lax.rem(worker - me + members, members)
     return jnp.where(away == 0, 0, capacity + light * (away - 1)) + rank
 
 
@@ -252,7 +257,7 @@
     for away, rows in enumerate(incoming):
         height = rows.shape[0]
         span = capacity if away == 0 else wide
-        sender = lax.rem(me - away + members, members)
+        sender = partner(me, away if members & (members - 1) == 0 else members - away, members)
         rows_in[at : at + height, :] = rows[...]
         if span > height:
             rows_in[at + height : at + span, :] = jnp.zeros((span - height, rows_in.shape[1]), BF16)
@@ -265,8 +270,10 @@
         mixed[ball * BALL : (ball + 1) * BALL, :] = value
 
     attention(owned, w_qkv[...], store)
-    for index, out in zip(indices[1:], returned):
-        out[...] = dot(picks(index, points), mixed[...])[: out.shape[0]].astype(BF16)
+    chosen = jnp.concatenate([picks(index, points)[:light] for index in indices[1:]], axis=0)
+    back = dot(chosen, mixed[...]).astype(BF16)
+    for at, out in enumerate(returned):
+        out[...] = back[at * light : (at + 1) * light]
 
 
 def stayed_kernel(
@@ -347,9 +354,8 @@
 def relay(parts, members, back):
     moved = []
     for at, rows in enumerate(parts):
-        step = members - 1 - at if back else at + 1
-        turn = [(i, (i + step) % members) for i in range(members)]
-        moved.append(lax.ppermute(rows, "rot", turn))
+        pairs = [(i, int(partner(i, at + 1, members))) for i in range(members)]
+        moved.append(lax.ppermute(rows, "rot", [pair[::-1] for pair in pairs] if back else pairs))
     return moved
 
 
@@ -365,7 +371,7 @@
     light, wide = up_to(most, 16), up_to(most, LANES)
     digits = 2 * members * (capacity // width)
     rims_shape = [((rim, width), BF16)] * 4
-    first_shape = rims_shape[:2] + [((rim + digits, width), BF16)] * 2
+    first_shape = [((rim + digits, width), BF16)] * 4
     grid, grid16 = ((points, width), F32), ((points, width), BF16)
 
     (chosen,) = call(

time: 45.8 us -> 45.1 us (0.985)
  starting transfers between devices: 12.1 us -> 13 us
  waiting for transfers between devices: 5.6 us -> 4.72 us
  local copies, waits for them, and re-layouts: 1.81 us -> 1.22 us
    ppermute x6, waiting for transfers between devices: 2.46 us -> 1.81 us  [relay(): lax.ppermute(rows, 'rot', [pair[::-1] for pair in pairs] if back else pairs)]
    unnamed x40, local copies, waits for them, and re-layouts: 1.81 us -> 1.22 us
    ppermute x6, starting transfers between devices: 3.92 us -> 4.41 us  [relay(): lax.ppermute(rows, 'rot', [pair[::-1] for pair in pairs] if back else pairs)]
  transfers between devices with their start and end apart: 14 -> 14, of which waited for: 6 -> 6; matrix products, arithmetic and copies ran while one was open for 0% -> 0% of each run, Pallas kernels for 19% -> 20%
where the time goes in v5:
time: 45.1 us; the launch traced here: 44.6 us
  Pallas kernels  25.5 us (57%)
  starting transfers between devices  13 us (29%)
  waiting for transfers between devices  4.72 us (10%)
  local copies, waits for them, and re-layouts  1.22 us (3%)
    pallas_call x13, Pallas kernels, call(): pl.pallas_call(kernel, out_shape=[jax.ShapeDtypeStruct(shape, kind) for s...  25.5 us
    ppermute x8, starting transfers between devices, exchange(): moved[i] = lax.ppermute(rims[i], ('grp', 'rot'), plan[i])  8.6 us
    ppermute x6, starting transfers between devices, relay(): lax.ppermute(rows, 'rot', [pair[::-1] for pair in pairs] if back else pairs)  4.41 us
    ppermute x8, waiting for transfers between devices, exchange(): moved[i] = lax.ppermute(rims[i], ('grp', 'rot'), plan[i])  2.91 us
    ppermute x6, waiting for transfers between devices, relay(): lax.ppermute(rows, 'rot', [pair[::-1] for pair in pairs] if back else pairs)  1.81 us
    unnamed x40, local copies, waits for them, and re-layouts  1.22 us
  transfers between devices with their start and end apart: 14, of which 6 were waited for; matrix products, arithmetic and copies ran while one was open for 0% of the time, Pallas kernels for 20%

profile of v5, /device:TPU:0, one launch (start us, length us, event | category | flops | bytes accessed | tf_op | source)
XLA Modules:
  0.0 44.6 jit_solution(3574457706058591287)
XLA Ops:
  0.0 0.8 %copy-done.16 = s32[1,1,4,128]{3,2,1,0:T(4,128)S(1)} copy-done((s32[1,1,4,128]{3,2,1,0:T(4,128)S(1)}, s32[1,1,4,128]{3,2,1,0:T(4,128)}, u32[]{:S(2)}) %copy-start.16) | copy-done | bytes 2072
  0.8 0.1 rim_rows.2.chosen
  0.9 0.1 copy-done.5
  1.0 0.2 copy-done.3
  1.1 0.0 copy-done.14
  1.1 0.7 %first_messages.1 = (bf16[1024,256]{1,0:T(8,128)(2,1)S(1)}, bf16[144,256]{1,0:T(8,128)(2,1)S(1)}, bf16[144,256]{1,0:T(8,128)(2,1)S(1)}, bf16[144,256]{1,0:T(8,128)(2,1)S(1)}, bf16[144,256]{1,0:T(8,128)(2,1)S(1)}) custom-call(s32[4,128,128]{2,1,0:T(8,128)S(1)} %rim_rows.2.chosen, bf16[1024,256]{1,0:T(8,128)(2,1)S(1)} %copy-done.3, ...), custom_call_target="tpu_custom_call" | custom-call | bytes 1048576 | tf_op jit(solution)/shard_map/first_messages/pallas_call | solution.py:312
  1.9 3.0 %collective-permute-start = (bf16[144,256]{1,0:T(8,128)(2,1)S(1)}, bf16[144,256]{1,0:T(8,128)(2,1)S(1)}, u32[]{:S(2)}, u32[]{:S(2)}) collective-permute-start(bf16[144,256]{1,0:T(8,128)(2,1)S(1)} %get-tuple-element.28), channel_id=1, source_target_pairs={{0,4},{1,5},{2,6},{3,7},{4,0},{5,1},{6,2},{7,3},{8,12},{9,13},{10,... | collective-permute-start | bytes 221192 | tf_op jit(solution)/shard_map/ppermute | solution.py:350
  4.9 0.0 collective-permute-start.1
  4.9 0.5 %collective-permute-start.2 = (bf16[144,256]{1,0:T(8,128)(2,1)S(1)}, bf16[144,256]{1,0:T(8,128)(2,1)S(1)}, u32[]{:S(2)}, u32[]{:S(2)}) collective-permute-start(bf16[144,256]{1,0:T(8,128)(2,1)S(1)} %get-tuple-element.30), channel_id=1, source_target_pairs={{0,1},{1,0},{2,3},{3,2},{4,5},{5,4},{6,7},{7,6},{8,9},{9,8},{10,11... | collective-permute-start | bytes 221192 | tf_op jit(solution)/shard_map/ppermute | solution.py:350
  5.4 1.1 %collective-permute-start.3 = (bf16[144,256]{1,0:T(8,128)(2,1)S(1)}, bf16[144,256]{1,0:T(8,128)(2,1)S(1)}, u32[]{:S(2)}, u32[]{:S(2)}) collective-permute-start(bf16[144,256]{1,0:T(8,128)(2,1)S(1)} %get-tuple-element.31), channel_id=1, source_target_pairs={{0,3},{1,2},{2,1},{3,0},{4,7},{5,6},{6,5},{7,4},{8,11},{9,10},{10,... | collective-permute-start | bytes 221192 | tf_op jit(solution)/shard_map/ppermute | solution.py:350
  6.5 0.0 copy-done.17
  6.5 0.1 copy.20.source
  6.6 0.0 copy-done.18
  6.6 0.1 copy.21.live
  6.7 0.0 copy-done.2
  6.7 1.2 %local_edges.1.aggregate = f32[1024,256]{1,0:T(8,128)S(1)} custom-call(bf16[1024,256]{1,0:T(8,128)(2,1)S(1)} %get-tuple-element.27.messages, bf16[1,1,8,3,128,128]{5,4,3,2,1,0:T(8,128)(2,1)S(1)} %copy-done.2, s32[1,1,8,3]{3,2,1,0:T(8,128)S(1)} %copy.20.source, s32[1,1,8,3]{3,2,1,0:T(8,128)S(1)} %copy.21.live), custom_call_target="tpu_custom_call" | custom-call | bytes 1048576 | tf_op jit(solution)/shard_map/local_edges/pallas_call | solution.py:312
  7.9 0.3 collective-permute-done.rec0
  8.2 0.0 collective-permute-done.1.rec1
  8.2 0.0 collective-permute-done.2.rec2.refs_3_
  8.2 1.5 %collective-permute-done.3.rec3.refs_4_ = bf16[144,256]{1,0:T(8,128)(2,1)S(1)} collective-permute-done((bf16[144,256]{1,0:T(8,128)(2,1)S(1)}, bf16[144,256]{1,0:T(8,128)(2,1)S(1)}, u32[]{:S(2)}, u32[]{:S(2)}) %collective-permute-start.3) | collective-permute-done | bytes 73760 | tf_op jit(solution)/shard_map/ppermute | solution.py:350
  9.8 0.0 copy-done.6
  9.8 0.0 copy-done.7
  9.8 0.0 copy-done.15
  9.8 1.8 %second_messages.1 = (f32[1024,256]{1,0:T(8,128)S(1)}, bf16[1024,256]{1,0:T(8,128)(2,1)S(1)}, bf16[128,256]{1,0:T(8,128)(2,1)S(1)}, bf16[128,256]{1,0:T(8,128)(2...) custom-call(bf16[1024,256]{1,0:T(8,128)(2,1)S(1)} %copy-done.3, ...), custom_call_target="tpu_custom_call" | custom-call | bytes 1048576 | tf_op jit(solution)/shard_map/second_messages/pallas_call | solution.py:312
  11.6 2.2 %collective-permute-start.4 = (bf16[128,256]{1,0:T(8,128)(2,1)S(1)}, bf16[128,256]{1,0:T(8,128)(2,1)S(1)}, u32[]{:S(2)}, u32[]{:S(2)}) collective-permute-start(bf16[128,256]{1,0:T(8,128)(2,1)S(1)} %get-tuple-element.34), channel_id=1, source_target_pairs={{0,4},{1,5},{2,6},{3,7},{4,0},{5,1},{6,2},{7,3},{8,12},{9,13},{10,... | collective-permute-start | bytes 196616 | tf_op jit(solution)/shard_map/ppermute | solution.py:350
  13.8 0.2 collective-permute-start.5
  14.0 0.3 collective-permute-start.6
  14.3 1.3 %collective-permute-start.7 = (bf16[128,256]{1,0:T(8,128)(2,1)S(1)}, bf16[128,256]{1,0:T(8,128)(2,1)S(1)}, u32[]{:S(2)}, u32[]{:S(2)}) collective-permute-start(bf16[128,256]{1,0:T(8,128)(2,1)S(1)} %get-tuple-element.37), channel_id=1, source_target_pairs={{0,3},{1,2},{2,1},{3,0},{4,7},{5,6},{6,5},{7,4},{8,11},{9,10},{10,... | collective-permute-start | bytes 196616 | tf_op jit(solution)/shard_map/ppermute | solution.py:350
  15.6 1.2 %local_edges_again.1.aggregate = f32[1024,256]{1,0:T(8,128)S(1)} custom-call(bf16[1024,256]{1,0:T(8,128)(2,1)S(1)} %get-tuple-element.33.messages.refs_5_, bf16[1,1,8,3,128,128]{5,4,3,2,1,0:T(8,128)(2,1)S(1)} %copy-done.2, s32[1,1,8,3]{3,2,1,0:T(8,128)S(1)} %copy.20.source, s32[1,1,8,3]{3,2,1,0:T(8,128)S(1)} %copy.21.live), custom_call_target="tpu_custom_call" | custom-call | bytes 1048576 | tf_op jit(solution)/shard_map/local_edges_again/pallas_call | solution.py:312
  16.8 0.0 copy-done.11
  16.8 0.0 copy-done.12
  16.8 0.0 copy-done.13
  16.8 0.0 copy-start.9
  16.8 0.5 %slots.1 = (s32[2,1024]{1,0:T(2,128)S(1)}, s32[4,512]{1,0:T(4,128)S(1)}) custom-call(s32[1,1,1024]{2,1,0:T(1,128)S(1)} %copy-done.11, s32[1,1,1024]{2,1,0:T(1,128)S(1)} %copy-done.12, s32[1,1,1024]{2,1,0:T(1,128)S(1)} %copy-done.13, bf16[144,256]{1,0:T(8,128)(2,1)S(1)} %collective-permute-done.2.rec2.refs_3_, ...), custom_call_target="tpu_custom_call" | custom-call | bytes 1048576 | tf_op jit(solution)/shard_map/slots/pallas_call | solution.py:312
  17.3 0.0 collective-permute-done.4.rec0
  17.3 0.0 collective-permute-done.5.rec1
  17.3 0.0 collective-permute-done.6.rec2
  17.3 1.1 %collective-permute-done.7.rec3 = bf16[128,256]{1,0:T(8,128)(2,1)S(1)} collective-permute-done((bf16[128,256]{1,0:T(8,128)(2,1)S(1)}, bf16[128,256]{1,0:T(8,128)(2,1)S(1)}, u32[]{:S(2)}, u32[]{:S(2)}) %collective-permute-start.7) | collective-permute-done | bytes 65568 | tf_op jit(solution)/shard_map/ppermute | solution.py:350
  18.4 0.0 copy-done.9
  18.4 5.2 %ball_attention.1 = (f32[1024,256]{1,0:T(8,128)S(1)}, bf16[1024,256]{1,0:T(8,128)(2,1)S(1)}) custom-call(f32[1024,256]{1,0:T(8,128)S(1)} %get-tuple-element.32.state, f32[1024,256]{1,0:T(8,128)S(1)} %local_edges_again.1.aggregate, bf16[128,256]{1,0:T(8,128)(2,1)S(1)} %collective-permute-done.4.rec0, bf16[128,256]{1,0:T(8,128)(2,1)S(1)} %collective-permute-done.5.rec1, ...), custom_call_target="tpu_custom_call" | custom-call | bytes 1048576 | tf_op jit(solution)/shard_map/ball_attention/pallas_call | solution.py:312
  23.6 0.0 copy-done
  23.6 0.0 copy-done.1
  23.6 0.0 copy-done.4
  23.6 2.0 %light_rows.1 = (bf16[176,256]{1,0:T(8,128)(2,1)S(1)}, bf16[176,256]{1,0:T(8,128)(2,1)S(1)}, bf16[176,256]{1,0:T(8,128)(2,1)S(1)}) custom-call(f32[1024,256]{1,0:T(8,128)S(1)} %get-tuple-element.38.refs_0_.state, bf16[1024,256]{1,0:T(8,128)(2,1)S(1)} %get-tuple-element.39.refs_1_.mixed, s32[2,1024]{1,0:T(2,128)S(1)} %get-tuple-element.40.refs_2_, ...), custom_call_target="tpu_custom_call" | custom-call | bytes 1048576 | tf_op jit(solution)/shard_map/light_rows/pallas_call | solution.py:312
  25.6 1.6 %collective-permute-start.9 = (bf16[176,256]{1,0:T(8,128)(2,1)S(1)}, bf16[176,256]{1,0:T(8,128)(2,1)S(1)}, u32[]{:S(2)}, u32[]{:S(2)}) collective-permute-start(bf16[176,256]{1,0:T(8,128)(2,1)S(1)} %get-tuple-element.43), channel_id=1, source_target_pairs={{0,2},{1,3},{2,0},{3,1},{4,6},{5,7},{6,4},{7,5},{8,10},{9,11},{10,... | collective-permute-start | bytes 270344 | tf_op jit(solution)/shard_map/ppermute | solution.py:358
  27.2 0.0 collective-permute-start.10
  27.2 0.6 %collective-permute-start.8 = (bf16[176,256]{1,0:T(8,128)(2,1)S(1)}, bf16[176,256]{1,0:T(8,128)(2,1)S(1)}, u32[]{:S(2)}, u32[]{:S(2)}) collective-permute-start(bf16[176,256]{1,0:T(8,128)(2,1)S(1)} %get-tuple-element.41.refs_6_), channel_id=1, source_target_pairs={{0,1},{1,0},{2,3},{3,2},{4,5},{5,4},{6,7},{7,6},{8,9},{9,8},{10,11... | collective-permute-start | bytes 270344 | tf_op jit(solution)/shard_map/ppermute | solution.py:358
  27.8 2.1 %heavy_rows.1.after.refs_3_ = bf16[512,256]{1,0:T(8,128)(2,1)S(1)} custom-call(f32[1024,256]{1,0:T(8,128)S(1)} %get-tuple-element.38.refs_0_.state, bf16[1024,256]{1,0:T(8,128)(2,1)S(1)} %get-tuple-element.39.refs_1_.mixed, s32[2,1024]{1,0:T(2,128)S(1)} %get-tuple-element.40.refs_2_, bf16[256,256]{1,0:T(8,128)(2,1)S(1)} %copy-done.4, ...), custom_call_target="tpu_custom_call" | custom-call | bytes 1048576 | tf_op jit(solution)/shard_map/heavy_rows/pallas_call | solution.py:312
  29.9 0.0 copy-start.10
  29.9 1.0 %kept_rows.1.refs_0_ = f32[1024,256]{1,0:T(8,128)S(1)} custom-call(f32[1024,256]{1,0:T(8,128)S(1)} %get-tuple-element.38.refs_0_.state, bf16[1024,256]{1,0:T(8,128)(2,1)S(1)} %get-tuple-element.39.refs_1_.mixed, s32[1,1,1024]{2,1,0:T(1,128)S(1)} %copy-done.11, bf16[256,256]{1,0:T(8,128)(2,1)S(1)} %copy-done.4, bf16[512,256]{1,0:T(8,128)(2,1)S(1)} %heavy_rows.1.after.refs_3_), custom_call_target="tpu_custom_call" | custom-call | bytes 1048576 | tf_op jit(solution)/shard_map/kept_rows/pallas_call | solution.py:312
  30.9 0.0 collective-permute-done.9.refs_5_
  30.9 1.2 %collective-permute-done.10.refs_6_ = bf16[176,256]{1,0:T(8,128)(2,1)S(1)} collective-permute-done((bf16[176,256]{1,0:T(8,128)(2,1)S(1)}, bf16[176,256]{1,0:T(8,128)(2,1)S(1)}, u32[]{:S(2)}, u32[]{:S(2)}) %collective-permute-start.10) | collective-permute-done | bytes 90144 | tf_op jit(solution)/shard_map/ppermute | solution.py:358
  32.1 0.0 collective-permute-done.8.refs_4_
  32.1 0.0 copy-done.10
  32.1 4.9 %owner_layer.1 = (bf16[176,256]{1,0:T(8,128)(2,1)S(1)}, bf16[176,256]{1,0:T(8,128)(2,1)S(1)}, bf16[176,256]{1,0:T(8,128)(2,1)S(1)}, bf16[1024,256]{1,0:T(8,128)(2,1)S(1)}) custom-call(f32[1024,256]{1,0:T(8,128)S(1)} %kept_rows.1.refs_0_, s32[4,512]{1,0:T(4,128)S(1)} %get-tuple-element.42.refs_1_.refs_2_, bf16[256,768]{1,0:T(8,128)(2,1)S(1)} %copy-done.10, ...), custom_call_target="tpu_custom_call" | custom-call | bytes 1048576 | tf_op jit(solution)/shard_map/owner_layer/pallas_call | solution.py:312
  36.9 0.9 %collective-permute-start.12 = (bf16[176,256]{1,0:T(8,128)(2,1)S(1)}, bf16[176,256]{1,0:T(8,128)(2,1)S(1)}, u32[]{:S(2)}, u32[]{:S(2)}) collective-permute-start(bf16[176,256]{1,0:T(8,128)(2,1)S(1)} %get-tuple-element.47), channel_id=1, source_target_pairs={{2,0},{3,1},{0,2},{1,3},{6,4},{7,5},{4,6},{5,7},{10,8},{11,9},{8,1... | collective-permute-start | bytes 270344 | tf_op jit(solution)/shard_map/ppermute | solution.py:358
  37.8 0.7 %collective-permute-start.13 = (bf16[176,256]{1,0:T(8,128)(2,1)S(1)}, bf16[176,256]{1,0:T(8,128)(2,1)S(1)}, u32[]{:S(2)}, u32[]{:S(2)}) collective-permute-start(bf16[176,256]{1,0:T(8,128)(2,1)S(1)} %get-tuple-element.48), channel_id=1, source_target_pairs={{3,0},{2,1},{1,2},{0,3},{7,4},{6,5},{5,6},{4,7},{11,8},{10,9},{9,1... | collective-permute-start | bytes 270344 | tf_op jit(solution)/shard_map/ppermute | solution.py:358
  38.5 0.7 %collective-permute-start.11 = (bf16[176,256]{1,0:T(8,128)(2,1)S(1)}, bf16[176,256]{1,0:T(8,128)(2,1)S(1)}, u32[]{:S(2)}, u32[]{:S(2)}) collective-permute-start(bf16[176,256]{1,0:T(8,128)(2,1)S(1)} %get-tuple-element.46.refs_8_), channel_id=1, source_target_pairs={{1,0},{0,1},{3,2},{2,3},{5,4},{4,5},{7,6},{6,7},{9,8},{8,9},{11,10... | collective-permute-start | bytes 270344 | tf_op jit(solution)/shard_map/ppermute | solution.py:358
  39.2 0.0 copy-done.8
  39.2 3.0 %stayed_changes.1.refs_0_ = f32[1024,256]{1,0:T(8,128)S(1)} custom-call(f32[1024,256]{1,0:T(8,128)S(1)} %kept_rows.1.refs_0_, bf16[1024,256]{1,0:T(8,128)(2,1)S(1)} %get-tuple-element.45.refs_1_, s32[4,512]{1,0:T(4,128)S(1)} %get-tuple-element.42.refs_1_.refs_2_, s32[1,1,1024]{2,1,0:T(1,128)S(1)} %copy-done.12, s32[1,1,1024]{2,1,0:T(1,128)S(1)} %copy-done.13, ...), custom_call_target="tpu_custom_call" | custom-call | bytes 1048576 | tf_op jit(solution)/shard_map/stayed_changes/pallas_call | solution.py:312
  42.1 0.3 collective-permute-done.12.refs_5_
  42.5 0.3 collective-permute-done.13.refs_6_
  42.8 0.0 collective-permute-done.11.refs_4_
  42.8 1.9 %relayed_changes.1 = f32[1024,256]{1,0:T(8,128)} custom-call(f32[1024,256]{1,0:T(8,128)S(1)} %stayed_changes.1.refs_0_, s32[1,1,1024]{2,1,0:T(1,128)S(1)} %copy-done.12, s32[1,1,1024]{2,1,0:T(1,128)S(1)} %copy-done.13, bf16[256,256]{1,0:T(8,128)(2,1)S(1)} %copy-done.8, bf16[176,256]{1,0:T(8,128)(2,1)S(1)} %collective-permute-done.11.refs_4_, ...), custom_call_target="tpu_custom_call" | custom-call | bytes 1048576 | tf_op jit(solution)/shard_map/relayed_changes/pallas_call | solution.py:312
  (17 shorter events, 0.0 us)
Async XLA Ops:
  0.0 0.9 %copy-start.5 = (bf16[2,256,256]{2,1,0:T(8,128)(2,1)S(1)}, bf16[2,256,256]{2,1,0:T(8,128)(2,1)}, u32[]{:S(2)}) copy-start(bf16[2,256,256]{2,1,0:T(8,128)(2,1)} %w_msg.3) | copy-start | bytes 786436
  0.0 1.1 %copy-start.3 = (bf16[1024,256]{1,0:T(8,128)(2,1)S(1)}, bf16[1024,256]{1,0:T(8,128)(2,1)}, u32[]{:S(2)}) copy-start(bf16[1024,256]{1,0:T(8,128)(2,1)} %state.1) | copy-start | bytes 1572868
  0.0 1.1 %copy-start.14 = (s32[1,1,4,512]{3,2,1,0:T(4,128)S(1)}, s32[1,1,4,512]{3,2,1,0:T(4,128)}, u32[]{:S(2)}) copy-start(s32[1,1,4,512]{3,2,1,0:T(4,128)} %inbox.1) | copy-start | bytes 24580
  0.0 0.8 %copy-start.16 = (s32[1,1,4,128]{3,2,1,0:T(4,128)S(1)}, s32[1,1,4,128]{3,2,1,0:T(4,128)}, u32[]{:S(2)}) copy-start(s32[1,1,4,128]{3,2,1,0:T(4,128)} %rim_rows.3) | copy-start | bytes 6148
  1.1 5.5 %copy-start.2 = (bf16[1,1,8,3,128,128]{5,4,3,2,1,0:T(8,128)(2,1)S(1)}, bf16[1,1,8,3,128,128]{5,4,3,2,1,0:T(8,128)(2,1)}, u32[]{:S(2)}) copy-start(bf16[1,1,8,3,128,128]{5,4,3,2,1,0:T(8,128)(2,1)} %tiles.6) | copy-start | bytes 2359300
  1.9 6.4 %collective-permute-start = (bf16[144,256]{1,0:T(8,128)(2,1)S(1)}, bf16[144,256]{1,0:T(8,128)(2,1)S(1)}, u32[]{:S(2)}, u32[]{:S(2)}) collective-permute-start(bf16[144,256]{1,0:T(8,128)(2,1)S(1)} %get-tuple-element.28), channel_id=1, source_target_pairs={{0,4},{1,5},{2,6},{3,7},{4,0},{5,1},{6,2},{7,3},{8,12},{9,13},{10,... | collective-permute-start | bytes 221192 | tf_op jit(solution)/shard_map/ppermute | solution.py:350
  4.9 1.6 %copy-start.17 = (s32[1,1,8,3]{2,1,3,0:T(1,128)S(1)}, s32[1,1,8,3]{2,1,3,0:T(1,128)}, u32[]{:S(2)}) copy-start(s32[1,1,8,3]{2,1,3,0:T(1,128)} %param.23) | copy-start | bytes 292
  4.9 3.4 %collective-permute-start.1 = (bf16[144,256]{1,0:T(8,128)(2,1)S(1)}, bf16[144,256]{1,0:T(8,128)(2,1)S(1)}, u32[]{:S(2)}, u32[]{:S(2)}) collective-permute-start(bf16[144,256]{1,0:T(8,128)(2,1)S(1)} %get-tuple-element.29), channel_id=1, source_target_pairs={{0,1},{1,0},{2,3},{3,2},{4,8},{5,9},{6,10},{7,11},{8,4},{9,5},{10,... | collective-permute-start | bytes 221192 | tf_op jit(solution)/shard_map/ppermute | solution.py:350
  4.9 3.4 %collective-permute-start.2 = (bf16[144,256]{1,0:T(8,128)(2,1)S(1)}, bf16[144,256]{1,0:T(8,128)(2,1)S(1)}, u32[]{:S(2)}, u32[]{:S(2)}) collective-permute-start(bf16[144,256]{1,0:T(8,128)(2,1)S(1)} %get-tuple-element.30), channel_id=1, source_target_pairs={{0,1},{1,0},{2,3},{3,2},{4,5},{5,4},{6,7},{7,6},{8,9},{9,8},{10,11... | collective-permute-start | bytes 221192 | tf_op jit(solution)/shard_map/ppermute | solution.py:350
  5.4 1.2 %copy-start.18 = (s32[1,1,8,3]{2,1,3,0:T(1,128)S(1)}, s32[1,1,8,3]{2,1,3,0:T(1,128)}, u32[]{:S(2)}) copy-start(s32[1,1,8,3]{2,1,3,0:T(1,128)} %param.24) | copy-start | bytes 292
  5.4 4.4 %collective-permute-start.3 = (bf16[144,256]{1,0:T(8,128)(2,1)S(1)}, bf16[144,256]{1,0:T(8,128)(2,1)S(1)}, u32[]{:S(2)}, u32[]{:S(2)}) collective-permute-start(bf16[144,256]{1,0:T(8,128)(2,1)S(1)} %get-tuple-element.31), channel_id=1, source_target_pairs={{0,3},{1,2},{2,1},{3,0},{4,7},{5,6},{6,5},{7,4},{8,11},{9,10},{10,... | collective-permute-start | bytes 221192 | tf_op jit(solution)/shard_map/ppermute | solution.py:350
  6.7 3.1 %copy-start.6 = (bf16[2,256,256]{2,1,0:T(8,128)(2,1)S(1)}, bf16[2,256,256]{2,1,0:T(8,128)(2,1)}, u32[]{:S(2)}) copy-start(bf16[2,256,256]{2,1,0:T(8,128)(2,1)} %w_upd.3) | copy-start | bytes 786436
  6.7 3.1 %copy-start.7 = (bf16[1,1,4,128,128]{4,3,2,1,0:T(8,128)(2,1)S(1)}, bf16[1,1,4,128,128]{4,3,2,1,0:T(8,128)(2,1)}, u32[]{:S(2)}) copy-start(bf16[1,1,4,128,128]{4,3,2,1,0:T(8,128)(2,1)} %tiles.7) | copy-start | bytes 393220
  6.7 3.1 %copy-start.15 = (s32[1,1,4]{2,1,0:T(1,128)S(1)}, s32[1,1,4]{2,1,0:T(1,128)}, u32[]{:S(2)}) copy-start(s32[1,1,4]{2,1,0:T(1,128)} %block.3) | copy-start | bytes 52
  11.6 5.7 %collective-permute-start.4 = (bf16[128,256]{1,0:T(8,128)(2,1)S(1)}, bf16[128,256]{1,0:T(8,128)(2,1)S(1)}, u32[]{:S(2)}, u32[]{:S(2)}) collective-permute-start(bf16[128,256]{1,0:T(8,128)(2,1)S(1)} %get-tuple-element.34), channel_id=1, source_target_pairs={{0,4},{1,5},{2,6},{3,7},{4,0},{5,1},{6,2},{7,3},{8,12},{9,13},{10,... | collective-permute-start | bytes 196616 | tf_op jit(solution)/shard_map/ppermute | solution.py:350
  13.8 3.6 %collective-permute-start.5 = (bf16[128,256]{1,0:T(8,128)(2,1)S(1)}, bf16[128,256]{1,0:T(8,128)(2,1)S(1)}, u32[]{:S(2)}, u32[]{:S(2)}) collective-permute-start(bf16[128,256]{1,0:T(8,128)(2,1)S(1)} %get-tuple-element.35), channel_id=1, source_target_pairs={{0,1},{1,0},{2,3},{3,2},{4,8},{5,9},{6,10},{7,11},{8,4},{9,5},{10,... | collective-permute-start | bytes 196616 | tf_op jit(solution)/shard_map/ppermute | solution.py:350
  14.0 3.4 %collective-permute-start.6 = (bf16[128,256]{1,0:T(8,128)(2,1)S(1)}, bf16[128,256]{1,0:T(8,128)(2,1)S(1)}, u32[]{:S(2)}, u32[]{:S(2)}) collective-permute-start(bf16[128,256]{1,0:T(8,128)(2,1)S(1)} %get-tuple-element.36), channel_id=1, source_target_pairs={{0,1},{1,0},{2,3},{3,2},{4,5},{5,4},{6,7},{7,6},{8,9},{9,8},{10,11... | collective-permute-start | bytes 196616 | tf_op jit(solution)/shard_map/ppermute | solution.py:350
  14.3 4.1 %collective-permute-start.7 = (bf16[128,256]{1,0:T(8,128)(2,1)S(1)}, bf16[128,256]{1,0:T(8,128)(2,1)S(1)}, u32[]{:S(2)}, u32[]{:S(2)}) collective-permute-start(bf16[128,256]{1,0:T(8,128)(2,1)S(1)} %get-tuple-element.37), channel_id=1, source_target_pairs={{0,3},{1,2},{2,1},{3,0},{4,7},{5,6},{6,5},{7,4},{8,11},{9,10},{10,... | collective-permute-start | bytes 196616 | tf_op jit(solution)/shard_map/ppermute | solution.py:350
  15.6 1.2 %copy-start.11 = (s32[1,1,1024]{2,1,0:T(1,128)S(1)}, s32[1,1,1024]{2,1,0:T(1,128)}, u32[]{:S(2)}) copy-start(s32[1,1,1024]{2,1,0:T(1,128)} %order.3) | copy-start | bytes 12292
  15.6 1.2 %copy-start.12 = (s32[1,1,1024]{2,1,0:T(1,128)S(1)}, s32[1,1,1024]{2,1,0:T(1,128)}, u32[]{:S(2)}) copy-start(s32[1,1,1024]{2,1,0:T(1,128)} %refs_1_.3) | copy-start | bytes 12292
  15.6 1.2 %copy-start.13 = (s32[1,1,1024]{2,1,0:T(1,128)S(1)}, s32[1,1,1024]{2,1,0:T(1,128)}, u32[]{:S(2)}) copy-start(s32[1,1,1024]{2,1,0:T(1,128)} %refs_2_.5) | copy-start | bytes 12292
  16.8 1.6 %copy-start.9 = (bf16[256,768]{1,0:T(8,128)(2,1)S(1)}, bf16[256,768]{1,0:T(8,128)(2,1)}, u32[]{:S(2)}) copy-start(bf16[256,768]{1,0:T(8,128)(2,1)} %w_qkv.1) | copy-start | bytes 1179652
  18.4 5.2 %copy-start = (bf16[256,1024]{1,0:T(8,128)(2,1)S(1)}, bf16[256,1024]{1,0:T(8,128)(2,1)}, u32[]{:S(2)}) copy-start(bf16[256,1024]{1,0:T(8,128)(2,1)} %refs_5_.5) | copy-start | bytes 1572868
  18.4 5.2 %copy-start.1 = (bf16[1024,256]{1,0:T(8,128)(2,1)S(1)}, bf16[1024,256]{1,0:T(8,128)(2,1)}, u32[]{:S(2)}) copy-start(bf16[1024,256]{1,0:T(8,128)(2,1)} %refs_6_.1) | copy-start | bytes 1572868
  18.4 5.2 %copy-start.4 = (bf16[256,256]{1,0:T(8,128)(2,1)S(1)}, bf16[256,256]{1,0:T(8,128)(2,1)}, u32[]{:S(2)}) copy-start(bf16[256,256]{1,0:T(8,128)(2,1)} %w_out.1) | copy-start | bytes 393220
  25.6 5.3 %collective-permute-start.9 = (bf16[176,256]{1,0:T(8,128)(2,1)S(1)}, bf16[176,256]{1,0:T(8,128)(2,1)S(1)}, u32[]{:S(2)}, u32[]{:S(2)}) collective-permute-start(bf16[176,256]{1,0:T(8,128)(2,1)S(1)} %get-tuple-element.43), channel_id=1, source_target_pairs={{0,2},{1,3},{2,0},{3,1},{4,6},{5,7},{6,4},{7,5},{8,10},{9,11},{10,... | collective-permute-start | bytes 270344 | tf_op jit(solution)/shard_map/ppermute | solution.py:358
  27.2 4.9 %collective-permute-start.10 = (bf16[176,256]{1,0:T(8,128)(2,1)S(1)}, bf16[176,256]{1,0:T(8,128)(2,1)S(1)}, u32[]{:S(2)}, u32[]{:S(2)}) collective-permute-start(bf16[176,256]{1,0:T(8,128)(2,1)S(1)} %get-tuple-element.44), channel_id=1, source_target_pairs={{0,3},{1,2},{2,1},{3,0},{4,7},{5,6},{6,5},{7,4},{8,11},{9,10},{10,... | collective-permute-start | bytes 270344 | tf_op jit(solution)/shard_map/ppermute | solution.py:358
  27.2 4.9 %collective-permute-start.8 = (bf16[176,256]{1,0:T(8,128)(2,1)S(1)}, bf16[176,256]{1,0:T(8,128)(2,1)S(1)}, u32[]{:S(2)}, u32[]{:S(2)}) collective-permute-start(bf16[176,256]{1,0:T(8,128)(2,1)S(1)} %get-tuple-element.41.refs_6_), channel_id=1, source_target_pairs={{0,1},{1,0},{2,3},{3,2},{4,5},{5,4},{6,7},{7,6},{8,9},{9,8},{10,11... | collective-permute-start | bytes 270344 | tf_op jit(solution)/shard_map/ppermute | solution.py:358
  29.9 2.2 %copy-start.10 = (bf16[256,768]{1,0:T(8,128)(2,1)S(1)}, bf16[256,768]{1,0:T(8,128)(2,1)}, u32[]{:S(2)}) copy-start(bf16[256,768]{1,0:T(8,128)(2,1)} %refs_2_.4) | copy-start | bytes 1179652
  32.1 7.1 %copy-start.8 = (bf16[256,256]{1,0:T(8,128)(2,1)S(1)}, bf16[256,256]{1,0:T(8,128)(2,1)}, u32[]{:S(2)}) copy-start(bf16[256,256]{1,0:T(8,128)(2,1)} %refs_3_.7) | copy-start | bytes 393220
  36.9 5.5 %collective-permute-start.12 = (bf16[176,256]{1,0:T(8,128)(2,1)S(1)}, bf16[176,256]{1,0:T(8,128)(2,1)S(1)}, u32[]{:S(2)}, u32[]{:S(2)}) collective-permute-start(bf16[176,256]{1,0:T(8,128)(2,1)S(1)} %get-tuple-element.47), channel_id=1, source_target_pairs={{2,0},{3,1},{0,2},{1,3},{6,4},{7,5},{4,6},{5,7},{10,8},{11,9},{8,1... | collective-permute-start | bytes 270344 | tf_op jit(solution)/shard_map/ppermute | solution.py:358
  37.8 4.9 %collective-permute-start.13 = (bf16[176,256]{1,0:T(8,128)(2,1)S(1)}, bf16[176,256]{1,0:T(8,128)(2,1)S(1)}, u32[]{:S(2)}, u32[]{:S(2)}) collective-permute-start(bf16[176,256]{1,0:T(8,128)(2,1)S(1)} %get-tuple-element.48), channel_id=1, source_target_pairs={{3,0},{2,1},{1,2},{0,3},{7,4},{6,5},{5,6},{4,7},{11,8},{10,9},{9,1... | collective-permute-start | bytes 270344 | tf_op jit(solution)/shard_map/ppermute | solution.py:358
  38.5 4.3 %collective-permute-start.11 = (bf16[176,256]{1,0:T(8,128)(2,1)S(1)}, bf16[176,256]{1,0:T(8,128)(2,1)S(1)}, u32[]{:S(2)}, u32[]{:S(2)}) collective-permute-start(bf16[176,256]{1,0:T(8,128)(2,1)S(1)} %get-tuple-element.46.refs_8_), channel_id=1, source_target_pairs={{1,0},{0,1},{3,2},{2,3},{5,4},{4,5},{7,6},{6,7},{9,8},{8,9},{11,10... | collective-permute-start | bytes 270344 | tf_op jit(solution)/shard_map/ppermute | solution.py:358

commit v6 on v5

--- a/solution.py
+++ b/solution.py
@@ -62,7 +62,7 @@
     return hot(iota((height, lane_rows.shape[1]), 0) == lane_rows)
 
 
-def attention(rows_in, weight_qkv, store):
+def attention(rows_in, weight_qkv, store, late=False):
     width = rows_in.shape[1]
     head = width // HEADS
     scale = math.log2(math.e) / math.sqrt(head)
@@ -70,24 +70,31 @@
     masks = [hot(lane_head == h) for h in range(HEADS)]
     joined = dot(rows_in, weight_qkv).astype(BF16)
 
-    def mix(ball, weights, values):
+    def mix(ball, weights, scales, values):
         spread = jnp.concatenate([values * mask for mask in masks], axis=0)
-        store(ball, dot(jnp.concatenate(weights, axis=1), spread).astype(BF16))
+        mixed = dot(jnp.concatenate(weights, axis=1), spread)
+        if late:
+            scale_of = jnp.broadcast_to(scales[0], mixed.shape)
+            for h in range(1, HEADS):
+                scale_of = jnp.where(lane_head == h, scales[h], scale_of)
+            mixed = mixed * scale_of
+        store(ball, mixed.astype(BF16))
 
     pending = None
     for ball in range(rows_in.shape[0] // BALL):
         own = joined[ball * BALL : (ball + 1) * BALL]
         query, keys, values = own[:, :width], own[:, width : 2 * width], own[:, 2 * width :]
-        weights = []
+        weights, scales = [], []
         for h in range(HEADS):
             near = slice(h * head // LANES * LANES, (h * head // LANES + 1) * LANES)
             scores = dot_rows(query[:, near] * masks[h][:, near], keys[:, near])
             top = jnp.max(scores, axis=-1, keepdims=True)
             raw = jnp.exp2((scores - top) * scale)
-            weights.append((raw * (1.0 / jnp.sum(raw, axis=-1, keepdims=True))).astype(BF16))
+            scales.append(1.0 / jnp.sum(raw, axis=-1, keepdims=True))
+            weights.append((raw if late else raw * scales[-1]).astype(BF16))
         if pending is not None:
             mix(*pending)
-        pending = (ball, weights, values)
+        pending = (ball, weights, scales, values)
     mix(*pending)
 
 
@@ -214,7 +221,7 @@
     def store(ball, value):
         mixed[ball * BALL : (ball + 1) * BALL, :] = value
 
-    attention(jnp.concatenate(balled, axis=0), w_qkv[...], store)
+    attention(jnp.concatenate(balled, axis=0), w_qkv[...], store, late=True)
 
 
 def feed(pieces, w_in, w_mlp_out):
@@ -291,7 +298,7 @@
 
 
 def last_kernel(state, peer, rank, w_out, *refs, members, capacity, light, wide):
-    returned, out, rows_in = refs[: members - 1], *refs[members - 1 :]
+    returned, out, rows_in, new, sems = refs[: members - 1], *refs[members - 1 :]
     me = lax.axis_index("rot")
     for at, rows in enumerate(returned):
         rows_in[at * wide : at * wide + light, :] = rows[...]
@@ -300,21 +307,31 @@
                 (wide - light, rows_in.shape[1]), BF16
             )
     slots = slot_of(peer[0], rank[0], me, members, capacity, wide) - capacity
-    update = dot(picks(slots, rows_in.shape[0]), rows_in[...]).astype(BF16)
-    out[...] = state[...] + dot(update, w_out[...])
+    change = dot(rows_in[...], w_out[...]).astype(BF16)
+    update = dot(picks(slots, rows_in.shape[0]), change)
+    step = state.shape[0] // 4
+    copies = []
+    for c in range(4):
+        rows = slice(c * step, (c + 1) * step)
+        new[rows, :] = state[rows, :] + update[rows]
+        copies.append(pltpu.make_async_copy(new.at[rows], out.at[rows], sems.at[c]))
+        copies[-1].start()
+    for copy in copies:
+        copy.wait()
 
 
 VMEM = pl.BlockSpec(memory_space=pltpu.VMEM)
 SMEM = pl.BlockSpec(memory_space=pltpu.SMEM)
 
 
-def call(kernel, args, outs, scalars=(), scratch=(), flops=0, moved=1 << 20, name=None):
+def call(kernel, args, outs, scalars=(), far_outs=(), scratch=(), sems=0, flops=0, moved=1 << 20, name=None):
     return pl.pallas_call(
         kernel,
         out_shape=[jax.ShapeDtypeStruct(shape, kind) for shape, kind in outs],
         in_specs=[SMEM if i in scalars else VMEM for i in range(len(args))],
-        out_specs=[VMEM] * len(outs),
-        scratch_shapes=[pltpu.VMEM(shape, kind) for shape, kind in scratch],
+        out_specs=[pl.BlockSpec(memory_space=pl.ANY) if i in far_outs else VMEM for i in range(len(outs))],
+        scratch_shapes=[pltpu.VMEM(shape, kind) for shape, kind in scratch]
+        + ([pltpu.SemaphoreType.DMA((sems,))] if sems else []),
         compiler_params=pltpu.CompilerParams(vmem_limit_bytes=48 * 1024 * 1024),
         cost_estimate=pl.CostEstimate(flops=flops, bytes_accessed=moved, transcendentals=0),
         name=name,
@@ -442,7 +459,7 @@
     rows_in = (((members - 1) * wide, width), BF16)
     (out,) = call(
         bound(last_kernel, wide=wide, **sizes), (state, relay_peer, relay_rank, w_rot_out, *parts),
-        [grid], scratch=[rows_in], name="relayed_changes",
+        [grid], far_outs=(0,), scratch=[rows_in, grid], sems=4, name="relayed_changes",
     )
     return out
 

time: 45.1 us -> 45 us (level)
  no operation moved by 1% of the time
where the time goes in v6:
time: 45 us; the launch traced here: 44.6 us
  Pallas kernels  25.2 us (56%)
  starting transfers between devices  13 us (29%)
  waiting for transfers between devices  4.73 us (11%)
  local copies, waits for them, and re-layouts  1.22 us (3%)
    pallas_call x13, Pallas kernels, call(): pl.pallas_call(kernel, out_shape=[jax.ShapeDtypeStruct(shape, kind) for s...  25.2 us
    ppermute x8, starting transfers between devices, exchange(): moved[i] = lax.ppermute(rims[i], ('grp', 'rot'), plan[i])  8.6 us
    ppermute x6, starting transfers between devices, relay(): lax.ppermute(rows, 'rot', [pair[::-1] for pair in pairs] if back else pairs)  4.41 us
    ppermute x8, waiting for transfers between devices, exchange(): moved[i] = lax.ppermute(rims[i], ('grp', 'rot'), plan[i])  2.91 us
    ppermute x6, waiting for transfers between devices, relay(): lax.ppermute(rows, 'rot', [pair[::-1] for pair in pairs] if back else pairs)  1.82 us
    unnamed x40, local copies, waits for them, and re-layouts  1.22 us
  transfers between devices with their start and end apart: 14, of which 6 were waited for; matrix products, arithmetic and copies ran while one was open for 0% of the time, Pallas kernels for 20%

profile of v6, /device:TPU:0, one launch (start us, length us, event | category | flops | bytes accessed | tf_op | source)
XLA Modules:
  0.0 44.6 jit_solution(7519258966006197607)
XLA Ops:
  0.0 0.8 %copy-done.16 = s32[1,1,4,128]{3,2,1,0:T(4,128)S(1)} copy-done((s32[1,1,4,128]{3,2,1,0:T(4,128)S(1)}, s32[1,1,4,128]{3,2,1,0:T(4,128)}, u32[]{:S(2)}) %copy-start.16) | copy-done | bytes 2072
  0.8 0.1 rim_rows.2.chosen
  0.9 0.1 copy-done.5
  1.0 0.2 copy-done.3
  1.1 0.0 copy-done.14
  1.1 0.7 %first_messages.1 = (bf16[1024,256]{1,0:T(8,128)(2,1)S(1)}, bf16[144,256]{1,0:T(8,128)(2,1)S(1)}, bf16[144,256]{1,0:T(8,128)(2,1)S(1)}, bf16[144,256]{1,0:T(8,128)(2,1)S(1)}, bf16[144,256]{1,0:T(8,128)(2,1)S(1)}) custom-call(s32[4,128,128]{2,1,0:T(8,128)S(1)} %rim_rows.2.chosen, bf16[1024,256]{1,0:T(8,128)(2,1)S(1)} %copy-done.3, ...), custom_call_target="tpu_custom_call" | custom-call | bytes 1048576 | tf_op jit(solution)/shard_map/first_messages/pallas_call | solution.py:328
  1.9 3.0 %collective-permute-start = (bf16[144,256]{1,0:T(8,128)(2,1)S(1)}, bf16[144,256]{1,0:T(8,128)(2,1)S(1)}, u32[]{:S(2)}, u32[]{:S(2)}) collective-permute-start(bf16[144,256]{1,0:T(8,128)(2,1)S(1)} %get-tuple-element.28), channel_id=1, source_target_pairs={{0,4},{1,5},{2,6},{3,7},{4,0},{5,1},{6,2},{7,3},{8,12},{9,13},{10,... | collective-permute-start | bytes 221192 | tf_op jit(solution)/shard_map/ppermute | solution.py:367
  4.9 0.0 collective-permute-start.1
  4.9 0.5 %collective-permute-start.2 = (bf16[144,256]{1,0:T(8,128)(2,1)S(1)}, bf16[144,256]{1,0:T(8,128)(2,1)S(1)}, u32[]{:S(2)}, u32[]{:S(2)}) collective-permute-start(bf16[144,256]{1,0:T(8,128)(2,1)S(1)} %get-tuple-element.30), channel_id=1, source_target_pairs={{0,1},{1,0},{2,3},{3,2},{4,5},{5,4},{6,7},{7,6},{8,9},{9,8},{10,11... | collective-permute-start | bytes 221192 | tf_op jit(solution)/shard_map/ppermute | solution.py:367
  5.4 1.1 %collective-permute-start.3 = (bf16[144,256]{1,0:T(8,128)(2,1)S(1)}, bf16[144,256]{1,0:T(8,128)(2,1)S(1)}, u32[]{:S(2)}, u32[]{:S(2)}) collective-permute-start(bf16[144,256]{1,0:T(8,128)(2,1)S(1)} %get-tuple-element.31), channel_id=1, source_target_pairs={{0,3},{1,2},{2,1},{3,0},{4,7},{5,6},{6,5},{7,4},{8,11},{9,10},{10,... | collective-permute-start | bytes 221192 | tf_op jit(solution)/shard_map/ppermute | solution.py:367
  6.5 0.0 copy-done.17
  6.5 0.1 copy.20.source
  6.6 0.0 copy-done.18
  6.6 0.1 copy.21.live
  6.7 0.0 copy-done.2
  6.7 1.2 %local_edges.1.aggregate = f32[1024,256]{1,0:T(8,128)S(1)} custom-call(bf16[1024,256]{1,0:T(8,128)(2,1)S(1)} %get-tuple-element.27.messages, bf16[1,1,8,3,128,128]{5,4,3,2,1,0:T(8,128)(2,1)S(1)} %copy-done.2, s32[1,1,8,3]{3,2,1,0:T(8,128)S(1)} %copy.20.source, s32[1,1,8,3]{3,2,1,0:T(8,128)S(1)} %copy.21.live), custom_call_target="tpu_custom_call" | custom-call | bytes 1048576 | tf_op jit(solution)/shard_map/local_edges/pallas_call | solution.py:328
  7.9 0.3 collective-permute-done.rec0
  8.2 0.0 collective-permute-done.1.rec1
  8.2 0.0 collective-permute-done.2.rec2.refs_3_
  8.2 1.5 %collective-permute-done.3.rec3.refs_4_ = bf16[144,256]{1,0:T(8,128)(2,1)S(1)} collective-permute-done((bf16[144,256]{1,0:T(8,128)(2,1)S(1)}, bf16[144,256]{1,0:T(8,128)(2,1)S(1)}, u32[]{:S(2)}, u32[]{:S(2)}) %collective-permute-start.3) | collective-permute-done | bytes 73760 | tf_op jit(solution)/shard_map/ppermute | solution.py:367
  9.8 0.0 copy-done.6
  9.8 0.0 copy-done.7
  9.8 0.0 copy-done.15
  9.8 1.8 %second_messages.1 = (f32[1024,256]{1,0:T(8,128)S(1)}, bf16[1024,256]{1,0:T(8,128)(2,1)S(1)}, bf16[128,256]{1,0:T(8,128)(2,1)S(1)}, bf16[128,256]{1,0:T(8,128)(2...) custom-call(bf16[1024,256]{1,0:T(8,128)(2,1)S(1)} %copy-done.3, ...), custom_call_target="tpu_custom_call" | custom-call | bytes 1048576 | tf_op jit(solution)/shard_map/second_messages/pallas_call | solution.py:328
  11.6 2.2 %collective-permute-start.4 = (bf16[128,256]{1,0:T(8,128)(2,1)S(1)}, bf16[128,256]{1,0:T(8,128)(2,1)S(1)}, u32[]{:S(2)}, u32[]{:S(2)}) collective-permute-start(bf16[128,256]{1,0:T(8,128)(2,1)S(1)} %get-tuple-element.34), channel_id=1, source_target_pairs={{0,4},{1,5},{2,6},{3,7},{4,0},{5,1},{6,2},{7,3},{8,12},{9,13},{10,... | collective-permute-start | bytes 196616 | tf_op jit(solution)/shard_map/ppermute | solution.py:367
  13.8 0.2 collective-permute-start.5
  14.0 0.3 collective-permute-start.6
  14.3 1.3 %collective-permute-start.7 = (bf16[128,256]{1,0:T(8,128)(2,1)S(1)}, bf16[128,256]{1,0:T(8,128)(2,1)S(1)}, u32[]{:S(2)}, u32[]{:S(2)}) collective-permute-start(bf16[128,256]{1,0:T(8,128)(2,1)S(1)} %get-tuple-element.37), channel_id=1, source_target_pairs={{0,3},{1,2},{2,1},{3,0},{4,7},{5,6},{6,5},{7,4},{8,11},{9,10},{10,... | collective-permute-start | bytes 196616 | tf_op jit(solution)/shard_map/ppermute | solution.py:367
  15.6 1.2 %local_edges_again.1.aggregate = f32[1024,256]{1,0:T(8,128)S(1)} custom-call(bf16[1024,256]{1,0:T(8,128)(2,1)S(1)} %get-tuple-element.33.messages.refs_5_, bf16[1,1,8,3,128,128]{5,4,3,2,1,0:T(8,128)(2,1)S(1)} %copy-done.2, s32[1,1,8,3]{3,2,1,0:T(8,128)S(1)} %copy.20.source, s32[1,1,8,3]{3,2,1,0:T(8,128)S(1)} %copy.21.live), custom_call_target="tpu_custom_call" | custom-call | bytes 1048576 | tf_op jit(solution)/shard_map/local_edges_again/pallas_call | solution.py:328
  16.8 0.0 copy-done.11
  16.8 0.0 copy-done.12
  16.8 0.0 copy-done.13
  16.8 0.0 copy-start.9
  16.8 0.5 %slots.1 = (s32[2,1024]{1,0:T(2,128)S(1)}, s32[4,512]{1,0:T(4,128)S(1)}) custom-call(s32[1,1,1024]{2,1,0:T(1,128)S(1)} %copy-done.11, s32[1,1,1024]{2,1,0:T(1,128)S(1)} %copy-done.12, s32[1,1,1024]{2,1,0:T(1,128)S(1)} %copy-done.13, bf16[144,256]{1,0:T(8,128)(2,1)S(1)} %collective-permute-done.2.rec2.refs_3_, ...), custom_call_target="tpu_custom_call" | custom-call | bytes 1048576 | tf_op jit(solution)/shard_map/slots/pallas_call | solution.py:328
  17.3 0.0 collective-permute-done.4.rec0
  17.3 0.0 collective-permute-done.5.rec1
  17.3 0.0 collective-permute-done.6.rec2
  17.3 1.1 %collective-permute-done.7.rec3 = bf16[128,256]{1,0:T(8,128)(2,1)S(1)} collective-permute-done((bf16[128,256]{1,0:T(8,128)(2,1)S(1)}, bf16[128,256]{1,0:T(8,128)(2,1)S(1)}, u32[]{:S(2)}, u32[]{:S(2)}) %collective-permute-start.7) | collective-permute-done | bytes 65568 | tf_op jit(solution)/shard_map/ppermute | solution.py:367
  18.4 0.0 copy-done.9
  18.4 5.1 %ball_attention.1 = (f32[1024,256]{1,0:T(8,128)S(1)}, bf16[1024,256]{1,0:T(8,128)(2,1)S(1)}) custom-call(f32[1024,256]{1,0:T(8,128)S(1)} %get-tuple-element.32.state, f32[1024,256]{1,0:T(8,128)S(1)} %local_edges_again.1.aggregate, bf16[128,256]{1,0:T(8,128)(2,1)S(1)} %collective-permute-done.4.rec0, bf16[128,256]{1,0:T(8,128)(2,1)S(1)} %collective-permute-done.5.rec1, ...), custom_call_target="tpu_custom_call" | custom-call | bytes 1048576 | tf_op jit(solution)/shard_map/ball_attention/pallas_call | solution.py:328
  23.5 0.0 copy-done
  23.5 0.0 copy-done.1
  23.5 0.0 copy-done.4
  23.5 2.0 %light_rows.1 = (bf16[176,256]{1,0:T(8,128)(2,1)S(1)}, bf16[176,256]{1,0:T(8,128)(2,1)S(1)}, bf16[176,256]{1,0:T(8,128)(2,1)S(1)}) custom-call(f32[1024,256]{1,0:T(8,128)S(1)} %get-tuple-element.38.refs_0_.state, bf16[1024,256]{1,0:T(8,128)(2,1)S(1)} %get-tuple-element.39.refs_1_.mixed, s32[2,1024]{1,0:T(2,128)S(1)} %get-tuple-element.40.refs_2_, ...), custom_call_target="tpu_custom_call" | custom-call | bytes 1048576 | tf_op jit(solution)/shard_map/light_rows/pallas_call | solution.py:328
  25.5 1.6 %collective-permute-start.9 = (bf16[176,256]{1,0:T(8,128)(2,1)S(1)}, bf16[176,256]{1,0:T(8,128)(2,1)S(1)}, u32[]{:S(2)}, u32[]{:S(2)}) collective-permute-start(bf16[176,256]{1,0:T(8,128)(2,1)S(1)} %get-tuple-element.43), channel_id=1, source_target_pairs={{0,2},{1,3},{2,0},{3,1},{4,6},{5,7},{6,4},{7,5},{8,10},{9,11},{10,... | collective-permute-start | bytes 270344 | tf_op jit(solution)/shard_map/ppermute | solution.py:375
  27.1 0.0 collective-permute-start.10
  27.1 0.6 %collective-permute-start.8 = (bf16[176,256]{1,0:T(8,128)(2,1)S(1)}, bf16[176,256]{1,0:T(8,128)(2,1)S(1)}, u32[]{:S(2)}, u32[]{:S(2)}) collective-permute-start(bf16[176,256]{1,0:T(8,128)(2,1)S(1)} %get-tuple-element.41.refs_6_), channel_id=1, source_target_pairs={{0,1},{1,0},{2,3},{3,2},{4,5},{5,4},{6,7},{7,6},{8,9},{9,8},{10,11... | collective-permute-start | bytes 270344 | tf_op jit(solution)/shard_map/ppermute | solution.py:375
  27.7 2.1 %heavy_rows.1.after.refs_3_ = bf16[512,256]{1,0:T(8,128)(2,1)S(1)} custom-call(f32[1024,256]{1,0:T(8,128)S(1)} %get-tuple-element.38.refs_0_.state, bf16[1024,256]{1,0:T(8,128)(2,1)S(1)} %get-tuple-element.39.refs_1_.mixed, s32[2,1024]{1,0:T(2,128)S(1)} %get-tuple-element.40.refs_2_, bf16[256,256]{1,0:T(8,128)(2,1)S(1)} %copy-done.4, ...), custom_call_target="tpu_custom_call" | custom-call | bytes 1048576 | tf_op jit(solution)/shard_map/heavy_rows/pallas_call | solution.py:328
  29.8 0.0 copy-start.10
  29.8 1.0 %kept_rows.1.refs_0_ = f32[1024,256]{1,0:T(8,128)S(1)} custom-call(f32[1024,256]{1,0:T(8,128)S(1)} %get-tuple-element.38.refs_0_.state, bf16[1024,256]{1,0:T(8,128)(2,1)S(1)} %get-tuple-element.39.refs_1_.mixed, s32[1,1,1024]{2,1,0:T(1,128)S(1)} %copy-done.11, bf16[256,256]{1,0:T(8,128)(2,1)S(1)} %copy-done.4, bf16[512,256]{1,0:T(8,128)(2,1)S(1)} %heavy_rows.1.after.refs_3_), custom_call_target="tpu_custom_call" | custom-call | bytes 1048576 | tf_op jit(solution)/shard_map/kept_rows/pallas_call | solution.py:328
  30.8 0.0 collective-permute-done.9.refs_5_
  30.8 1.2 %collective-permute-done.10.refs_6_ = bf16[176,256]{1,0:T(8,128)(2,1)S(1)} collective-permute-done((bf16[176,256]{1,0:T(8,128)(2,1)S(1)}, bf16[176,256]{1,0:T(8,128)(2,1)S(1)}, u32[]{:S(2)}, u32[]{:S(2)}) %collective-permute-start.10) | collective-permute-done | bytes 90144 | tf_op jit(solution)/shard_map/ppermute | solution.py:375
  32.0 0.0 collective-permute-done.8.refs_4_
  32.0 0.0 copy-done.10
  32.0 4.9 %owner_layer.1 = (bf16[176,256]{1,0:T(8,128)(2,1)S(1)}, bf16[176,256]{1,0:T(8,128)(2,1)S(1)}, bf16[176,256]{1,0:T(8,128)(2,1)S(1)}, bf16[1024,256]{1,0:T(8,128)(2,1)S(1)}) custom-call(f32[1024,256]{1,0:T(8,128)S(1)} %kept_rows.1.refs_0_, s32[4,512]{1,0:T(4,128)S(1)} %get-tuple-element.42.refs_1_.refs_2_, bf16[256,768]{1,0:T(8,128)(2,1)S(1)} %copy-done.10, ...), custom_call_target="tpu_custom_call" | custom-call | bytes 1048576 | tf_op jit(solution)/shard_map/owner_layer/pallas_call | solution.py:328
  36.9 0.9 %collective-permute-start.12 = (bf16[176,256]{1,0:T(8,128)(2,1)S(1)}, bf16[176,256]{1,0:T(8,128)(2,1)S(1)}, u32[]{:S(2)}, u32[]{:S(2)}) collective-permute-start(bf16[176,256]{1,0:T(8,128)(2,1)S(1)} %get-tuple-element.47), channel_id=1, source_target_pairs={{2,0},{3,1},{0,2},{1,3},{6,4},{7,5},{4,6},{5,7},{10,8},{11,9},{8,1... | collective-permute-start | bytes 270344 | tf_op jit(solution)/shard_map/ppermute | solution.py:375
  37.7 0.7 %collective-permute-start.13 = (bf16[176,256]{1,0:T(8,128)(2,1)S(1)}, bf16[176,256]{1,0:T(8,128)(2,1)S(1)}, u32[]{:S(2)}, u32[]{:S(2)}) collective-permute-start(bf16[176,256]{1,0:T(8,128)(2,1)S(1)} %get-tuple-element.48), channel_id=1, source_target_pairs={{3,0},{2,1},{1,2},{0,3},{7,4},{6,5},{5,6},{4,7},{11,8},{10,9},{9,1... | collective-permute-start | bytes 270344 | tf_op jit(solution)/shard_map/ppermute | solution.py:375
  38.4 0.7 %collective-permute-start.11 = (bf16[176,256]{1,0:T(8,128)(2,1)S(1)}, bf16[176,256]{1,0:T(8,128)(2,1)S(1)}, u32[]{:S(2)}, u32[]{:S(2)}) collective-permute-start(bf16[176,256]{1,0:T(8,128)(2,1)S(1)} %get-tuple-element.46.refs_8_), channel_id=1, source_target_pairs={{1,0},{0,1},{3,2},{2,3},{5,4},{4,5},{7,6},{6,7},{9,8},{8,9},{11,10... | collective-permute-start | bytes 270344 | tf_op jit(solution)/shard_map/ppermute | solution.py:375
  39.1 0.0 copy-done.8
  39.1 3.0 %stayed_changes.1.refs_0_ = f32[1024,256]{1,0:T(8,128)S(1)} custom-call(f32[1024,256]{1,0:T(8,128)S(1)} %kept_rows.1.refs_0_, bf16[1024,256]{1,0:T(8,128)(2,1)S(1)} %get-tuple-element.45.refs_1_, s32[4,512]{1,0:T(4,128)S(1)} %get-tuple-element.42.refs_1_.refs_2_, s32[1,1,1024]{2,1,0:T(1,128)S(1)} %copy-done.12, s32[1,1,1024]{2,1,0:T(1,128)S(1)} %copy-done.13, ...), custom_call_target="tpu_custom_call" | custom-call | bytes 1048576 | tf_op jit(solution)/shard_map/stayed_changes/pallas_call | solution.py:328
  42.0 0.3 collective-permute-done.12.refs_5_
  42.4 0.3 collective-permute-done.13.refs_6_
  42.7 0.0 collective-permute-done.11.refs_4_
  42.7 1.7 %relayed_changes.1 = f32[1024,256]{1,0:T(8,128)} custom-call(f32[1024,256]{1,0:T(8,128)S(1)} %stayed_changes.1.refs_0_, s32[1,1,1024]{2,1,0:T(1,128)S(1)} %copy-done.12, s32[1,1,1024]{2,1,0:T(1,128)S(1)} %copy-done.13, bf16[256,256]{1,0:T(8,128)(2,1)S(1)} %copy-done.8, bf16[176,256]{1,0:T(8,128)(2,1)S(1)} %collective-permute-done.11.refs_4_, ...), custom_call_target="tpu_custom_call" | custom-call | bytes 1048576 | tf_op jit(solution)/shard_map/relayed_changes/pallas_call | solution.py:328
  (17 shorter events, 0.0 us)
Async XLA Ops:
  0.0 0.9 %copy-start.5 = (bf16[2,256,256]{2,1,0:T(8,128)(2,1)S(1)}, bf16[2,256,256]{2,1,0:T(8,128)(2,1)}, u32[]{:S(2)}) copy-start(bf16[2,256,256]{2,1,0:T(8,128)(2,1)} %w_msg.3) | copy-start | bytes 786436
  0.0 1.1 %copy-start.3 = (bf16[1024,256]{1,0:T(8,128)(2,1)S(1)}, bf16[1024,256]{1,0:T(8,128)(2,1)}, u32[]{:S(2)}) copy-start(bf16[1024,256]{1,0:T(8,128)(2,1)} %state.1) | copy-start | bytes 1572868
  0.0 1.1 %copy-start.14 = (s32[1,1,4,512]{3,2,1,0:T(4,128)S(1)}, s32[1,1,4,512]{3,2,1,0:T(4,128)}, u32[]{:S(2)}) copy-start(s32[1,1,4,512]{3,2,1,0:T(4,128)} %inbox.1) | copy-start | bytes 24580
  0.0 0.8 %copy-start.16 = (s32[1,1,4,128]{3,2,1,0:T(4,128)S(1)}, s32[1,1,4,128]{3,2,1,0:T(4,128)}, u32[]{:S(2)}) copy-start(s32[1,1,4,128]{3,2,1,0:T(4,128)} %rim_rows.3) | copy-start | bytes 6148
  1.1 5.5 %copy-start.2 = (bf16[1,1,8,3,128,128]{5,4,3,2,1,0:T(8,128)(2,1)S(1)}, bf16[1,1,8,3,128,128]{5,4,3,2,1,0:T(8,128)(2,1)}, u32[]{:S(2)}) copy-start(bf16[1,1,8,3,128,128]{5,4,3,2,1,0:T(8,128)(2,1)} %tiles.6) | copy-start | bytes 2359300
  1.9 6.4 %collective-permute-start = (bf16[144,256]{1,0:T(8,128)(2,1)S(1)}, bf16[144,256]{1,0:T(8,128)(2,1)S(1)}, u32[]{:S(2)}, u32[]{:S(2)}) collective-permute-start(bf16[144,256]{1,0:T(8,128)(2,1)S(1)} %get-tuple-element.28), channel_id=1, source_target_pairs={{0,4},{1,5},{2,6},{3,7},{4,0},{5,1},{6,2},{7,3},{8,12},{9,13},{10,... | collective-permute-start | bytes 221192 | tf_op jit(solution)/shard_map/ppermute | solution.py:367
  4.9 1.6 %copy-start.17 = (s32[1,1,8,3]{2,1,3,0:T(1,128)S(1)}, s32[1,1,8,3]{2,1,3,0:T(1,128)}, u32[]{:S(2)}) copy-start(s32[1,1,8,3]{2,1,3,0:T(1,128)} %param.23) | copy-start | bytes 292
  4.9 3.4 %collective-permute-start.1 = (bf16[144,256]{1,0:T(8,128)(2,1)S(1)}, bf16[144,256]{1,0:T(8,128)(2,1)S(1)}, u32[]{:S(2)}, u32[]{:S(2)}) collective-permute-start(bf16[144,256]{1,0:T(8,128)(2,1)S(1)} %get-tuple-element.29), channel_id=1, source_target_pairs={{0,1},{1,0},{2,3},{3,2},{4,8},{5,9},{6,10},{7,11},{8,4},{9,5},{10,... | collective-permute-start | bytes 221192 | tf_op jit(solution)/shard_map/ppermute | solution.py:367
  4.9 3.4 %collective-permute-start.2 = (bf16[144,256]{1,0:T(8,128)(2,1)S(1)}, bf16[144,256]{1,0:T(8,128)(2,1)S(1)}, u32[]{:S(2)}, u32[]{:S(2)}) collective-permute-start(bf16[144,256]{1,0:T(8,128)(2,1)S(1)} %get-tuple-element.30), channel_id=1, source_target_pairs={{0,1},{1,0},{2,3},{3,2},{4,5},{5,4},{6,7},{7,6},{8,9},{9,8},{10,11... | collective-permute-start | bytes 221192 | tf_op jit(solution)/shard_map/ppermute | solution.py:367
  5.4 1.2 %copy-start.18 = (s32[1,1,8,3]{2,1,3,0:T(1,128)S(1)}, s32[1,1,8,3]{2,1,3,0:T(1,128)}, u32[]{:S(2)}) copy-start(s32[1,1,8,3]{2,1,3,0:T(1,128)} %param.24) | copy-start | bytes 292
  5.4 4.4 %collective-permute-start.3 = (bf16[144,256]{1,0:T(8,128)(2,1)S(1)}, bf16[144,256]{1,0:T(8,128)(2,1)S(1)}, u32[]{:S(2)}, u32[]{:S(2)}) collective-permute-start(bf16[144,256]{1,0:T(8,128)(2,1)S(1)} %get-tuple-element.31), channel_id=1, source_target_pairs={{0,3},{1,2},{2,1},{3,0},{4,7},{5,6},{6,5},{7,4},{8,11},{9,10},{10,... | collective-permute-start | bytes 221192 | tf_op jit(solution)/shard_map/ppermute | solution.py:367
  6.7 3.1 %copy-start.6 = (bf16[2,256,256]{2,1,0:T(8,128)(2,1)S(1)}, bf16[2,256,256]{2,1,0:T(8,128)(2,1)}, u32[]{:S(2)}) copy-start(bf16[2,256,256]{2,1,0:T(8,128)(2,1)} %w_upd.3) | copy-start | bytes 786436
  6.7 3.1 %copy-start.7 = (bf16[1,1,4,128,128]{4,3,2,1,0:T(8,128)(2,1)S(1)}, bf16[1,1,4,128,128]{4,3,2,1,0:T(8,128)(2,1)}, u32[]{:S(2)}) copy-start(bf16[1,1,4,128,128]{4,3,2,1,0:T(8,128)(2,1)} %tiles.7) | copy-start | bytes 393220
  6.7 3.1 %copy-start.15 = (s32[1,1,4]{2,1,0:T(1,128)S(1)}, s32[1,1,4]{2,1,0:T(1,128)}, u32[]{:S(2)}) copy-start(s32[1,1,4]{2,1,0:T(1,128)} %block.3) | copy-start | bytes 52
  11.6 5.7 %collective-permute-start.4 = (bf16[128,256]{1,0:T(8,128)(2,1)S(1)}, bf16[128,256]{1,0:T(8,128)(2,1)S(1)}, u32[]{:S(2)}, u32[]{:S(2)}) collective-permute-start(bf16[128,256]{1,0:T(8,128)(2,1)S(1)} %get-tuple-element.34), channel_id=1, source_target_pairs={{0,4},{1,5},{2,6},{3,7},{4,0},{5,1},{6,2},{7,3},{8,12},{9,13},{10,... | collective-permute-start | bytes 196616 | tf_op jit(solution)/shard_map/ppermute | solution.py:367
  13.8 3.6 %collective-permute-start.5 = (bf16[128,256]{1,0:T(8,128)(2,1)S(1)}, bf16[128,256]{1,0:T(8,128)(2,1)S(1)}, u32[]{:S(2)}, u32[]{:S(2)}) collective-permute-start(bf16[128,256]{1,0:T(8,128)(2,1)S(1)} %get-tuple-element.35), channel_id=1, source_target_pairs={{0,1},{1,0},{2,3},{3,2},{4,8},{5,9},{6,10},{7,11},{8,4},{9,5},{10,... | collective-permute-start | bytes 196616 | tf_op jit(solution)/shard_map/ppermute | solution.py:367
  14.0 3.4 %collective-permute-start.6 = (bf16[128,256]{1,0:T(8,128)(2,1)S(1)}, bf16[128,256]{1,0:T(8,128)(2,1)S(1)}, u32[]{:S(2)}, u32[]{:S(2)}) collective-permute-start(bf16[128,256]{1,0:T(8,128)(2,1)S(1)} %get-tuple-element.36), channel_id=1, source_target_pairs={{0,1},{1,0},{2,3},{3,2},{4,5},{5,4},{6,7},{7,6},{8,9},{9,8},{10,11... | collective-permute-start | bytes 196616 | tf_op jit(solution)/shard_map/ppermute | solution.py:367
  14.3 4.1 %collective-permute-start.7 = (bf16[128,256]{1,0:T(8,128)(2,1)S(1)}, bf16[128,256]{1,0:T(8,128)(2,1)S(1)}, u32[]{:S(2)}, u32[]{:S(2)}) collective-permute-start(bf16[128,256]{1,0:T(8,128)(2,1)S(1)} %get-tuple-element.37), channel_id=1, source_target_pairs={{0,3},{1,2},{2,1},{3,0},{4,7},{5,6},{6,5},{7,4},{8,11},{9,10},{10,... | collective-permute-start | bytes 196616 | tf_op jit(solution)/shard_map/ppermute | solution.py:367
  15.6 1.2 %copy-start.11 = (s32[1,1,1024]{2,1,0:T(1,128)S(1)}, s32[1,1,1024]{2,1,0:T(1,128)}, u32[]{:S(2)}) copy-start(s32[1,1,1024]{2,1,0:T(1,128)} %order.3) | copy-start | bytes 12292
  15.6 1.2 %copy-start.12 = (s32[1,1,1024]{2,1,0:T(1,128)S(1)}, s32[1,1,1024]{2,1,0:T(1,128)}, u32[]{:S(2)}) copy-start(s32[1,1,1024]{2,1,0:T(1,128)} %refs_1_.3) | copy-start | bytes 12292
  15.6 1.2 %copy-start.13 = (s32[1,1,1024]{2,1,0:T(1,128)S(1)}, s32[1,1,1024]{2,1,0:T(1,128)}, u32[]{:S(2)}) copy-start(s32[1,1,1024]{2,1,0:T(1,128)} %refs_2_.5) | copy-start | bytes 12292
  16.8 1.6 %copy-start.9 = (bf16[256,768]{1,0:T(8,128)(2,1)S(1)}, bf16[256,768]{1,0:T(8,128)(2,1)}, u32[]{:S(2)}) copy-start(bf16[256,768]{1,0:T(8,128)(2,1)} %w_qkv.1) | copy-start | bytes 1179652
  18.4 5.1 %copy-start = (bf16[256,1024]{1,0:T(8,128)(2,1)S(1)}, bf16[256,1024]{1,0:T(8,128)(2,1)}, u32[]{:S(2)}) copy-start(bf16[256,1024]{1,0:T(8,128)(2,1)} %refs_5_.5) | copy-start | bytes 1572868
  18.4 5.1 %copy-start.1 = (bf16[1024,256]{1,0:T(8,128)(2,1)S(1)}, bf16[1024,256]{1,0:T(8,128)(2,1)}, u32[]{:S(2)}) copy-start(bf16[1024,256]{1,0:T(8,128)(2,1)} %refs_6_.1) | copy-start | bytes 1572868
  18.4 5.1 %copy-start.4 = (bf16[256,256]{1,0:T(8,128)(2,1)S(1)}, bf16[256,256]{1,0:T(8,128)(2,1)}, u32[]{:S(2)}) copy-start(bf16[256,256]{1,0:T(8,128)(2,1)} %w_out.1) | copy-start | bytes 393220
  25.5 5.3 %collective-permute-start.9 = (bf16[176,256]{1,0:T(8,128)(2,1)S(1)}, bf16[176,256]{1,0:T(8,128)(2,1)S(1)}, u32[]{:S(2)}, u32[]{:S(2)}) collective-permute-start(bf16[176,256]{1,0:T(8,128)(2,1)S(1)} %get-tuple-element.43), channel_id=1, source_target_pairs={{0,2},{1,3},{2,0},{3,1},{4,6},{5,7},{6,4},{7,5},{8,10},{9,11},{10,... | collective-permute-start | bytes 270344 | tf_op jit(solution)/shard_map/ppermute | solution.py:375
  27.1 4.9 %collective-permute-start.10 = (bf16[176,256]{1,0:T(8,128)(2,1)S(1)}, bf16[176,256]{1,0:T(8,128)(2,1)S(1)}, u32[]{:S(2)}, u32[]{:S(2)}) collective-permute-start(bf16[176,256]{1,0:T(8,128)(2,1)S(1)} %get-tuple-element.44), channel_id=1, source_target_pairs={{0,3},{1,2},{2,1},{3,0},{4,7},{5,6},{6,5},{7,4},{8,11},{9,10},{10,... | collective-permute-start | bytes 270344 | tf_op jit(solution)/shard_map/ppermute | solution.py:375
  27.1 4.9 %collective-permute-start.8 = (bf16[176,256]{1,0:T(8,128)(2,1)S(1)}, bf16[176,256]{1,0:T(8,128)(2,1)S(1)}, u32[]{:S(2)}, u32[]{:S(2)}) collective-permute-start(bf16[176,256]{1,0:T(8,128)(2,1)S(1)} %get-tuple-element.41.refs_6_), channel_id=1, source_target_pairs={{0,1},{1,0},{2,3},{3,2},{4,5},{5,4},{6,7},{7,6},{8,9},{9,8},{10,11... | collective-permute-start | bytes 270344 | tf_op jit(solution)/shard_map/ppermute | solution.py:375
  29.8 2.2 %copy-start.10 = (bf16[256,768]{1,0:T(8,128)(2,1)S(1)}, bf16[256,768]{1,0:T(8,128)(2,1)}, u32[]{:S(2)}) copy-start(bf16[256,768]{1,0:T(8,128)(2,1)} %refs_2_.4) | copy-start | bytes 1179652
  32.0 7.1 %copy-start.8 = (bf16[256,256]{1,0:T(8,128)(2,1)S(1)}, bf16[256,256]{1,0:T(8,128)(2,1)}, u32[]{:S(2)}) copy-start(bf16[256,256]{1,0:T(8,128)(2,1)} %refs_3_.7) | copy-start | bytes 393220
  36.9 5.5 %collective-permute-start.12 = (bf16[176,256]{1,0:T(8,128)(2,1)S(1)}, bf16[176,256]{1,0:T(8,128)(2,1)S(1)}, u32[]{:S(2)}, u32[]{:S(2)}) collective-permute-start(bf16[176,256]{1,0:T(8,128)(2,1)S(1)} %get-tuple-element.47), channel_id=1, source_target_pairs={{2,0},{3,1},{0,2},{1,3},{6,4},{7,5},{4,6},{5,7},{10,8},{11,9},{8,1... | collective-permute-start | bytes 270344 | tf_op jit(solution)/shard_map/ppermute | solution.py:375
  37.7 4.9 %collective-permute-start.13 = (bf16[176,256]{1,0:T(8,128)(2,1)S(1)}, bf16[176,256]{1,0:T(8,128)(2,1)S(1)}, u32[]{:S(2)}, u32[]{:S(2)}) collective-permute-start(bf16[176,256]{1,0:T(8,128)(2,1)S(1)} %get-tuple-element.48), channel_id=1, source_target_pairs={{3,0},{2,1},{1,2},{0,3},{7,4},{6,5},{5,6},{4,7},{11,8},{10,9},{9,1... | collective-permute-start | bytes 270344 | tf_op jit(solution)/shard_map/ppermute | solution.py:375
  38.4 4.3 %collective-permute-start.11 = (bf16[176,256]{1,0:T(8,128)(2,1)S(1)}, bf16[176,256]{1,0:T(8,128)(2,1)S(1)}, u32[]{:S(2)}, u32[]{:S(2)}) collective-permute-start(bf16[176,256]{1,0:T(8,128)(2,1)S(1)} %get-tuple-element.46.refs_8_), channel_id=1, source_target_pairs={{1,0},{0,1},{3,2},{2,3},{5,4},{4,5},{7,6},{6,7},{9,8},{8,9},{11,10... | collective-permute-start | bytes 270344 | tf_op jit(solution)/shard_map/ppermute | solution.py:375

commit v7 on v6

--- a/solution.py
+++ b/solution.py
@@ -239,8 +239,8 @@
     at_ball = hot(iota((count, slots.shape[1]), 0) + start == slots[1:2, :])
     back = dot(at_ball, mixed[...]).astype(BF16)
     rows = dot(at_row, state[...].astype(BF16))
-    step = up_to(count // 2, 16)
-    cuts = [slice(0, step), slice(step, count)]
+    step = up_to(count // 3, 16)
+    cuts = [slice(at, min(at + step, count)) for at in range(0, count, step)]
     done = feed([rows[cut] + dot(back[cut], w_out[...]) for cut in cuts], w_in, w_mlp_out)
     units = jnp.concatenate([normed(piece).astype(BF16) for piece in done], axis=0)
     at = 0

time: 45 us -> 45 us (level)
  no operation moved by 1% of the time
where the time goes in v7:
time: 45 us; the launch traced here: 44.6 us
  Pallas kernels  25.1 us (56%)
  starting transfers between devices  13 us (29%)
  waiting for transfers between devices  4.83 us (11%)
  local copies, waits for them, and re-layouts  1.22 us (3%)
    pallas_call x13, Pallas kernels, call(): pl.pallas_call(kernel, out_shape=[jax.ShapeDtypeStruct(shape, kind) for s...  25.1 us
    ppermute x8, starting transfers between devices, exchange(): moved[i] = lax.ppermute(rims[i], ('grp', 'rot'), plan[i])  8.6 us
    ppermute x6, starting transfers between devices, relay(): lax.ppermute(rows, 'rot', [pair[::-1] for pair in pairs] if back else pairs)  4.41 us
    ppermute x8, waiting for transfers between devices, exchange(): moved[i] = lax.ppermute(rims[i], ('grp', 'rot'), plan[i])  2.91 us
    ppermute x6, waiting for transfers between devices, relay(): lax.ppermute(rows, 'rot', [pair[::-1] for pair in pairs] if back else pairs)  1.91 us
    unnamed x40, local copies, waits for them, and re-layouts  1.22 us
  transfers between devices with their start and end apart: 14, of which 6 were waited for; matrix products, arithmetic and copies ran while one was open for 0% of the time, Pallas kernels for 20%

profile of v7, /device:TPU:0, one launch (start us, length us, event | category | flops | bytes accessed | tf_op | source)
XLA Modules:
  0.0 44.6 jit_solution(11542985275197351102)
XLA Ops:
  0.0 0.8 %copy-done.16 = s32[1,1,4,128]{3,2,1,0:T(4,128)S(1)} copy-done((s32[1,1,4,128]{3,2,1,0:T(4,128)S(1)}, s32[1,1,4,128]{3,2,1,0:T(4,128)}, u32[]{:S(2)}) %copy-start.16) | copy-done | bytes 2072
  0.8 0.1 rim_rows.2.chosen
  0.9 0.1 copy-done.5
  1.0 0.2 copy-done.3
  1.1 0.0 copy-done.14
  1.1 0.7 %first_messages.1 = (bf16[1024,256]{1,0:T(8,128)(2,1)S(1)}, bf16[144,256]{1,0:T(8,128)(2,1)S(1)}, bf16[144,256]{1,0:T(8,128)(2,1)S(1)}, bf16[144,256]{1,0:T(8,128)(2,1)S(1)}, bf16[144,256]{1,0:T(8,128)(2,1)S(1)}) custom-call(s32[4,128,128]{2,1,0:T(8,128)S(1)} %rim_rows.2.chosen, bf16[1024,256]{1,0:T(8,128)(2,1)S(1)} %copy-done.3, ...), custom_call_target="tpu_custom_call" | custom-call | bytes 1048576 | tf_op jit(solution)/shard_map/first_messages/pallas_call | solution.py:328
  1.9 3.0 %collective-permute-start = (bf16[144,256]{1,0:T(8,128)(2,1)S(1)}, bf16[144,256]{1,0:T(8,128)(2,1)S(1)}, u32[]{:S(2)}, u32[]{:S(2)}) collective-permute-start(bf16[144,256]{1,0:T(8,128)(2,1)S(1)} %get-tuple-element.28), channel_id=1, source_target_pairs={{0,4},{1,5},{2,6},{3,7},{4,0},{5,1},{6,2},{7,3},{8,12},{9,13},{10,... | collective-permute-start | bytes 221192 | tf_op jit(solution)/shard_map/ppermute | solution.py:367
  4.9 0.0 collective-permute-start.1
  4.9 0.5 %collective-permute-start.2 = (bf16[144,256]{1,0:T(8,128)(2,1)S(1)}, bf16[144,256]{1,0:T(8,128)(2,1)S(1)}, u32[]{:S(2)}, u32[]{:S(2)}) collective-permute-start(bf16[144,256]{1,0:T(8,128)(2,1)S(1)} %get-tuple-element.30), channel_id=1, source_target_pairs={{0,1},{1,0},{2,3},{3,2},{4,5},{5,4},{6,7},{7,6},{8,9},{9,8},{10,11... | collective-permute-start | bytes 221192 | tf_op jit(solution)/shard_map/ppermute | solution.py:367
  5.4 1.1 %collective-permute-start.3 = (bf16[144,256]{1,0:T(8,128)(2,1)S(1)}, bf16[144,256]{1,0:T(8,128)(2,1)S(1)}, u32[]{:S(2)}, u32[]{:S(2)}) collective-permute-start(bf16[144,256]{1,0:T(8,128)(2,1)S(1)} %get-tuple-element.31), channel_id=1, source_target_pairs={{0,3},{1,2},{2,1},{3,0},{4,7},{5,6},{6,5},{7,4},{8,11},{9,10},{10,... | collective-permute-start | bytes 221192 | tf_op jit(solution)/shard_map/ppermute | solution.py:367
  6.5 0.0 copy-done.17
  6.5 0.1 copy.20.source
  6.6 0.0 copy-done.18
  6.6 0.1 copy.21.live
  6.7 0.0 copy-done.2
  6.7 1.2 %local_edges.1.aggregate = f32[1024,256]{1,0:T(8,128)S(1)} custom-call(bf16[1024,256]{1,0:T(8,128)(2,1)S(1)} %get-tuple-element.27.messages, bf16[1,1,8,3,128,128]{5,4,3,2,1,0:T(8,128)(2,1)S(1)} %copy-done.2, s32[1,1,8,3]{3,2,1,0:T(8,128)S(1)} %copy.20.source, s32[1,1,8,3]{3,2,1,0:T(8,128)S(1)} %copy.21.live), custom_call_target="tpu_custom_call" | custom-call | bytes 1048576 | tf_op jit(solution)/shard_map/local_edges/pallas_call | solution.py:328
  7.9 0.3 collective-permute-done.rec0
  8.2 0.0 collective-permute-done.1.rec1
  8.2 0.0 collective-permute-done.2.rec2.refs_3_
  8.2 1.5 %collective-permute-done.3.rec3.refs_4_ = bf16[144,256]{1,0:T(8,128)(2,1)S(1)} collective-permute-done((bf16[144,256]{1,0:T(8,128)(2,1)S(1)}, bf16[144,256]{1,0:T(8,128)(2,1)S(1)}, u32[]{:S(2)}, u32[]{:S(2)}) %collective-permute-start.3) | collective-permute-done | bytes 73760 | tf_op jit(solution)/shard_map/ppermute | solution.py:367
  9.8 0.0 copy-done.6
  9.8 0.0 copy-done.7
  9.8 0.0 copy-done.15
  9.8 1.8 %second_messages.1 = (f32[1024,256]{1,0:T(8,128)S(1)}, bf16[1024,256]{1,0:T(8,128)(2,1)S(1)}, bf16[128,256]{1,0:T(8,128)(2,1)S(1)}, bf16[128,256]{1,0:T(8,128)(2...) custom-call(bf16[1024,256]{1,0:T(8,128)(2,1)S(1)} %copy-done.3, ...), custom_call_target="tpu_custom_call" | custom-call | bytes 1048576 | tf_op jit(solution)/shard_map/second_messages/pallas_call | solution.py:328
  11.6 2.2 %collective-permute-start.4 = (bf16[128,256]{1,0:T(8,128)(2,1)S(1)}, bf16[128,256]{1,0:T(8,128)(2,1)S(1)}, u32[]{:S(2)}, u32[]{:S(2)}) collective-permute-start(bf16[128,256]{1,0:T(8,128)(2,1)S(1)} %get-tuple-element.34), channel_id=1, source_target_pairs={{0,4},{1,5},{2,6},{3,7},{4,0},{5,1},{6,2},{7,3},{8,12},{9,13},{10,... | collective-permute-start | bytes 196616 | tf_op jit(solution)/shard_map/ppermute | solution.py:367
  13.8 0.2 collective-permute-start.5
  14.0 0.3 collective-permute-start.6
  14.3 1.3 %collective-permute-start.7 = (bf16[128,256]{1,0:T(8,128)(2,1)S(1)}, bf16[128,256]{1,0:T(8,128)(2,1)S(1)}, u32[]{:S(2)}, u32[]{:S(2)}) collective-permute-start(bf16[128,256]{1,0:T(8,128)(2,1)S(1)} %get-tuple-element.37), channel_id=1, source_target_pairs={{0,3},{1,2},{2,1},{3,0},{4,7},{5,6},{6,5},{7,4},{8,11},{9,10},{10,... | collective-permute-start | bytes 196616 | tf_op jit(solution)/shard_map/ppermute | solution.py:367
  15.6 1.2 %local_edges_again.1.aggregate = f32[1024,256]{1,0:T(8,128)S(1)} custom-call(bf16[1024,256]{1,0:T(8,128)(2,1)S(1)} %get-tuple-element.33.messages.refs_5_, bf16[1,1,8,3,128,128]{5,4,3,2,1,0:T(8,128)(2,1)S(1)} %copy-done.2, s32[1,1,8,3]{3,2,1,0:T(8,128)S(1)} %copy.20.source, s32[1,1,8,3]{3,2,1,0:T(8,128)S(1)} %copy.21.live), custom_call_target="tpu_custom_call" | custom-call | bytes 1048576 | tf_op jit(solution)/shard_map/local_edges_again/pallas_call | solution.py:328
  16.8 0.0 copy-done.11
  16.8 0.0 copy-done.12
  16.8 0.0 copy-done.13
  16.8 0.0 copy-start.9
  16.8 0.5 %slots.1 = (s32[2,1024]{1,0:T(2,128)S(1)}, s32[4,512]{1,0:T(4,128)S(1)}) custom-call(s32[1,1,1024]{2,1,0:T(1,128)S(1)} %copy-done.11, s32[1,1,1024]{2,1,0:T(1,128)S(1)} %copy-done.12, s32[1,1,1024]{2,1,0:T(1,128)S(1)} %copy-done.13, bf16[144,256]{1,0:T(8,128)(2,1)S(1)} %collective-permute-done.2.rec2.refs_3_, ...), custom_call_target="tpu_custom_call" | custom-call | bytes 1048576 | tf_op jit(solution)/shard_map/slots/pallas_call | solution.py:328
  17.3 0.0 collective-permute-done.4.rec0
  17.3 0.0 collective-permute-done.5.rec1
  17.3 0.0 collective-permute-done.6.rec2
  17.3 1.1 %collective-permute-done.7.rec3 = bf16[128,256]{1,0:T(8,128)(2,1)S(1)} collective-permute-done((bf16[128,256]{1,0:T(8,128)(2,1)S(1)}, bf16[128,256]{1,0:T(8,128)(2,1)S(1)}, u32[]{:S(2)}, u32[]{:S(2)}) %collective-permute-start.7) | collective-permute-done | bytes 65568 | tf_op jit(solution)/shard_map/ppermute | solution.py:367
  18.4 0.0 copy-done.9
  18.4 5.1 %ball_attention.1 = (f32[1024,256]{1,0:T(8,128)S(1)}, bf16[1024,256]{1,0:T(8,128)(2,1)S(1)}) custom-call(f32[1024,256]{1,0:T(8,128)S(1)} %get-tuple-element.32.state, f32[1024,256]{1,0:T(8,128)S(1)} %local_edges_again.1.aggregate, bf16[128,256]{1,0:T(8,128)(2,1)S(1)} %collective-permute-done.4.rec0, bf16[128,256]{1,0:T(8,128)(2,1)S(1)} %collective-permute-done.5.rec1, ...), custom_call_target="tpu_custom_call" | custom-call | bytes 1048576 | tf_op jit(solution)/shard_map/ball_attention/pallas_call | solution.py:328
  23.5 0.0 copy-done
  23.5 0.0 copy-done.1
  23.5 0.0 copy-done.4
  23.5 2.0 %light_rows.1 = (bf16[176,256]{1,0:T(8,128)(2,1)S(1)}, bf16[176,256]{1,0:T(8,128)(2,1)S(1)}, bf16[176,256]{1,0:T(8,128)(2,1)S(1)}) custom-call(f32[1024,256]{1,0:T(8,128)S(1)} %get-tuple-element.38.refs_0_.state, bf16[1024,256]{1,0:T(8,128)(2,1)S(1)} %get-tuple-element.39.refs_1_.mixed, s32[2,1024]{1,0:T(2,128)S(1)} %get-tuple-element.40.refs_2_, ...), custom_call_target="tpu_custom_call" | custom-call | bytes 1048576 | tf_op jit(solution)/shard_map/light_rows/pallas_call | solution.py:328
  25.5 1.6 %collective-permute-start.9 = (bf16[176,256]{1,0:T(8,128)(2,1)S(1)}, bf16[176,256]{1,0:T(8,128)(2,1)S(1)}, u32[]{:S(2)}, u32[]{:S(2)}) collective-permute-start(bf16[176,256]{1,0:T(8,128)(2,1)S(1)} %get-tuple-element.43), channel_id=1, source_target_pairs={{0,2},{1,3},{2,0},{3,1},{4,6},{5,7},{6,4},{7,5},{8,10},{9,11},{10,... | collective-permute-start | bytes 270344 | tf_op jit(solution)/shard_map/ppermute | solution.py:375
  27.1 0.0 collective-permute-start.10
  27.1 0.6 %collective-permute-start.8 = (bf16[176,256]{1,0:T(8,128)(2,1)S(1)}, bf16[176,256]{1,0:T(8,128)(2,1)S(1)}, u32[]{:S(2)}, u32[]{:S(2)}) collective-permute-start(bf16[176,256]{1,0:T(8,128)(2,1)S(1)} %get-tuple-element.41.refs_6_), channel_id=1, source_target_pairs={{0,1},{1,0},{2,3},{3,2},{4,5},{5,4},{6,7},{7,6},{8,9},{9,8},{10,11... | collective-permute-start | bytes 270344 | tf_op jit(solution)/shard_map/ppermute | solution.py:375
  27.7 2.0 %heavy_rows.1.after.refs_3_ = bf16[512,256]{1,0:T(8,128)(2,1)S(1)} custom-call(f32[1024,256]{1,0:T(8,128)S(1)} %get-tuple-element.38.refs_0_.state, bf16[1024,256]{1,0:T(8,128)(2,1)S(1)} %get-tuple-element.39.refs_1_.mixed, s32[2,1024]{1,0:T(2,128)S(1)} %get-tuple-element.40.refs_2_, bf16[256,256]{1,0:T(8,128)(2,1)S(1)} %copy-done.4, ...), custom_call_target="tpu_custom_call" | custom-call | bytes 1048576 | tf_op jit(solution)/shard_map/heavy_rows/pallas_call | solution.py:328
  29.7 0.0 copy-start.10
  29.7 1.0 %kept_rows.1.refs_0_ = f32[1024,256]{1,0:T(8,128)S(1)} custom-call(f32[1024,256]{1,0:T(8,128)S(1)} %get-tuple-element.38.refs_0_.state, bf16[1024,256]{1,0:T(8,128)(2,1)S(1)} %get-tuple-element.39.refs_1_.mixed, s32[1,1,1024]{2,1,0:T(1,128)S(1)} %copy-done.11, bf16[256,256]{1,0:T(8,128)(2,1)S(1)} %copy-done.4, bf16[512,256]{1,0:T(8,128)(2,1)S(1)} %heavy_rows.1.after.refs_3_), custom_call_target="tpu_custom_call" | custom-call | bytes 1048576 | tf_op jit(solution)/shard_map/kept_rows/pallas_call | solution.py:328
  30.7 0.0 collective-permute-done.9.refs_5_
  30.7 1.3 %collective-permute-done.10.refs_6_ = bf16[176,256]{1,0:T(8,128)(2,1)S(1)} collective-permute-done((bf16[176,256]{1,0:T(8,128)(2,1)S(1)}, bf16[176,256]{1,0:T(8,128)(2,1)S(1)}, u32[]{:S(2)}, u32[]{:S(2)}) %collective-permute-start.10) | collective-permute-done | bytes 90144 | tf_op jit(solution)/shard_map/ppermute | solution.py:375
  32.0 0.0 collective-permute-done.8.refs_4_
  32.0 0.0 copy-done.10
  32.0 4.9 %owner_layer.1 = (bf16[176,256]{1,0:T(8,128)(2,1)S(1)}, bf16[176,256]{1,0:T(8,128)(2,1)S(1)}, bf16[176,256]{1,0:T(8,128)(2,1)S(1)}, bf16[1024,256]{1,0:T(8,128)(2,1)S(1)}) custom-call(f32[1024,256]{1,0:T(8,128)S(1)} %kept_rows.1.refs_0_, s32[4,512]{1,0:T(4,128)S(1)} %get-tuple-element.42.refs_1_.refs_2_, bf16[256,768]{1,0:T(8,128)(2,1)S(1)} %copy-done.10, ...), custom_call_target="tpu_custom_call" | custom-call | bytes 1048576 | tf_op jit(solution)/shard_map/owner_layer/pallas_call | solution.py:328
  36.9 0.8 %collective-permute-start.12 = (bf16[176,256]{1,0:T(8,128)(2,1)S(1)}, bf16[176,256]{1,0:T(8,128)(2,1)S(1)}, u32[]{:S(2)}, u32[]{:S(2)}) collective-permute-start(bf16[176,256]{1,0:T(8,128)(2,1)S(1)} %get-tuple-element.47), channel_id=1, source_target_pairs={{2,0},{3,1},{0,2},{1,3},{6,4},{7,5},{4,6},{5,7},{10,8},{11,9},{8,1... | collective-permute-start | bytes 270344 | tf_op jit(solution)/shard_map/ppermute | solution.py:375
  37.7 0.7 %collective-permute-start.13 = (bf16[176,256]{1,0:T(8,128)(2,1)S(1)}, bf16[176,256]{1,0:T(8,128)(2,1)S(1)}, u32[]{:S(2)}, u32[]{:S(2)}) collective-permute-start(bf16[176,256]{1,0:T(8,128)(2,1)S(1)} %get-tuple-element.48), channel_id=1, source_target_pairs={{3,0},{2,1},{1,2},{0,3},{7,4},{6,5},{5,6},{4,7},{11,8},{10,9},{9,1... | collective-permute-start | bytes 270344 | tf_op jit(solution)/shard_map/ppermute | solution.py:375
  38.4 0.7 %collective-permute-start.11 = (bf16[176,256]{1,0:T(8,128)(2,1)S(1)}, bf16[176,256]{1,0:T(8,128)(2,1)S(1)}, u32[]{:S(2)}, u32[]{:S(2)}) collective-permute-start(bf16[176,256]{1,0:T(8,128)(2,1)S(1)} %get-tuple-element.46.refs_8_), channel_id=1, source_target_pairs={{1,0},{0,1},{3,2},{2,3},{5,4},{4,5},{7,6},{6,7},{9,8},{8,9},{11,10... | collective-permute-start | bytes 270344 | tf_op jit(solution)/shard_map/ppermute | solution.py:375
  39.1 0.0 copy-done.8
  39.1 3.0 %stayed_changes.1.refs_0_ = f32[1024,256]{1,0:T(8,128)S(1)} custom-call(f32[1024,256]{1,0:T(8,128)S(1)} %kept_rows.1.refs_0_, bf16[1024,256]{1,0:T(8,128)(2,1)S(1)} %get-tuple-element.45.refs_1_, s32[4,512]{1,0:T(4,128)S(1)} %get-tuple-element.42.refs_1_.refs_2_, s32[1,1,1024]{2,1,0:T(1,128)S(1)} %copy-done.12, s32[1,1,1024]{2,1,0:T(1,128)S(1)} %copy-done.13, ...), custom_call_target="tpu_custom_call" | custom-call | bytes 1048576 | tf_op jit(solution)/shard_map/stayed_changes/pallas_call | solution.py:328
  42.0 0.4 collective-permute-done.12.refs_5_
  42.4 0.3 collective-permute-done.13.refs_6_
  42.7 0.0 collective-permute-done.11.refs_4_
  42.7 1.7 %relayed_changes.1 = f32[1024,256]{1,0:T(8,128)} custom-call(f32[1024,256]{1,0:T(8,128)S(1)} %stayed_changes.1.refs_0_, s32[1,1,1024]{2,1,0:T(1,128)S(1)} %copy-done.12, s32[1,1,1024]{2,1,0:T(1,128)S(1)} %copy-done.13, bf16[256,256]{1,0:T(8,128)(2,1)S(1)} %copy-done.8, bf16[176,256]{1,0:T(8,128)(2,1)S(1)} %collective-permute-done.11.refs_4_, ...), custom_call_target="tpu_custom_call" | custom-call | bytes 1048576 | tf_op jit(solution)/shard_map/relayed_changes/pallas_call | solution.py:328
  (17 shorter events, 0.0 us)
Async XLA Ops:
  0.0 0.9 %copy-start.5 = (bf16[2,256,256]{2,1,0:T(8,128)(2,1)S(1)}, bf16[2,256,256]{2,1,0:T(8,128)(2,1)}, u32[]{:S(2)}) copy-start(bf16[2,256,256]{2,1,0:T(8,128)(2,1)} %w_msg.3) | copy-start | bytes 786436
  0.0 1.1 %copy-start.3 = (bf16[1024,256]{1,0:T(8,128)(2,1)S(1)}, bf16[1024,256]{1,0:T(8,128)(2,1)}, u32[]{:S(2)}) copy-start(bf16[1024,256]{1,0:T(8,128)(2,1)} %state.1) | copy-start | bytes 1572868
  0.0 1.1 %copy-start.14 = (s32[1,1,4,512]{3,2,1,0:T(4,128)S(1)}, s32[1,1,4,512]{3,2,1,0:T(4,128)}, u32[]{:S(2)}) copy-start(s32[1,1,4,512]{3,2,1,0:T(4,128)} %inbox.1) | copy-start | bytes 24580
  0.0 0.8 %copy-start.16 = (s32[1,1,4,128]{3,2,1,0:T(4,128)S(1)}, s32[1,1,4,128]{3,2,1,0:T(4,128)}, u32[]{:S(2)}) copy-start(s32[1,1,4,128]{3,2,1,0:T(4,128)} %rim_rows.3) | copy-start | bytes 6148
  1.1 5.5 %copy-start.2 = (bf16[1,1,8,3,128,128]{5,4,3,2,1,0:T(8,128)(2,1)S(1)}, bf16[1,1,8,3,128,128]{5,4,3,2,1,0:T(8,128)(2,1)}, u32[]{:S(2)}) copy-start(bf16[1,1,8,3,128,128]{5,4,3,2,1,0:T(8,128)(2,1)} %tiles.6) | copy-start | bytes 2359300
  1.9 6.4 %collective-permute-start = (bf16[144,256]{1,0:T(8,128)(2,1)S(1)}, bf16[144,256]{1,0:T(8,128)(2,1)S(1)}, u32[]{:S(2)}, u32[]{:S(2)}) collective-permute-start(bf16[144,256]{1,0:T(8,128)(2,1)S(1)} %get-tuple-element.28), channel_id=1, source_target_pairs={{0,4},{1,5},{2,6},{3,7},{4,0},{5,1},{6,2},{7,3},{8,12},{9,13},{10,... | collective-permute-start | bytes 221192 | tf_op jit(solution)/shard_map/ppermute | solution.py:367
  4.9 1.6 %copy-start.17 = (s32[1,1,8,3]{2,1,3,0:T(1,128)S(1)}, s32[1,1,8,3]{2,1,3,0:T(1,128)}, u32[]{:S(2)}) copy-start(s32[1,1,8,3]{2,1,3,0:T(1,128)} %param.23) | copy-start | bytes 292
  4.9 3.4 %collective-permute-start.1 = (bf16[144,256]{1,0:T(8,128)(2,1)S(1)}, bf16[144,256]{1,0:T(8,128)(2,1)S(1)}, u32[]{:S(2)}, u32[]{:S(2)}) collective-permute-start(bf16[144,256]{1,0:T(8,128)(2,1)S(1)} %get-tuple-element.29), channel_id=1, source_target_pairs={{0,1},{1,0},{2,3},{3,2},{4,8},{5,9},{6,10},{7,11},{8,4},{9,5},{10,... | collective-permute-start | bytes 221192 | tf_op jit(solution)/shard_map/ppermute | solution.py:367
  4.9 3.4 %collective-permute-start.2 = (bf16[144,256]{1,0:T(8,128)(2,1)S(1)}, bf16[144,256]{1,0:T(8,128)(2,1)S(1)}, u32[]{:S(2)}, u32[]{:S(2)}) collective-permute-start(bf16[144,256]{1,0:T(8,128)(2,1)S(1)} %get-tuple-element.30), channel_id=1, source_target_pairs={{0,1},{1,0},{2,3},{3,2},{4,5},{5,4},{6,7},{7,6},{8,9},{9,8},{10,11... | collective-permute-start | bytes 221192 | tf_op jit(solution)/shard_map/ppermute | solution.py:367
  5.4 1.2 %copy-start.18 = (s32[1,1,8,3]{2,1,3,0:T(1,128)S(1)}, s32[1,1,8,3]{2,1,3,0:T(1,128)}, u32[]{:S(2)}) copy-start(s32[1,1,8,3]{2,1,3,0:T(1,128)} %param.24) | copy-start | bytes 292
  5.4 4.4 %collective-permute-start.3 = (bf16[144,256]{1,0:T(8,128)(2,1)S(1)}, bf16[144,256]{1,0:T(8,128)(2,1)S(1)}, u32[]{:S(2)}, u32[]{:S(2)}) collective-permute-start(bf16[144,256]{1,0:T(8,128)(2,1)S(1)} %get-tuple-element.31), channel_id=1, source_target_pairs={{0,3},{1,2},{2,1},{3,0},{4,7},{5,6},{6,5},{7,4},{8,11},{9,10},{10,... | collective-permute-start | bytes 221192 | tf_op jit(solution)/shard_map/ppermute | solution.py:367
  6.7 3.1 %copy-start.6 = (bf16[2,256,256]{2,1,0:T(8,128)(2,1)S(1)}, bf16[2,256,256]{2,1,0:T(8,128)(2,1)}, u32[]{:S(2)}) copy-start(bf16[2,256,256]{2,1,0:T(8,128)(2,1)} %w_upd.3) | copy-start | bytes 786436
  6.7 3.1 %copy-start.7 = (bf16[1,1,4,128,128]{4,3,2,1,0:T(8,128)(2,1)S(1)}, bf16[1,1,4,128,128]{4,3,2,1,0:T(8,128)(2,1)}, u32[]{:S(2)}) copy-start(bf16[1,1,4,128,128]{4,3,2,1,0:T(8,128)(2,1)} %tiles.7) | copy-start | bytes 393220
  6.7 3.1 %copy-start.15 = (s32[1,1,4]{2,1,0:T(1,128)S(1)}, s32[1,1,4]{2,1,0:T(1,128)}, u32[]{:S(2)}) copy-start(s32[1,1,4]{2,1,0:T(1,128)} %block.3) | copy-start | bytes 52
  11.6 5.7 %collective-permute-start.4 = (bf16[128,256]{1,0:T(8,128)(2,1)S(1)}, bf16[128,256]{1,0:T(8,128)(2,1)S(1)}, u32[]{:S(2)}, u32[]{:S(2)}) collective-permute-start(bf16[128,256]{1,0:T(8,128)(2,1)S(1)} %get-tuple-element.34), channel_id=1, source_target_pairs={{0,4},{1,5},{2,6},{3,7},{4,0},{5,1},{6,2},{7,3},{8,12},{9,13},{10,... | collective-permute-start | bytes 196616 | tf_op jit(solution)/shard_map/ppermute | solution.py:367
  13.8 3.6 %collective-permute-start.5 = (bf16[128,256]{1,0:T(8,128)(2,1)S(1)}, bf16[128,256]{1,0:T(8,128)(2,1)S(1)}, u32[]{:S(2)}, u32[]{:S(2)}) collective-permute-start(bf16[128,256]{1,0:T(8,128)(2,1)S(1)} %get-tuple-element.35), channel_id=1, source_target_pairs={{0,1},{1,0},{2,3},{3,2},{4,8},{5,9},{6,10},{7,11},{8,4},{9,5},{10,... | collective-permute-start | bytes 196616 | tf_op jit(solution)/shard_map/ppermute | solution.py:367
  14.0 3.4 %collective-permute-start.6 = (bf16[128,256]{1,0:T(8,128)(2,1)S(1)}, bf16[128,256]{1,0:T(8,128)(2,1)S(1)}, u32[]{:S(2)}, u32[]{:S(2)}) collective-permute-start(bf16[128,256]{1,0:T(8,128)(2,1)S(1)} %get-tuple-element.36), channel_id=1, source_target_pairs={{0,1},{1,0},{2,3},{3,2},{4,5},{5,4},{6,7},{7,6},{8,9},{9,8},{10,11... | collective-permute-start | bytes 196616 | tf_op jit(solution)/shard_map/ppermute | solution.py:367
  14.3 4.1 %collective-permute-start.7 = (bf16[128,256]{1,0:T(8,128)(2,1)S(1)}, bf16[128,256]{1,0:T(8,128)(2,1)S(1)}, u32[]{:S(2)}, u32[]{:S(2)}) collective-permute-start(bf16[128,256]{1,0:T(8,128)(2,1)S(1)} %get-tuple-element.37), channel_id=1, source_target_pairs={{0,3},{1,2},{2,1},{3,0},{4,7},{5,6},{6,5},{7,4},{8,11},{9,10},{10,... | collective-permute-start | bytes 196616 | tf_op jit(solution)/shard_map/ppermute | solution.py:367
  15.6 1.2 %copy-start.11 = (s32[1,1,1024]{2,1,0:T(1,128)S(1)}, s32[1,1,1024]{2,1,0:T(1,128)}, u32[]{:S(2)}) copy-start(s32[1,1,1024]{2,1,0:T(1,128)} %order.3) | copy-start | bytes 12292
  15.6 1.2 %copy-start.12 = (s32[1,1,1024]{2,1,0:T(1,128)S(1)}, s32[1,1,1024]{2,1,0:T(1,128)}, u32[]{:S(2)}) copy-start(s32[1,1,1024]{2,1,0:T(1,128)} %refs_1_.3) | copy-start | bytes 12292
  15.6 1.2 %copy-start.13 = (s32[1,1,1024]{2,1,0:T(1,128)S(1)}, s32[1,1,1024]{2,1,0:T(1,128)}, u32[]{:S(2)}) copy-start(s32[1,1,1024]{2,1,0:T(1,128)} %refs_2_.5) | copy-start | bytes 12292
  16.8 1.6 %copy-start.9 = (bf16[256,768]{1,0:T(8,128)(2,1)S(1)}, bf16[256,768]{1,0:T(8,128)(2,1)}, u32[]{:S(2)}) copy-start(bf16[256,768]{1,0:T(8,128)(2,1)} %w_qkv.1) | copy-start | bytes 1179652
  18.4 5.1 %copy-start = (bf16[256,1024]{1,0:T(8,128)(2,1)S(1)}, bf16[256,1024]{1,0:T(8,128)(2,1)}, u32[]{:S(2)}) copy-start(bf16[256,1024]{1,0:T(8,128)(2,1)} %refs_5_.5) | copy-start | bytes 1572868
  18.4 5.1 %copy-start.1 = (bf16[1024,256]{1,0:T(8,128)(2,1)S(1)}, bf16[1024,256]{1,0:T(8,128)(2,1)}, u32[]{:S(2)}) copy-start(bf16[1024,256]{1,0:T(8,128)(2,1)} %refs_6_.1) | copy-start | bytes 1572868
  18.4 5.1 %copy-start.4 = (bf16[256,256]{1,0:T(8,128)(2,1)S(1)}, bf16[256,256]{1,0:T(8,128)(2,1)}, u32[]{:S(2)}) copy-start(bf16[256,256]{1,0:T(8,128)(2,1)} %w_out.1) | copy-start | bytes 393220
  25.5 5.2 %collective-permute-start.9 = (bf16[176,256]{1,0:T(8,128)(2,1)S(1)}, bf16[176,256]{1,0:T(8,128)(2,1)S(1)}, u32[]{:S(2)}, u32[]{:S(2)}) collective-permute-start(bf16[176,256]{1,0:T(8,128)(2,1)S(1)} %get-tuple-element.43), channel_id=1, source_target_pairs={{0,2},{1,3},{2,0},{3,1},{4,6},{5,7},{6,4},{7,5},{8,10},{9,11},{10,... | collective-permute-start | bytes 270344 | tf_op jit(solution)/shard_map/ppermute | solution.py:375
  27.1 4.9 %collective-permute-start.10 = (bf16[176,256]{1,0:T(8,128)(2,1)S(1)}, bf16[176,256]{1,0:T(8,128)(2,1)S(1)}, u32[]{:S(2)}, u32[]{:S(2)}) collective-permute-start(bf16[176,256]{1,0:T(8,128)(2,1)S(1)} %get-tuple-element.44), channel_id=1, source_target_pairs={{0,3},{1,2},{2,1},{3,0},{4,7},{5,6},{6,5},{7,4},{8,11},{9,10},{10,... | collective-permute-start | bytes 270344 | tf_op jit(solution)/shard_map/ppermute | solution.py:375
  27.1 4.9 %collective-permute-start.8 = (bf16[176,256]{1,0:T(8,128)(2,1)S(1)}, bf16[176,256]{1,0:T(8,128)(2,1)S(1)}, u32[]{:S(2)}, u32[]{:S(2)}) collective-permute-start(bf16[176,256]{1,0:T(8,128)(2,1)S(1)} %get-tuple-element.41.refs_6_), channel_id=1, source_target_pairs={{0,1},{1,0},{2,3},{3,2},{4,5},{5,4},{6,7},{7,6},{8,9},{9,8},{10,11... | collective-permute-start | bytes 270344 | tf_op jit(solution)/shard_map/ppermute | solution.py:375
  29.7 2.3 %copy-start.10 = (bf16[256,768]{1,0:T(8,128)(2,1)S(1)}, bf16[256,768]{1,0:T(8,128)(2,1)}, u32[]{:S(2)}) copy-start(bf16[256,768]{1,0:T(8,128)(2,1)} %refs_2_.4) | copy-start | bytes 1179652
  32.0 7.1 %copy-start.8 = (bf16[256,256]{1,0:T(8,128)(2,1)S(1)}, bf16[256,256]{1,0:T(8,128)(2,1)}, u32[]{:S(2)}) copy-start(bf16[256,256]{1,0:T(8,128)(2,1)} %refs_3_.7) | copy-start | bytes 393220
  36.9 5.5 %collective-permute-start.12 = (bf16[176,256]{1,0:T(8,128)(2,1)S(1)}, bf16[176,256]{1,0:T(8,128)(2,1)S(1)}, u32[]{:S(2)}, u32[]{:S(2)}) collective-permute-start(bf16[176,256]{1,0:T(8,128)(2,1)S(1)} %get-tuple-element.47), channel_id=1, source_target_pairs={{2,0},{3,1},{0,2},{1,3},{6,4},{7,5},{4,6},{5,7},{10,8},{11,9},{8,1... | collective-permute-start | bytes 270344 | tf_op jit(solution)/shard_map/ppermute | solution.py:375
  37.7 5.0 %collective-permute-start.13 = (bf16[176,256]{1,0:T(8,128)(2,1)S(1)}, bf16[176,256]{1,0:T(8,128)(2,1)S(1)}, u32[]{:S(2)}, u32[]{:S(2)}) collective-permute-start(bf16[176,256]{1,0:T(8,128)(2,1)S(1)} %get-tuple-element.48), channel_id=1, source_target_pairs={{3,0},{2,1},{1,2},{0,3},{7,4},{6,5},{5,6},{4,7},{11,8},{10,9},{9,1... | collective-permute-start | bytes 270344 | tf_op jit(solution)/shard_map/ppermute | solution.py:375
  38.4 4.3 %collective-permute-start.11 = (bf16[176,256]{1,0:T(8,128)(2,1)S(1)}, bf16[176,256]{1,0:T(8,128)(2,1)S(1)}, u32[]{:S(2)}, u32[]{:S(2)}) collective-permute-start(bf16[176,256]{1,0:T(8,128)(2,1)S(1)} %get-tuple-element.46.refs_8_), channel_id=1, source_target_pairs={{1,0},{0,1},{3,2},{2,3},{5,4},{4,5},{7,6},{6,7},{9,8},{8,9},{11,10... | collective-permute-start | bytes 270344 | tf_op jit(solution)/shard_map/ppermute | solution.py:375
